TPU v7x, 32 devices: a whole 2x2x4 slice. The times are simulated.
32 devices in a mesh: groups: 2 (over y), expert: 4 (over z), narrow: 4 (over x, core).
Axes of the slice: x: 2, y: 2, z: 4, core: 2. Of those that a mesh axis runs over, the one named last changes fastest.
Arguments:
- tokens: bfloat16 [256, 3584], P(('groups', 'expert', 'narrow')), parts along dimension 0, may hold values from -6 to 6
- expert_ids: int32 [256, 8], P(('groups', 'expert', 'narrow')), parts along dimension 0, may hold values from 0 to 31, all different within a row; in each aligned block of 32 rows (0 to 31, 32 to 63, ...) at most 13 rows name the same one
- route_weights: bfloat16 [256, 8], P(('groups', 'expert', 'narrow')), parts along dimension 0, may hold values from 0.019897461 to 0.5
- expert_gate: bfloat16 [32, 3584, 2048], P('expert', None, 'narrow'), may hold values from -0.09375 to 0.09375
- expert_up: bfloat16 [32, 3584, 2048], P('expert', None, 'narrow'), may hold values from -0.09375 to 0.09375
- expert_down: bfloat16 [32, 2048, 3584], P('expert', 'narrow'), may hold values from -0.125 to 0.125
- shared_gate: bfloat16 [3584, 10240], P('expert', 'narrow'), may hold values from -0.09375 to 0.09375
- shared_up: bfloat16 [3584, 10240], P('expert', 'narrow'), may hold values from -0.09375 to 0.09375
- shared_down: bfloat16 [10240, 3584], P('narrow', 'expert'), may hold values from -0.0625 to 0.0625
- shared_scale: float32 [3584], replicated, may hold values from -0.09375 to 0.09375
Outputs:
- moe_out: bfloat16 [256, 3584], P(('groups', 'expert', 'narrow')), parts along dimension 0
There are 2 independent parts, one for each index of `groups`. A program takes and returns all parts, laid end to end along the dimension named above; an argument that names none is the same for every part. Nothing has to cross between parts.
Inputs may be any that keep to these rules, and one draw needn't show every extreme that they name: `expert_ids`: each row names 8 different experts. In each aligned block of 32 rows no expert is named by more than 13 rows, and in some block one expert is named by exactly 13 rows.
All inputs are finite; a program needn't handle non-finite values.
Results may differ from a plain program's by a relative error of at most 0.0054.
Values may be sent and summed in bfloat16 or wider, within the bound.
No kernel may reach another device: no remote copies, remote signals or barrier semaphores. Data moves between devices by JAX's collectives and lax.ppermute only.
A program may use at most 256 MiB of HBM per device.

v0:
```python
import jax
import jax.numpy as jnp
from jax import lax
from jax.sharding import PartitionSpec as P

EXPERTS = 32


def slot_targets(expert_list, experts, capacity):
    flat_ids = expert_list.reshape(-1)
    onehot = (flat_ids[:, None] == jnp.arange(experts, dtype=jnp.int32)[None, :]).astype(jnp.int32)
    before = jnp.cumsum(onehot, axis=0) - onehot
    return flat_ids * capacity + jnp.sum(before * onehot, axis=1)


def body(
    tokens,
    expert_ids,
    route_weights,
    expert_gate,
    expert_up,
    expert_down,
    shared_gate,
    shared_up,
    shared_down,
    shared_scale,
):
    group_ids = lax.all_gather(expert_ids, "narrow", axis=0, tiled=True)
    group_rows, group_weights = (
        lax.all_gather(tokens, "narrow", axis=0, tiled=True),
        lax.all_gather(route_weights, "narrow", axis=0, tiled=True),
    )
    row_count, feat_width = group_rows.shape
    chosen = expert_ids.shape[1]
    spread = lax.axis_size("expert")
    local_count = expert_gate.shape[0]
    capacity = row_count * chosen * 13 // (8 * EXPERTS)
    targets = slot_targets(group_ids, EXPERTS, capacity)
    sources = jnp.arange(targets.shape[0], dtype=jnp.int32) // chosen
    slot_table = jnp.full((EXPERTS * capacity,), row_count, jnp.int32).at[targets].set(sources)
    padded = jnp.concatenate([group_rows, jnp.zeros((1, feat_width), group_rows.dtype)], axis=0)
    outgoing = padded[slot_table].reshape(spread, local_count, capacity, feat_width)
    arrived = lax.all_to_all(outgoing, "expert", split_axis=0, concat_axis=0, tiled=True)
    gate_part = jnp.einsum(
        "slcd,ldf->slcf", arrived, expert_gate, preferred_element_type=jnp.float32
    )
    up_part = jnp.einsum("slcd,ldf->slcf", arrived, expert_up, preferred_element_type=jnp.float32)
    activated = (jax.nn.silu(gate_part) * up_part).astype(jnp.bfloat16)
    result = jnp.einsum(
        "slcf,lfd->slcd", activated, expert_down, preferred_element_type=jnp.float32
    ).astype(jnp.bfloat16)
    returned = lax.all_to_all(result, "expert", split_axis=0, concat_axis=0, tiled=True)
    picked = returned.reshape(EXPERTS * capacity, feat_width)[targets].astype(jnp.float32)
    scaled = picked * group_weights.reshape(-1).astype(jnp.float32)[:, None]
    routed = jnp.sum(scaled.reshape(row_count, chosen, feat_width), axis=1)
    local_rows = lax.all_to_all(group_rows, "expert", split_axis=1, concat_axis=0, tiled=True)
    hidden_sums = lax.psum_scatter(
        jnp.concatenate(
            [
                jnp.dot(local_rows, shared_gate, preferred_element_type=jnp.float32),
                jnp.dot(local_rows, shared_up, preferred_element_type=jnp.float32),
            ],
            axis=1,
        ),
        "expert",
        scatter_dimension=0,
        tiled=True,
    )
    gate_total, up_total = jnp.split(hidden_sums, 2, axis=1)
    shared_act = (jax.nn.silu(gate_total) * up_total).astype(jnp.bfloat16)
    shared_out = jnp.dot(
        shared_act,
        lax.all_gather(shared_down, "expert", axis=1, tiled=True),
        preferred_element_type=jnp.float32,
    )
    branch_gate = jax.nn.sigmoid(
        jnp.dot(group_rows.astype(jnp.float32), shared_scale, precision=lax.Precision.HIGHEST)
    )
    combined = routed + branch_gate[:, None] * shared_out
    return lax.psum_scatter(combined, "narrow", scatter_dimension=0, tiled=True).astype(
        jnp.bfloat16
    )


def solution(mesh):
    return jax.shard_map(
        body,
        mesh=mesh,
        in_specs=(
            P(("groups", "expert", "narrow"), None),
            P(("groups", "expert", "narrow"), None),
            P(("groups", "expert", "narrow"), None),
            P("expert", None, "narrow"),
            P("expert", None, "narrow"),
            P("expert", "narrow", None),
            P("expert", "narrow"),
            P("expert", "narrow"),
            P("narrow", "expert"),
            P(),
        ),
        out_specs=P(("groups", "expert", "narrow"), None),
        check_vma=False,
    )
```

profile of v0, /device:TPU:0, one launch (start us, length us, event | category | flops | bytes accessed | tf_op | source)
XLA Modules:
  0.0 545.8 jit_solution(16536552166342382818)
XLA Ops:
  6.5 0.0 reduce-scatter.3.cloned.1.call-start
  6.5 0.0 copy-start
  6.5 7.3 %all_gather.12 = bf16[32,3584]{1,0:T(8,128)(2,1)S(1)} all-gather(bf16[8,3584]{1,0:T(8,128)(2,1)} %param.10), channel_id=1, replica_groups=mesh['groups'=2,'expert'=4,'narrow'=4] {'narrow'}, dimensions={0}, use_global_device_ids=true | all-gather | bytes 286720 | tf_op jit(solution)/shard_map/all_gather | solution.py:30
  13.9 13.5 %all_to_all.29 = bf16[32,4,896]{2,0,1:T(8,128)(2,1)S(1)} all-to-all(bf16[32,4,896]{2,0,1:T(8,128)(2,1)S(1)} %bitcast.92), channel_id=1, replica_groups=mesh['groups'=2,'expert'=4,'narrow'=4] {'expert'}, dimensions={1} | all-to-all | bytes 458752 | tf_op jit(solution)/shard_map/all_to_all | solution.py:56
  27.4 3.2 fusion.61
  30.6 0.0 copy-done
  30.6 0.8 fusion.62
  31.4 1.8 pad_maximum_fusion
  33.2 0.0 copy-start.2
  33.2 0.0 reduce-scatter.3.cloned.1.call-update
  33.2 0.0 all-gather.2.cloned.1.call-start
  33.3 0.7 all-gather.2.cloned.1.call-update
  34.0 0.0 copy-done.2
  34.0 5.2 all_gather.13
  39.2 0.1 eq.29
  39.3 0.1 eq.25
  39.4 0.6 reduce-window.6
  40.0 0.2 slice_reduce_fusion
  40.2 0.1 mul.52
  40.3 0.1 fusion.55
  40.4 1.4 scatter_custom_fusion
  41.9 3.2 gather_fusion
  45.0 2.7 reshape.71
  47.8 3.8 copy.16
  51.6 132.6 %all_to_all.30 = bf16[4,8,13,3584]{3,1,2,0:T(8,128)(2,1)S(1)} all-to-all(bf16[4,8,13,3584]{3,1,2,0:T(8,128)(2,1)S(1)} %copy.16), channel_id=1, replica_groups=mesh['groups'=2,'expert'=4,'narrow'=4] {'expert'}, dimensions={0} | all-to-all | bytes 5963776 | tf_op jit(solution)/shard_map/all_to_all | solution.py:43
  184.2 13.2 %fusion.16 = f32[4,8,13,512]{3,2,0,1:T(8,128)} fusion(bf16[8,3584,512]{2,1,0:T(8,128)(2,1)} %param.13, bf16[4,8,13,3584]{3,1,2,0:T(8,128)(2,1)S(1)} %all_to_all.30), kind=kOutput, calls=%fused_computation.18 | convolution fusion | flops 1526726656 | bytes 33193984 | tf_op jit(solution)/shard_map/slcd,ldf->slcf/dot_general | solution.py:44
  197.4 23.4 %fusion.9 = bf16[4,8,13,3584]{3,2,0,1:T(8,128)(2,1)} fusion(bf16[8,512,3584]{2,1,0:T(8,128)(2,1)} %param.15, bf16[8,3584,512]{2,1,0:T(8,128)(2,1)} %param.14, bf16[4,8,13,3584]{3,1,2,0:T(8,128)(2,1)S(1)} %all_to_all.30, f32[4,8,13,512]{3,2,0,1:T(8,128)} %fusion.16), kind=kOutput, calls=%fused_computation.10 | convolution fusion | flops 3056222208 | bytes 65536000 | tf_op jit(solution)/shard_map/slcf,lfd->slcd/dot_general | solution.py:49
  220.7 5.4 copy.19
  226.2 0.0 copy-start.3
  226.2 0.0 copy-start.1
  226.2 3.8 all-to-all-start.1
  230.0 0.0 reduce-scatter.5.cloned.1.call-start
  230.0 0.0 copy-done.3
  230.0 5.4 all_gather.14
  235.4 0.0 copy-done.1
  235.5 0.3 fusion.43
  235.7 143.6 %all-to-all-done.1 = bf16[4,8,13,3584]{3,1,2,0:T(8,128)(2,1)S(1)} async-done(((bf16[4,8,13,3584]{3,1,2,0:T(8,128)(2,1)}), bf16[4,8,13,3584]{3,1,2,0:T(8,128)(2,1)S(1)}, u32[]{:S(2)}, u32[]{:S(2)}) %all-to-all-start.1) | async-done | bytes 2981920 | tf_op jit(solution)/shard_map/all_to_all | solution.py:52
  379.4 2.9 copy.20
  382.2 3.2 reshape.72
  385.5 2.9 gather_fusion.1
  388.4 2.9 fusion.13
  391.4 0.0 reduce-scatter.3.cloned.1.call-done
  391.4 115.5 %all-gather.2.cloned.1.call-done = bf16[2560,3584]{1,0:T(8,128)(2,1)} async-done(((bf16[2560,896]{1,0:T(8,128)(2,1)}), bf16[2560,3584]{1,0:T(8,128)(2,1)}) %all-gather.2.cloned.1.call-update) | async-done | bytes 18350096 | tf_op jit(solution)/shard_map/all_gather | solution.py:73
  506.9 10.4 %fusion.12 = f32[32,3584]{1,0:T(8,128)} fusion(f32[32,3584]{1,0:T(8,128)S(1)} %fusion.13, bf16[2560,3584]{1,0:T(8,128)(2,1)} %all-gather.2.cloned.1.call-done, f32[32]{0:T(128)S(1)} %fusion.43, f32[32,5120]{1,0:T(8,128)} %reduce-scatter.3.cloned.1.call-done), kind=kOutput, calls=%fused_computation.12 | convolution fusion | flops 587923456 | bytes 19923072 | tf_op jit(solution)/shard_map/dot_general | solution.py:71
  517.3 0.0 reduce-scatter.5.cloned.1.call-update
  517.3 20.4 %reduce-scatter.5.cloned.1.call-done = f32[8,3584]{1,0:T(8,128)} async-done(((f32[32,3584]{1,0:T(8,128)}), f32[8,3584]{1,0:T(8,128)}) %reduce-scatter.5.cloned.1.call-update) | async-done | bytes 114704 | tf_op jit(solution)/shard_map/reduce_scatter | solution.py:80
  537.7 1.5 convert_element_type.46
  (13 shorter events, 0.1 us)
Async XLA Ops:
  6.5 384.9 %reduce-scatter.3.cloned.1.call-start = ((), (), s32[]{:S(2)}) async-start(), calls=%async_computation.5 | async-start | bytes 3276800 | tf_op jit(solution)/shard_map/reduce_scatter | solution.py:57
  6.5 24.0 %copy-start = (bf16[896,2560]{1,0:T(8,128)(2,1)S(1)}, bf16[896,2560]{1,0:T(8,128)(2,1)}, u32[]{:S(2)}) copy-start(bf16[896,2560]{1,0:T(8,128)(2,1)} %param.17) | copy-start | bytes 13762564
  33.2 0.8 copy-start.2
  33.2 473.7 %all-gather.2.cloned.1.call-start = ((), (), s32[]{:S(2)}) async-start(), calls=%async_computation.6 | async-start | bytes 22937600 | tf_op jit(solution)/shard_map/all_gather | solution.py:73
  226.2 3.9 copy-start.3
  226.2 9.3 %copy-start.1 = (f32[3584]{0:T(1024)S(1)}, f32[3584]{0:T(1024)}, u32[]{:S(2)}) copy-start(f32[3584]{0:T(1024)} %param.19) | copy-start | bytes 43012
  226.2 153.2 %all-to-all-start.1 = ((bf16[4,8,13,3584]{3,1,2,0:T(8,128)(2,1)}), bf16[4,8,13,3584]{3,1,2,0:T(8,128)(2,1)S(1)}, u32[]{:S(2)}, u32[]{:S(2)}) async-start(bf16[4,8,13,3584]{3,1,2,0:T(8,128)(2,1)} %copy.19), calls=%async_computation.1 | async-start | bytes 5963776 | tf_op jit(solution)/shard_map/all_to_all | solution.py:52
  230.0 307.8 %reduce-scatter.5.cloned.1.call-start = ((), (), s32[]{:S(2)}) async-start(), calls=%async_computation.7 | async-start | bytes 573440 | tf_op jit(solution)/shard_map/reduce_scatter | solution.py:80
Sparse Core Ops, SparseCore 0:
  33.3 75.6 reduce-scatter.2
  110.6 396.2 all-gather.1
  517.5 20.2 reduce-scatter.4
where the time goes:
time: 546 us
  waiting for transfers between devices  280 us (51%)
  blocking collectives  164 us (30%)
  matrix products  51.3 us (9%)
  local copies, waits for them, and re-layouts  26.1 us (5%)
  between operations  13.3 us (2%)
  other arithmetic  6.99 us (1%)
    all_to_all x1, waiting for transfers between devices, body(): lax.all_to_all(result, 'expert', split_axis=0, concat_axis=0, tiled=True)  144 us
    all_to_all x1, blocking collectives, body(): lax.all_to_all(outgoing, 'expert', split_axis=0, concat_axis=0, tiled=True)  133 us
    all_gather x1, waiting for transfers between devices, body(): lax.all_gather(shared_down, 'expert', axis=1, tiled=True)  115 us
    dot_general x1, matrix products, body(): jnp.einsum('slcf,lfd->slcd', activated, expert_down, preferred_element_ty...  23.4 us
    reduce_scatter x1, waiting for transfers between devices, body(): lax.psum_scatter(combined, 'narrow', scatter_dimension=0, tiled=True)  20.4 us
    all_to_all x1, blocking collectives, body(): lax.all_to_all(group_rows, 'expert', split_axis=1, concat_axis=0, tiled=T...  13.5 us
    dot_general x1, matrix products, body(): jnp.einsum('slcd,ldf->slcf', arrived, expert_gate, preferred_element_type...  13.2 us
  transfers between devices with their start and end apart: 4, of which 3 were waited for; matrix products, arithmetic and copies ran while one was open for 12% of the time, Pallas kernels for 0%

commit v1 on v0

v1 whole, which is shorter than its diff:
```python
import functools

import jax
import jax.numpy as jnp
from jax import lax
from jax.experimental import pallas as pl
from jax.experimental.pallas import tpu as pltpu
from jax.sharding import PartitionSpec as P

EXPERTS = 32
LANES = 128
VMEM_LIMIT = 48 * 2**20


def chunk_of(width, most):
    best = width
    for size in range(LANES, most + 1, LANES):
        if width % size == 0:
            best = size
    return best


def z_shift(value, step):
    spread = lax.axis_size("expert")
    return lax.ppermute(value, "expert", [(i, (i + step) % spread) for i in range(spread)])


def x_shift(value, step):
    size = lax.axis_size("narrow")
    return lax.ppermute(value, "narrow", [(i, (i + 2 * step) % size) for i in range(size)])


def core_swap(value):
    size = lax.axis_size("narrow")
    return lax.ppermute(value, "narrow", [(i, i ^ 1) for i in range(size)])


def gather_rows(own):
    spread, chips = lax.axis_size("expert"), lax.axis_size("narrow") // 2
    column = jnp.concatenate([own] + [z_shift(own, d) for d in range(1, spread)], axis=0)
    plane = jnp.concatenate([column] + [x_shift(column, d) for d in range(1, chips)], axis=0)
    return jnp.concatenate([plane, core_swap(plane)], axis=0)


def shared_in_kernel(sizes, x_ref, gate_ref, up_ref, *out_refs):
    outer, spread, rows = sizes
    x = x_ref[...]
    for half, w_ref in enumerate((gate_ref, up_ref)):
        sums = jnp.dot(x, w_ref[...], preferred_element_type=jnp.float32)
        sums = sums.reshape(outer, spread, rows, sums.shape[1])
        for d in range(spread):
            block = sums[:, d].reshape(outer * rows, sums.shape[3])
            out_refs[d][half] = block.astype(jnp.bfloat16)


def shared_in(x, gate, up, rows):
    count, depth = x.shape
    hidden = gate.shape[1]
    spread = lax.axis_size("expert")
    outer = count // (spread * rows)
    width = chunk_of(hidden, 512)
    w_spec = pl.BlockSpec((depth, width), lambda j: (0, j))
    out_spec = pl.BlockSpec((2, outer * rows, width), lambda j: (0, 0, j))
    return pl.pallas_call(
        functools.partial(shared_in_kernel, (outer, spread, rows)),
        grid=(hidden // width,),
        in_specs=[pl.BlockSpec((count, depth), lambda j: (0, 0)), w_spec, w_spec],
        out_specs=[out_spec] * spread,
        out_shape=[jax.ShapeDtypeStruct((2, outer * rows, hidden), jnp.bfloat16)] * spread,
        compiler_params=pltpu.CompilerParams(vmem_limit_bytes=VMEM_LIMIT),
        cost_estimate=pl.CostEstimate(
            flops=4 * count * depth * hidden,
            bytes_accessed=4 * depth * hidden + 4 * count * hidden,
            transcendentals=0,
        ),
        name="shared_in",
    )(x, gate, up)


def expert_in_kernel(feat, first_ref, x_ref, gate_ref, up_ref, out_ref):
    chosen = first_ref[0] + pl.program_id(0)
    x = x_ref[:, :feat]
    gate = jnp.dot(x, gate_ref[0], preferred_element_type=jnp.float32)
    up = jnp.dot(x, up_ref[0], preferred_element_type=jnp.float32)
    table = x_ref[:, feat:].astype(jnp.float32)
    lane = lax.broadcasted_iota(jnp.int32, table.shape, 1)
    weight = jnp.sum(jnp.where(lane == chosen, table, 0.0), axis=1, keepdims=True)
    value = gate / (1.0 + jnp.exp(-gate)) * up * weight
    out_ref[...] = jnp.where(weight == 0.0, 0.0, value).astype(jnp.bfloat16)


def expert_in(x, gate, up, first):
    count, wide = x.shape
    local, feat, hidden = gate.shape
    w_spec = pl.BlockSpec((1, feat, hidden), lambda i: (i, 0, 0))
    return pl.pallas_call(
        functools.partial(expert_in_kernel, feat),
        grid=(local,),
        in_specs=[
            pl.BlockSpec(memory_space=pltpu.SMEM),
            pl.BlockSpec((count, wide), lambda i: (0, 0)),
            w_spec,
            w_spec,
        ],
        out_specs=pl.BlockSpec((count, hidden), lambda i: (0, i)),
        out_shape=jax.ShapeDtypeStruct((count, local * hidden), jnp.bfloat16),
        compiler_params=pltpu.CompilerParams(vmem_limit_bytes=VMEM_LIMIT),
        cost_estimate=pl.CostEstimate(
            flops=4 * count * local * feat * hidden,
            bytes_accessed=4 * local * feat * hidden,
            transcendentals=count * local * hidden,
        ),
        name="expert_in",
    )(first, x, gate, up)


def expert_out_kernel(act_ref, down_ref, keep_ref, send_ref):
    local, hidden, width = down_ref.shape
    sums = jnp.dot(
        act_ref[...],
        down_ref[...].reshape(local * hidden, width),
        preferred_element_type=jnp.float32,
    )
    half = sums.shape[0] // 2
    keep_ref[...] = sums[:half]
    send_ref[...] = sums[half:].astype(jnp.bfloat16)


def expert_out(act, down):
    count = act.shape[0]
    local, hidden, feat = down.shape
    width = chunk_of(feat, 512)
    out_spec = pl.BlockSpec((count // 2, width), lambda j: (0, j))
    return pl.pallas_call(
        expert_out_kernel,
        grid=(feat // width,),
        in_specs=[
            pl.BlockSpec(act.shape, lambda j: (0, 0)),
            pl.BlockSpec((local, hidden, width), lambda j: (0, 0, j)),
        ],
        out_specs=[out_spec, out_spec],
        out_shape=[
            jax.ShapeDtypeStruct((count // 2, feat), jnp.float32),
            jax.ShapeDtypeStruct((count // 2, feat), jnp.bfloat16),
        ],
        compiler_params=pltpu.CompilerParams(vmem_limit_bytes=VMEM_LIMIT),
        cost_estimate=pl.CostEstimate(
            flops=2 * count * local * hidden * feat,
            bytes_accessed=2 * local * hidden * feat,
            transcendentals=0,
        ),
        name="expert_out",
    )(act, down)


def shared_out_kernel(sizes, feat, x_ref, scale_ref, down_ref, *refs):
    outer, spread, rows = sizes
    act_refs, (keep_ref, send_ref) = refs[:spread], refs[spread:]
    parts = [
        jnp.dot(act[...], down_ref[...], preferred_element_type=jnp.float32) for act in act_refs
    ]
    sums = jnp.stack([part.reshape(outer, rows, part.shape[1]) for part in parts], axis=1)
    sums = sums.reshape(outer * spread * rows, sums.shape[3])
    inner = jnp.sum(
        x_ref[:, :feat].astype(jnp.float32) * scale_ref[...], axis=1, keepdims=True
    )
    sums = sums / (1.0 + jnp.exp(-inner))
    half = sums.shape[0] // 2
    keep_ref[...] = sums[:half]
    send_ref[...] = sums[half:]


def shared_out(x, scale, down, acts, rows):
    count, spread = x.shape[0], len(acts)
    outer = count // (spread * rows)
    out = jax.ShapeDtypeStruct((count // 2, down.shape[1]), jnp.float32)
    return pl.pallas_call(
        functools.partial(shared_out_kernel, (outer, spread, rows), scale.shape[0]),
        out_shape=[out, out],
        compiler_params=pltpu.CompilerParams(vmem_limit_bytes=VMEM_LIMIT),
        cost_estimate=pl.CostEstimate(
            flops=2 * count * down.shape[0] * down.shape[1],
            bytes_accessed=2 * down.shape[0] * down.shape[1],
            transcendentals=count,
        ),
        name="shared_out",
    )(x, scale.reshape(1, -1), down, *acts)


def narrow_sum(keep, send, kind):
    chips = lax.axis_size("narrow") // 2
    total = keep + core_swap(send).astype(jnp.float32)
    part = total.shape[0] // chips
    result = total[:part]
    for d in range(1, chips):
        result = result + x_shift(total[d * part : (d + 1) * part].astype(kind), -d).astype(
            jnp.float32
        )
    return result


def body(
    tokens,
    expert_ids,
    route_weights,
    expert_gate,
    expert_up,
    expert_down,
    shared_gate,
    shared_up,
    shared_down,
    shared_scale,
):
    rows, feat = tokens.shape
    spread = lax.axis_size("expert")
    here = lax.axis_index("expert")
    local = expert_gate.shape[0]
    lane = jnp.arange(LANES, dtype=jnp.int32)
    table = jnp.sum(
        jnp.where(
            expert_ids[:, :, None] == lane, route_weights[:, :, None].astype(jnp.float32), 0.0
        ),
        axis=1,
    ).astype(jnp.bfloat16)
    x = gather_rows(jnp.concatenate([tokens, table], axis=1))

    depth = shared_gate.shape[0]
    x_part = lax.dynamic_slice_in_dim(x, here * depth, depth, axis=1)
    hidden_parts = shared_in(x_part, shared_gate, shared_up, rows)
    hidden = hidden_parts[0].astype(jnp.float32)
    for d in range(1, spread):
        hidden = hidden + z_shift(hidden_parts[d], -d).astype(jnp.float32)
    shared_act = (jax.nn.silu(hidden[0]) * hidden[1]).astype(jnp.bfloat16)
    acts = [shared_act] + [z_shift(shared_act, d) for d in range(1, spread)]

    first = (here * local).astype(jnp.int32).reshape(1)
    act = expert_in(x, expert_gate, expert_up, first)
    routed = narrow_sum(*expert_out(act, expert_down), jnp.bfloat16)
    total = routed[:rows]
    for d in range(1, spread):
        total = total + z_shift(
            routed[d * rows : (d + 1) * rows].astype(jnp.bfloat16), -d
        ).astype(jnp.float32)

    part = narrow_sum(*shared_out(x, shared_scale, shared_down, acts, rows), jnp.float32)
    width = part.shape[1]
    for d in range(spread):
        piece = part[:rows] if d == 0 else z_shift(part[d * rows : (d + 1) * rows], -d)
        at = lax.rem(here + d, spread) * width
        old = lax.dynamic_slice_in_dim(total, at, width, axis=1)
        total = lax.dynamic_update_slice_in_dim(total, old + piece, at, axis=1)
    return total.astype(jnp.bfloat16)


def solution(mesh):
    return jax.shard_map(
        body,
        mesh=mesh,
        in_specs=(
            P(("groups", "expert", "narrow"), None),
            P(("groups", "expert", "narrow"), None),
            P(("groups", "expert", "narrow"), None),
            P("expert", None, "narrow"),
            P("expert", None, "narrow"),
            P("expert", "narrow", None),
            P("expert", "narrow"),
            P("expert", "narrow"),
            P("narrow", "expert"),
            P(),
        ),
        out_specs=P(("groups", "expert", "narrow"), None),
        check_vma=False,
    )
```

time: 546 us -> 110 us (0.20)
  waiting for transfers between devices: 280 us -> 32.2 us
  blocking collectives: 164 us -> 0 us
  matrix products: 51.3 us -> 0 us
  Pallas kernels: 0 us -> 42.5 us
  starting transfers between devices: 3.9 us -> 27.6 us
  local copies, waits for them, and re-layouts: 26.1 us -> 2.51 us
  between operations: 13.3 us -> 0.22 us
    all_to_all x2 -> x0, blocking collectives: 146 us -> none  [the longest x1 133 us: body(): lax.all_to_all(outgoing, 'expert', split_axis=0, concat_axis=0, tiled=True)]
    all_to_all x1 -> x0, waiting for transfers between devices: 144 us -> none  [body(): lax.all_to_all(result, 'expert', split_axis=0, concat_axis=0, tiled=True)]
    all_gather x1 -> x0, waiting for transfers between devices: 115 us -> none  [body(): lax.all_gather(shared_down, 'expert', axis=1, tiled=True)]
    dot_general x6 -> x0, matrix products: 51.3 us -> none  [the longest x1 23.4 us: body(): jnp.einsum('slcf,lfd->slcd', activated, expert_down, preferred_element_ty...]
    pallas_call x0 -> x4, Pallas kernels: none -> 42.5 us  [the longest x1 19.8 us: expert_in(): pl.pallas_call(functools.partial(expert_in_kernel, feat), grid=(local,),...]
    ppermute x0 -> x21, waiting for transfers between devices: none -> 32.2 us  [the longest x15 22 us: z_shift(): lax.ppermute(value, 'expert', [(i, (i + step) % spread) for i in range(sp...]
    ppermute x0 -> x21, starting transfers between devices: none -> 27.6 us  [the longest x15 24 us: z_shift(): lax.ppermute(value, 'expert', [(i, (i + step) % spread) for i in range(sp...]
    reduce_scatter x2 -> x0, waiting for transfers between devices: 20.4 us -> none  [the longest x1 20.4 us: body(): lax.psum_scatter(combined, 'narrow', scatter_dimension=0, tiled=True)]
  transfers between devices with their start and end apart: 4 -> 21, of which waited for: 3 -> 14; matrix products, arithmetic and copies ran while one was open for 12% -> 0% of each run, Pallas kernels for 0% -> 34%
where the time goes in v1:
time: 110 us; the launch traced here: 109 us
  Pallas kernels  42.5 us (39%)
  waiting for transfers between devices  32.2 us (29%)
  starting transfers between devices  27.6 us (25%)
  other arithmetic  4.25 us (4%)
  local copies, waits for them, and re-layouts  2.51 us (2%)
    ppermute x15, starting transfers between devices, z_shift(): lax.ppermute(value, 'expert', [(i, (i + step) % spread) for i in range(sp...  24 us
    ppermute x15, waiting for transfers between devices, z_shift(): lax.ppermute(value, 'expert', [(i, (i + step) % spread) for i in range(sp...  22 us
    pallas_call x1, Pallas kernels, expert_in(): pl.pallas_call(functools.partial(expert_in_kernel, feat), grid=(local,),...  19.8 us
    pallas_call x1, Pallas kernels, expert_out(): pl.pallas_call(expert_out_kernel, grid=(feat // width,), in_specs=[pl.Blo...  12.2 us
    ppermute x3, waiting for transfers between devices, x_shift(): lax.ppermute(value, 'narrow', [(i, (i + 2 * step) % size) for i in range(...  6.78 us
    pallas_call x1, Pallas kernels, shared_out(): pl.pallas_call(functools.partial(shared_out_kernel, (outer, spread, rows)...  5.34 us
    pallas_call x1, Pallas kernels, shared_in(): pl.pallas_call(functools.partial(shared_in_kernel, (outer, spread, rows))...  5.16 us
    ppermute x3, waiting for transfers between devices, core_swap(): return lax.ppermute(value, 'narrow', [(i, i ^ 1) for i in range(size)])  3.44 us
  transfers between devices with their start and end apart: 21, of which 14 were waited for; matrix products, arithmetic and copies ran while one was open for 0% of the time, Pallas kernels for 34%

profile of v1, /device:TPU:0, one launch (start us, length us, event | category | flops | bytes accessed | tf_op | source)
XLA Modules:
  0.0 109.3 jit_solution(8266673826756653402)
XLA Ops:
  0.0 0.7 convert_element_type.44
  0.7 0.8 select_reduce_fusion
  1.5 0.8 constant_dynamic-update-slice_fusion.4
  2.3 3.1 %collective-permute-start = (bf16[8,3712]{1,0:T(8,128)(2,1)S(1)}, bf16[8,3712]{1,0:T(8,128)(2,1)S(1)}, u32[]{:S(2)}, u32[]{:S(2)}) collective-permute-start(bf16[8,3712]{1,0:T(8,128)(2,1)S(1)} %get-tuple-element.39), channel_id=1, source_target_pairs={{0,4},{4,8},{8,12},{12,0},{1,5},{5,9},{9,13},{13,1},{2,6},{6,10},{... | collective-permute-start | bytes 178184 | tf_op jit(solution)/shard_map/ppermute | solution.py:25
  5.4 2.6 %collective-permute-start.1 = (bf16[8,3712]{1,0:T(8,128)(2,1)S(1)}, bf16[8,3712]{1,0:T(8,128)(2,1)S(1)}, u32[]{:S(2)}, u32[]{:S(2)}) collective-permute-start(bf16[8,3712]{1,0:T(8,128)(2,1)S(1)} %get-tuple-element.39), channel_id=1, source_target_pairs={{0,8},{4,12},{8,0},{12,4},{1,9},{5,13},{9,1},{13,5},{2,10},{6,14},... | collective-permute-start | bytes 178184 | tf_op jit(solution)/shard_map/ppermute | solution.py:25
  8.0 1.3 %collective-permute-start.2 = (bf16[8,3712]{1,0:T(8,128)(2,1)S(1)}, bf16[8,3712]{1,0:T(8,128)(2,1)S(1)}, u32[]{:S(2)}, u32[]{:S(2)}) collective-permute-start(bf16[8,3712]{1,0:T(8,128)(2,1)S(1)} %get-tuple-element.39), channel_id=1, source_target_pairs={{0,12},{4,0},{8,4},{12,8},{1,13},{5,1},{9,5},{13,9},{2,14},{6,2},{... | collective-permute-start | bytes 178184 | tf_op jit(solution)/shard_map/ppermute | solution.py:25
  9.3 0.5 collective-permute-done
  9.8 2.3 %collective-permute-done.1 = bf16[8,3712]{1,0:T(8,128)(2,1)S(1)} collective-permute-done((bf16[8,3712]{1,0:T(8,128)(2,1)S(1)}, bf16[8,3712]{1,0:T(8,128)(2,1)S(1)}, u32[]{:S(2)}, u32[]{:S(2)}) %collective-permute-start.1) | collective-permute-done | bytes 59424 | tf_op jit(solution)/shard_map/ppermute | solution.py:25
  12.1 0.4 collective-permute-done.2
  12.5 0.8 pad_maximum_fusion
  13.3 1.5 %collective-permute-start.3 = (bf16[32,3712]{1,0:T(8,128)(2,1)S(1)}, bf16[32,3712]{1,0:T(8,128)(2,1)S(1)}, u32[]{:S(2)}, u32[]{:S(2)}) collective-permute-start(bf16[32,3712]{1,0:T(8,128)(2,1)S(1)} %pad_maximum_fusion), channel_id=1, source_target_pairs={{0,2},{1,3},{2,0},{3,1},{4,6},{5,7},{6,4},{7,5},{8,10},{9,11},{10,... | collective-permute-start | bytes 712712 | tf_op jit(solution)/shard_map/ppermute | solution.py:30
  14.9 5.5 %collective-permute-done.3 = bf16[32,3712]{1,0:T(8,128)(2,1)S(1)} collective-permute-done((bf16[32,3712]{1,0:T(8,128)(2,1)S(1)}, bf16[32,3712]{1,0:T(8,128)(2,1)S(1)}, u32[]{:S(2)}, u32[]{:S(2)}) %collective-permute-start.3) | collective-permute-done | bytes 237600 | tf_op jit(solution)/shard_map/ppermute | solution.py:30
  20.4 0.1 collective-permute-start.4
  20.5 1.8 %collective-permute-done.4 = bf16[64,3712]{1,0:T(8,128)(2,1)S(1)} collective-permute-done((bf16[64,3712]{1,0:T(8,128)(2,1)S(1)}, bf16[64,3712]{1,0:T(8,128)(2,1)S(1)}, u32[]{:S(2)}, u32[]{:S(2)}) %collective-permute-start.4) | collective-permute-done | bytes 475168 | tf_op jit(solution)/shard_map/ppermute | solution.py:35
  22.4 2.3 %copy-done = bf16[896,2560]{1,0:T(8,128)(2,1)S(1)} copy-done((bf16[896,2560]{1,0:T(8,128)(2,1)S(1)}, bf16[896,2560]{1,0:T(8,128)(2,1)}, u32[]{:S(2)}) %copy-start) | copy-done | bytes 4587544
  24.7 5.2 %shared_in.1 = (bf16[2,32,2560]{2,1,0:T(8,128)(2,1)S(1)}, bf16[2,32,2560]{2,1,0:T(8,128)(2,1)S(1)}, bf16[2,32,2560]{2,1,0:T(8,128)(2,1)S(1)}, bf16[2,32,2560]{2,1,0:T(8,128)(2,1)S(1)}) custom-call(bf16[128,896]{1,0:T(8,128)(2,1)S(1)} %constant_dynamic-slice_fusion.x_ref, bf16[896,2560]{1,0:T(8,128)(2,1)S(1)} %copy-done, bf16[896,2560]{1,0:T(8,128)(2,1)} %up_ref.3), custom_call_target="tpu_custom_call" | custom-call | flops 1174405120 | bytes 10485760 | tf_op jit(solution)/shard_map/shared_in/pallas_call | solution.py:64
  29.9 1.9 %collective-permute-start.12 = (bf16[2,32,2560]{2,1,0:T(8,128)(2,1)S(1)}, bf16[2,32,2560]{2,1,0:T(8,128)(2,1)S(1)}, u32[]{:S(2)}, u32[]{:S(2)}) collective-permute-start(bf16[2,32,2560]{2,1,0:T(8,128)(2,1)S(1)} %get-tuple-element.18), channel_id=1, source_target_pairs={{0,4},{4,8},{8,12},{12,0},{1,5},{5,9},{9,13},{13,1},{2,6},{6,10},{... | collective-permute-start | bytes 983048 | tf_op jit(solution)/shard_map/ppermute | solution.py:25
  31.8 0.7 collective-permute-start.11
  32.5 1.7 %collective-permute-start.10 = (bf16[2,32,2560]{2,1,0:T(8,128)(2,1)S(1)}, bf16[2,32,2560]{2,1,0:T(8,128)(2,1)S(1)}, u32[]{:S(2)}, u32[]{:S(2)}) collective-permute-start(bf16[2,32,2560]{2,1,0:T(8,128)(2,1)S(1)} %get-tuple-element.16), channel_id=1, source_target_pairs={{0,12},{4,0},{8,4},{12,8},{1,13},{5,1},{9,5},{13,9},{2,14},{6,2},{... | collective-permute-start | bytes 983048 | tf_op jit(solution)/shard_map/ppermute | solution.py:25
  34.2 19.8 %expert_in.1.act_ref = bf16[128,4096]{1,0:T(8,128)(2,1)S(1)} custom-call(s32[1]{0:T(128)} %bitcast.first_ref, bf16[128,3712]{1,0:T(8,128)(2,1)S(1)} %constant_dynamic-update-slice_fusion.5.x_ref, bf16[8,3584,512]{2,1,0:T(8,128)(2,1)} %gate_ref.2, bf16[8,3584,512]{2,1,0:T(8,128)(2,1)} %up_ref.2), custom_call_target="tpu_custom_call" | custom-call | flops 7516192768 | bytes 58720256 | tf_op jit(solution)/shard_map/expert_in/pallas_call | solution.py:96
  54.0 12.2 %expert_out.1 = (f32[64,3584]{1,0:T(8,128)S(1)}, bf16[64,3584]{1,0:T(8,128)(2,1)S(1)}) custom-call(bf16[128,4096]{1,0:T(8,128)(2,1)S(1)} %expert_in.1.act_ref, bf16[8,512,3584]{2,1,0:T(8,128)(2,1)} %down_ref.2), custom_call_target="tpu_custom_call" | custom-call | flops 3758096384 | bytes 29360128 | tf_op jit(solution)/shard_map/expert_out/pallas_call | solution.py:134
  66.2 0.1 collective-permute-start.5
  66.3 0.2 convert_add_fusion.1
  66.5 1.6 %collective-permute-done.5 = bf16[64,3584]{1,0:T(8,128)(2,1)S(1)} collective-permute-done((bf16[64,3584]{1,0:T(8,128)(2,1)S(1)}, bf16[64,3584]{1,0:T(8,128)(2,1)S(1)}, u32[]{:S(2)}, u32[]{:S(2)}) %collective-permute-start.5) | collective-permute-done | bytes 458784 | tf_op jit(solution)/shard_map/ppermute | solution.py:35
  68.1 0.1 convert_add_fusion
  68.2 1.3 %collective-permute-start.6 = (bf16[32,3584]{1,0:T(8,128)(2,1)S(1)}, bf16[32,3584]{1,0:T(8,128)(2,1)S(1)}, u32[]{:S(2)}, u32[]{:S(2)}) collective-permute-start(bf16[32,3584]{1,0:T(8,128)(2,1)S(1)} %slice.93), channel_id=1, source_target_pairs={{0,2},{1,3},{2,0},{3,1},{4,6},{5,7},{6,4},{7,5},{8,10},{9,11},{10,... | collective-permute-start | bytes 688136 | tf_op jit(solution)/shard_map/ppermute | solution.py:30
  69.5 0.1 fusion.1.refs_0_
  69.6 0.7 collective-permute-start.13
  70.3 1.9 %collective-permute-start.14 = (bf16[32,2560]{1,0:T(8,128)(2,1)S(1)}, bf16[32,2560]{1,0:T(8,128)(2,1)S(1)}, u32[]{:S(2)}, u32[]{:S(2)}) collective-permute-start(bf16[32,2560]{1,0:T(8,128)(2,1)S(1)} %fusion.1.refs_0_), channel_id=1, source_target_pairs={{0,8},{4,12},{8,0},{12,4},{1,9},{5,13},{9,1},{13,5},{2,10},{6,14},... | collective-permute-start | bytes 491528 | tf_op jit(solution)/shard_map/ppermute | solution.py:25
  72.2 1.7 %collective-permute-start.15 = (bf16[32,2560]{1,0:T(8,128)(2,1)S(1)}, bf16[32,2560]{1,0:T(8,128)(2,1)S(1)}, u32[]{:S(2)}, u32[]{:S(2)}) collective-permute-start(bf16[32,2560]{1,0:T(8,128)(2,1)S(1)} %fusion.1.refs_0_), channel_id=1, source_target_pairs={{0,12},{4,0},{8,4},{12,8},{1,13},{5,1},{9,5},{13,9},{2,14},{6,2},{... | collective-permute-start | bytes 491528 | tf_op jit(solution)/shard_map/ppermute | solution.py:25
  73.8 4.8 %collective-permute-done.13.refs_1_ = bf16[32,2560]{1,0:T(8,128)(2,1)S(1)} collective-permute-done((bf16[32,2560]{1,0:T(8,128)(2,1)S(1)}, bf16[32,2560]{1,0:T(8,128)(2,1)S(1)}, u32[]{:S(2)}, u32[]{:S(2)}) %collective-permute-start.13) | collective-permute-done | bytes 163872 | tf_op jit(solution)/shard_map/ppermute | solution.py:25
  78.6 6.0 %collective-permute-done.14.refs_2_ = bf16[32,2560]{1,0:T(8,128)(2,1)S(1)} collective-permute-done((bf16[32,2560]{1,0:T(8,128)(2,1)S(1)}, bf16[32,2560]{1,0:T(8,128)(2,1)S(1)}, u32[]{:S(2)}, u32[]{:S(2)}) %collective-permute-start.14) | collective-permute-done | bytes 163872 | tf_op jit(solution)/shard_map/ppermute | solution.py:25
  84.6 5.3 %shared_out.1 = (f32[64,896]{1,0:T(8,128)S(1)}, f32[64,896]{1,0:T(8,128)S(1)}) custom-call(bf16[128,3712]{1,0:T(8,128)(2,1)S(1)} %constant_dynamic-update-slice_fusion.5.x_ref, f32[1,3584]{1,0:T(1,128)S(1)} %reshape.10.scale_ref, bf16[2560,896]{1,0:T(8,128)(2,1)} %down_ref.3, bf16[32,2560]{1,0:T(8,128)(2,1)S(1)} %fusion.1.refs_0_, ...), custom_call_target="tpu_custom_call" | custom-call | flops 587202560 | bytes 4587520 | tf_op jit(solution)/shard_map/shared_out/pallas_call | solution.py:177
  90.0 0.1 collective-permute-start.16
  90.2 3.4 %collective-permute-start.9 = (bf16[8,3584]{1,0:T(8,128)(2,1)S(1)}, bf16[8,3584]{1,0:T(8,128)(2,1)S(1)}, u32[]{:S(2)}, u32[]{:S(2)}) collective-permute-start(bf16[8,3584]{1,0:T(8,128)(2,1)S(1)} %get-tuple-element.26), channel_id=1, source_target_pairs={{0,4},{4,8},{8,12},{12,0},{1,5},{5,9},{9,13},{13,1},{2,6},{6,10},{... | collective-permute-start | bytes 172040 | tf_op jit(solution)/shard_map/ppermute | solution.py:25
  93.6 0.9 collective-permute-start.8
  94.4 1.6 %collective-permute-start.7 = (bf16[8,3584]{1,0:T(8,128)(2,1)S(1)}, bf16[8,3584]{1,0:T(8,128)(2,1)S(1)}, u32[]{:S(2)}, u32[]{:S(2)}) collective-permute-start(bf16[8,3584]{1,0:T(8,128)(2,1)S(1)} %get-tuple-element.25), channel_id=1, source_target_pairs={{0,12},{4,0},{8,4},{12,8},{1,13},{5,1},{9,5},{13,9},{2,14},{6,2},{... | collective-permute-start | bytes 172040 | tf_op jit(solution)/shard_map/ppermute | solution.py:25
  96.1 0.6 collective-permute-start.17
  96.7 2.9 %collective-permute-done.8 = bf16[8,3584]{1,0:T(8,128)(2,1)S(1)} collective-permute-done((bf16[8,3584]{1,0:T(8,128)(2,1)S(1)}, bf16[8,3584]{1,0:T(8,128)(2,1)S(1)}, u32[]{:S(2)}, u32[]{:S(2)}) %collective-permute-start.8) | collective-permute-done | bytes 57376 | tf_op jit(solution)/shard_map/ppermute | solution.py:25
  99.6 0.1 collective-permute-done.7
  99.8 1.3 %collective-permute-done.17 = f32[32,896]{1,0:T(8,128)S(1)} collective-permute-done((f32[32,896]{1,0:T(8,128)S(1)}, f32[32,896]{1,0:T(8,128)S(1)}, u32[]{:S(2)}, u32[]{:S(2)}) %collective-permute-start.17) | collective-permute-done | bytes 114720 | tf_op jit(solution)/shard_map/ppermute | solution.py:30
  101.1 1.8 %collective-permute-start.18 = (f32[8,896]{1,0:T(8,128)S(1)}, f32[8,896]{1,0:T(8,128)S(1)}, u32[]{:S(2)}, u32[]{:S(2)}) collective-permute-start(f32[8,896]{1,0:T(8,128)S(1)} %get-tuple-element.30), channel_id=1, source_target_pairs={{0,12},{4,0},{8,4},{12,8},{1,13},{5,1},{9,5},{13,9},{2,14},{6,2},{... | collective-permute-start | bytes 86024 | tf_op jit(solution)/shard_map/ppermute | solution.py:25
  103.0 0.0 collective-permute-start.19
  103.0 0.7 collective-permute-start.20
  103.7 1.4 %collective-permute-done.18 = f32[8,896]{1,0:T(8,128)S(1)} collective-permute-done((f32[8,896]{1,0:T(8,128)S(1)}, f32[8,896]{1,0:T(8,128)S(1)}, u32[]{:S(2)}, u32[]{:S(2)}) %collective-permute-start.18) | collective-permute-done | bytes 28704 | tf_op jit(solution)/shard_map/ppermute | solution.py:25
  105.1 2.7 %collective-permute-done.19 = f32[8,896]{1,0:T(8,128)S(1)} collective-permute-done((f32[8,896]{1,0:T(8,128)S(1)}, f32[8,896]{1,0:T(8,128)S(1)}, u32[]{:S(2)}, u32[]{:S(2)}) %collective-permute-start.19) | collective-permute-done | bytes 28704 | tf_op jit(solution)/shard_map/ppermute | solution.py:25
  107.8 0.9 collective-permute-done.20
  108.6 0.6 convert_element_type.56
  (28 shorter events, 0.4 us)
Async XLA Ops:
  2.3 7.5 %collective-permute-start = (bf16[8,3712]{1,0:T(8,128)(2,1)S(1)}, bf16[8,3712]{1,0:T(8,128)(2,1)S(1)}, u32[]{:S(2)}, u32[]{:S(2)}) collective-permute-start(bf16[8,3712]{1,0:T(8,128)(2,1)S(1)} %get-tuple-element.39), channel_id=1, source_target_pairs={{0,4},{4,8},{8,12},{12,0},{1,5},{5,9},{9,13},{13,1},{2,6},{6,10},{... | collective-permute-start | bytes 178184 | tf_op jit(solution)/shard_map/ppermute | solution.py:25
  5.4 6.7 %collective-permute-start.1 = (bf16[8,3712]{1,0:T(8,128)(2,1)S(1)}, bf16[8,3712]{1,0:T(8,128)(2,1)S(1)}, u32[]{:S(2)}, u32[]{:S(2)}) collective-permute-start(bf16[8,3712]{1,0:T(8,128)(2,1)S(1)} %get-tuple-element.39), channel_id=1, source_target_pairs={{0,8},{4,12},{8,0},{12,4},{1,9},{5,13},{9,1},{13,5},{2,10},{6,14},... | collective-permute-start | bytes 178184 | tf_op jit(solution)/shard_map/ppermute | solution.py:25
  8.0 4.5 %collective-permute-start.2 = (bf16[8,3712]{1,0:T(8,128)(2,1)S(1)}, bf16[8,3712]{1,0:T(8,128)(2,1)S(1)}, u32[]{:S(2)}, u32[]{:S(2)}) collective-permute-start(bf16[8,3712]{1,0:T(8,128)(2,1)S(1)} %get-tuple-element.39), channel_id=1, source_target_pairs={{0,12},{4,0},{8,4},{12,8},{1,13},{5,1},{9,5},{13,9},{2,14},{6,2},{... | collective-permute-start | bytes 178184 | tf_op jit(solution)/shard_map/ppermute | solution.py:25
  13.3 7.1 %collective-permute-start.3 = (bf16[32,3712]{1,0:T(8,128)(2,1)S(1)}, bf16[32,3712]{1,0:T(8,128)(2,1)S(1)}, u32[]{:S(2)}, u32[]{:S(2)}) collective-permute-start(bf16[32,3712]{1,0:T(8,128)(2,1)S(1)} %pad_maximum_fusion), channel_id=1, source_target_pairs={{0,2},{1,3},{2,0},{3,1},{4,6},{5,7},{6,4},{7,5},{8,10},{9,11},{10,... | collective-permute-start | bytes 712712 | tf_op jit(solution)/shard_map/ppermute | solution.py:30
  20.4 1.9 %collective-permute-start.4 = (bf16[64,3712]{1,0:T(8,128)(2,1)S(1)}, bf16[64,3712]{1,0:T(8,128)(2,1)S(1)}, u32[]{:S(2)}, u32[]{:S(2)}) collective-permute-start(bf16[64,3712]{1,0:T(8,128)(2,1)S(1)} %get-tuple-element.23), channel_id=1, source_target_pairs={{0,1},{1,0},{2,3},{3,2},{4,5},{5,4},{6,7},{7,6},{8,9},{9,8},{10,11... | collective-permute-start | bytes 1425416 | tf_op jit(solution)/shard_map/ppermute | solution.py:35
  22.4 2.3 %copy-start = (bf16[896,2560]{1,0:T(8,128)(2,1)S(1)}, bf16[896,2560]{1,0:T(8,128)(2,1)}, u32[]{:S(2)}) copy-start(bf16[896,2560]{1,0:T(8,128)(2,1)} %gate_ref.3) | copy-start | bytes 13762564
  29.9 36.4 %collective-permute-start.12 = (bf16[2,32,2560]{2,1,0:T(8,128)(2,1)S(1)}, bf16[2,32,2560]{2,1,0:T(8,128)(2,1)S(1)}, u32[]{:S(2)}, u32[]{:S(2)}) collective-permute-start(bf16[2,32,2560]{2,1,0:T(8,128)(2,1)S(1)} %get-tuple-element.18), channel_id=1, source_target_pairs={{0,4},{4,8},{8,12},{12,0},{1,5},{5,9},{9,13},{13,1},{2,6},{6,10},{... | collective-permute-start | bytes 983048 | tf_op jit(solution)/shard_map/ppermute | solution.py:25
  31.8 34.5 %collective-permute-start.11 = (bf16[2,32,2560]{2,1,0:T(8,128)(2,1)S(1)}, bf16[2,32,2560]{2,1,0:T(8,128)(2,1)S(1)}, u32[]{:S(2)}, u32[]{:S(2)}) collective-permute-start(bf16[2,32,2560]{2,1,0:T(8,128)(2,1)S(1)} %get-tuple-element.17), channel_id=1, source_target_pairs={{0,8},{4,12},{8,0},{12,4},{1,9},{5,13},{9,1},{13,5},{2,10},{6,14},... | collective-permute-start | bytes 983048 | tf_op jit(solution)/shard_map/ppermute | solution.py:25
  32.5 33.8 %collective-permute-start.10 = (bf16[2,32,2560]{2,1,0:T(8,128)(2,1)S(1)}, bf16[2,32,2560]{2,1,0:T(8,128)(2,1)S(1)}, u32[]{:S(2)}, u32[]{:S(2)}) collective-permute-start(bf16[2,32,2560]{2,1,0:T(8,128)(2,1)S(1)} %get-tuple-element.16), channel_id=1, source_target_pairs={{0,12},{4,0},{8,4},{12,8},{1,13},{5,1},{9,5},{13,9},{2,14},{6,2},{... | collective-permute-start | bytes 983048 | tf_op jit(solution)/shard_map/ppermute | solution.py:25
  54.0 19.8 %copy-start.1 = (f32[3584]{0:T(1024)S(1)}, f32[3584]{0:T(1024)}, u32[]{:S(2)}) copy-start(f32[3584]{0:T(1024)} %param.19) | copy-start | bytes 43012
  66.2 1.9 %collective-permute-start.5 = (bf16[64,3584]{1,0:T(8,128)(2,1)S(1)}, bf16[64,3584]{1,0:T(8,128)(2,1)S(1)}, u32[]{:S(2)}, u32[]{:S(2)}) collective-permute-start(bf16[64,3584]{1,0:T(8,128)(2,1)S(1)} %get-tuple-element.14), channel_id=1, source_target_pairs={{0,1},{1,0},{2,3},{3,2},{4,5},{5,4},{6,7},{7,6},{8,9},{9,8},{10,11... | collective-permute-start | bytes 1376264 | tf_op jit(solution)/shard_map/ppermute | solution.py:35
  68.2 21.8 %collective-permute-start.6 = (bf16[32,3584]{1,0:T(8,128)(2,1)S(1)}, bf16[32,3584]{1,0:T(8,128)(2,1)S(1)}, u32[]{:S(2)}, u32[]{:S(2)}) collective-permute-start(bf16[32,3584]{1,0:T(8,128)(2,1)S(1)} %slice.93), channel_id=1, source_target_pairs={{0,2},{1,3},{2,0},{3,1},{4,6},{5,7},{6,4},{7,5},{8,10},{9,11},{10,... | collective-permute-start | bytes 688136 | tf_op jit(solution)/shard_map/ppermute | solution.py:30
  69.6 9.0 %collective-permute-start.13 = (bf16[32,2560]{1,0:T(8,128)(2,1)S(1)}, bf16[32,2560]{1,0:T(8,128)(2,1)S(1)}, u32[]{:S(2)}, u32[]{:S(2)}) collective-permute-start(bf16[32,2560]{1,0:T(8,128)(2,1)S(1)} %fusion.1.refs_0_), channel_id=1, source_target_pairs={{0,4},{4,8},{8,12},{12,0},{1,5},{5,9},{9,13},{13,1},{2,6},{6,10},{... | collective-permute-start | bytes 491528 | tf_op jit(solution)/shard_map/ppermute | solution.py:25
  70.3 14.4 %collective-permute-start.14 = (bf16[32,2560]{1,0:T(8,128)(2,1)S(1)}, bf16[32,2560]{1,0:T(8,128)(2,1)S(1)}, u32[]{:S(2)}, u32[]{:S(2)}) collective-permute-start(bf16[32,2560]{1,0:T(8,128)(2,1)S(1)} %fusion.1.refs_0_), channel_id=1, source_target_pairs={{0,8},{4,12},{8,0},{12,4},{1,9},{5,13},{9,1},{13,5},{2,10},{6,14},... | collective-permute-start | bytes 491528 | tf_op jit(solution)/shard_map/ppermute | solution.py:25
  72.2 12.5 %collective-permute-start.15 = (bf16[32,2560]{1,0:T(8,128)(2,1)S(1)}, bf16[32,2560]{1,0:T(8,128)(2,1)S(1)}, u32[]{:S(2)}, u32[]{:S(2)}) collective-permute-start(bf16[32,2560]{1,0:T(8,128)(2,1)S(1)} %fusion.1.refs_0_), channel_id=1, source_target_pairs={{0,12},{4,0},{8,4},{12,8},{1,13},{5,1},{9,5},{13,9},{2,14},{6,2},{... | collective-permute-start | bytes 491528 | tf_op jit(solution)/shard_map/ppermute | solution.py:25
  90.0 6.0 %collective-permute-start.16 = (f32[64,896]{1,0:T(8,128)S(1)}, f32[64,896]{1,0:T(8,128)S(1)}, u32[]{:S(2)}, u32[]{:S(2)}) collective-permute-start(f32[64,896]{1,0:T(8,128)S(1)} %get-tuple-element.20), channel_id=1, source_target_pairs={{0,1},{1,0},{2,3},{3,2},{4,5},{5,4},{6,7},{7,6},{8,9},{9,8},{10,11... | collective-permute-start | bytes 688136 | tf_op jit(solution)/shard_map/ppermute | solution.py:35
  90.2 6.5 %collective-permute-start.9 = (bf16[8,3584]{1,0:T(8,128)(2,1)S(1)}, bf16[8,3584]{1,0:T(8,128)(2,1)S(1)}, u32[]{:S(2)}, u32[]{:S(2)}) collective-permute-start(bf16[8,3584]{1,0:T(8,128)(2,1)S(1)} %get-tuple-element.26), channel_id=1, source_target_pairs={{0,4},{4,8},{8,12},{12,0},{1,5},{5,9},{9,13},{13,1},{2,6},{6,10},{... | collective-permute-start | bytes 172040 | tf_op jit(solution)/shard_map/ppermute | solution.py:25
  93.6 6.1 %collective-permute-start.8 = (bf16[8,3584]{1,0:T(8,128)(2,1)S(1)}, bf16[8,3584]{1,0:T(8,128)(2,1)S(1)}, u32[]{:S(2)}, u32[]{:S(2)}) collective-permute-start(bf16[8,3584]{1,0:T(8,128)(2,1)S(1)} %get-tuple-element.27), channel_id=1, source_target_pairs={{0,8},{4,12},{8,0},{12,4},{1,9},{5,13},{9,1},{13,5},{2,10},{6,14},... | collective-permute-start | bytes 172040 | tf_op jit(solution)/shard_map/ppermute | solution.py:25
  94.4 5.3 %collective-permute-start.7 = (bf16[8,3584]{1,0:T(8,128)(2,1)S(1)}, bf16[8,3584]{1,0:T(8,128)(2,1)S(1)}, u32[]{:S(2)}, u32[]{:S(2)}) collective-permute-start(bf16[8,3584]{1,0:T(8,128)(2,1)S(1)} %get-tuple-element.25), channel_id=1, source_target_pairs={{0,12},{4,0},{8,4},{12,8},{1,13},{5,1},{9,5},{13,9},{2,14},{6,2},{... | collective-permute-start | bytes 172040 | tf_op jit(solution)/shard_map/ppermute | solution.py:25
  96.1 5.0 %collective-permute-start.17 = (f32[32,896]{1,0:T(8,128)S(1)}, f32[32,896]{1,0:T(8,128)S(1)}, u32[]{:S(2)}, u32[]{:S(2)}) collective-permute-start(f32[32,896]{1,0:T(8,128)S(1)} %slice.69), channel_id=1, source_target_pairs={{0,2},{1,3},{2,0},{3,1},{4,6},{5,7},{6,4},{7,5},{8,10},{9,11},{10,... | collective-permute-start | bytes 344072 | tf_op jit(solution)/shard_map/ppermute | solution.py:30
  101.1 3.9 %collective-permute-start.18 = (f32[8,896]{1,0:T(8,128)S(1)}, f32[8,896]{1,0:T(8,128)S(1)}, u32[]{:S(2)}, u32[]{:S(2)}) collective-permute-start(f32[8,896]{1,0:T(8,128)S(1)} %get-tuple-element.30), channel_id=1, source_target_pairs={{0,12},{4,0},{8,4},{12,8},{1,13},{5,1},{9,5},{13,9},{2,14},{6,2},{... | collective-permute-start | bytes 86024 | tf_op jit(solution)/shard_map/ppermute | solution.py:25
  103.0 4.8 %collective-permute-start.19 = (f32[8,896]{1,0:T(8,128)S(1)}, f32[8,896]{1,0:T(8,128)S(1)}, u32[]{:S(2)}, u32[]{:S(2)}) collective-permute-start(f32[8,896]{1,0:T(8,128)S(1)} %get-tuple-element.29), channel_id=1, source_target_pairs={{0,8},{4,12},{8,0},{12,4},{1,9},{5,13},{9,1},{13,5},{2,10},{6,14},... | collective-permute-start | bytes 86024 | tf_op jit(solution)/shard_map/ppermute | solution.py:25
  103.0 5.7 %collective-permute-start.20 = (f32[8,896]{1,0:T(8,128)S(1)}, f32[8,896]{1,0:T(8,128)S(1)}, u32[]{:S(2)}, u32[]{:S(2)}) collective-permute-start(f32[8,896]{1,0:T(8,128)S(1)} %get-tuple-element.28), channel_id=1, source_target_pairs={{0,4},{4,8},{8,12},{12,0},{1,5},{5,9},{9,13},{13,1},{2,6},{6,10},{... | collective-permute-start | bytes 86024 | tf_op jit(solution)/shard_map/ppermute | solution.py:25

commit v2 on v1

v2 whole, which is shorter than its diff:
```python
import functools

import jax
import jax.numpy as jnp
from jax import lax
from jax.experimental import pallas as pl
from jax.experimental.pallas import tpu as pltpu
from jax.sharding import PartitionSpec as P

EXPERTS = 32
LANES = 128
VMEM_LIMIT = 48 * 2**20
VMEM_WHOLE = 60 * 2**20


def chunk_of(width, most):
    best = width
    for size in range(LANES, most + 1, LANES):
        if width % size == 0:
            best = size
    return best


def z_shift(value, step):
    spread = lax.axis_size("expert")
    return lax.ppermute(value, "expert", [(i, (i + step) % spread) for i in range(spread)])


def x_shift(value, step):
    size = lax.axis_size("narrow")
    return lax.ppermute(value, "narrow", [(i, (i + 2 * step) % size) for i in range(size)])


def core_swap(value):
    size = lax.axis_size("narrow")
    return lax.ppermute(value, "narrow", [(i, i ^ 1) for i in range(size)])


def gather_column(pieces):
    return [pieces[0]] + [z_shift(piece, d) for d, piece in enumerate(pieces) if d > 0]


def gather_plane(column):
    chips = lax.axis_size("narrow") // 2
    return [column] + [x_shift(column, d) for d in range(1, chips)]


def both_cores(plane):
    return jnp.concatenate([plane, core_swap(plane)], axis=0)


def join(*lists):
    values = iter(lax.optimization_barrier([value for part in lists for value in part]))
    return [[next(values) for _ in part] for part in lists]


def stream(source, buffer, sems, width, first=0):
    copies = []
    for j in range(buffer.shape[-1] // width):
        lead = (slice(None),) * (len(buffer.shape) - 1)
        copies.append(
            pltpu.make_async_copy(
                source.at[lead + (pl.ds(first + j * width, width),)],
                buffer.at[lead + (pl.ds(j * width, width),)],
                sems.at[j],
            )
        )
        copies[-1].start()
    return copies


def prepare_kernel(tokens_ref, ids_ref, weights_ref, out_ref):
    feat = tokens_ref.shape[1]
    ids = ids_ref[...]
    weights = weights_ref[...].astype(jnp.float32)
    lane = lax.broadcasted_iota(jnp.int32, (ids.shape[0], LANES), 1)
    table = jnp.zeros(lane.shape, jnp.float32)
    for k in range(ids.shape[1]):
        table = jnp.where(lane == ids[:, k : k + 1], weights[:, k : k + 1], table)
    out_ref[:, :feat] = tokens_ref[...]
    out_ref[:, feat:] = table.astype(jnp.bfloat16)


def prepare(tokens, ids, weights):
    rows, feat = tokens.shape
    return pl.pallas_call(
        prepare_kernel,
        out_shape=jax.ShapeDtypeStruct((rows, feat + LANES), jnp.bfloat16),
        compiler_params=pltpu.CompilerParams(vmem_limit_bytes=VMEM_WHOLE),
        cost_estimate=pl.CostEstimate(
            flops=0, bytes_accessed=4 * tokens.size, transcendentals=0
        ),
        name="prepare",
    )(tokens, ids, weights)


def shared_in_kernel(sizes, width, gate_ref, up_ref, *refs):
    outer, spread, rows = sizes
    x_refs, out_refs = refs[:outer], refs[outer : outer + spread]
    gate_buf, up_buf, sems = refs[outer + spread :]
    work = []
    for half, (ref, buf) in enumerate(((gate_ref, gate_buf), (up_ref, up_buf))):
        work.append((half, buf, pltpu.make_async_copy(ref, buf, sems.at[half])))
        work[-1][2].start()
    x = jnp.concatenate([ref[...].astype(jnp.float32) for ref in x_refs], axis=0)
    x = x.astype(jnp.bfloat16)
    for half, buf, copy in work:
        copy.wait()
        for j in range(buf.shape[1] // width):
            columns = pl.ds(j * width, width)
            sums = jnp.dot(x, buf[:, columns], preferred_element_type=jnp.float32)
            sums = sums.reshape(outer, spread, rows, width)
            for d in range(spread):
                block = sums[:, d].reshape(outer * rows, width)
                out_refs[d][half, :, columns] = block.astype(jnp.bfloat16)


def shared_in(pieces, gate, up, rows):
    depth, hidden = gate.shape
    outer, spread = len(pieces), lax.axis_size("expert")
    count = outer * spread * rows
    whole = pl.BlockSpec(memory_space=pltpu.VMEM)
    apart = pl.BlockSpec(memory_space=pl.ANY)
    return pl.pallas_call(
        functools.partial(shared_in_kernel, (outer, spread, rows), chunk_of(hidden, 512)),
        in_specs=[apart, apart] + [whole] * outer,
        out_shape=[jax.ShapeDtypeStruct((2, outer * rows, hidden), jnp.bfloat16)] * spread,
        scratch_shapes=[pltpu.VMEM(gate.shape, gate.dtype)] * 2 + [pltpu.SemaphoreType.DMA((2,))],
        compiler_params=pltpu.CompilerParams(vmem_limit_bytes=VMEM_WHOLE),
        cost_estimate=pl.CostEstimate(
            flops=4 * count * depth * hidden,
            bytes_accessed=4 * depth * hidden + 4 * count * hidden,
            transcendentals=0,
        ),
        name="shared_in",
    )(gate, up, *pieces)


def expert_in_kernel(feat, first_ref, x_ref, scale_ref, gate_ref, up_ref, out_ref, branch_ref):
    @pl.when(pl.program_id(0) == 0)
    def _():
        inner = jnp.sum(
            x_ref[:, :feat].astype(jnp.float32) * scale_ref[...], axis=1, keepdims=True
        )
        branch_ref[...] = jnp.broadcast_to(1.0 / (1.0 + jnp.exp(-inner)), branch_ref.shape)

    chosen = first_ref[0] + pl.program_id(0)
    x = x_ref[:, :feat]
    gate = jnp.dot(x, gate_ref[0], preferred_element_type=jnp.float32)
    up = jnp.dot(x, up_ref[0], preferred_element_type=jnp.float32)
    table = x_ref[:, feat:].astype(jnp.float32)
    lane = lax.broadcasted_iota(jnp.int32, table.shape, 1)
    weight = jnp.sum(jnp.where(lane == chosen, table, 0.0), axis=1, keepdims=True)
    value = gate / (1.0 + jnp.exp(-gate)) * up * weight
    out_ref[...] = jnp.where(weight == 0.0, 0.0, value).astype(jnp.bfloat16)


def expert_in(x, scale, gate, up, first):
    count, wide = x.shape
    local, feat, hidden = gate.shape
    w_spec = pl.BlockSpec((1, feat, hidden), lambda i: (i, 0, 0))
    return pl.pallas_call(
        functools.partial(expert_in_kernel, feat),
        grid=(local,),
        in_specs=[
            pl.BlockSpec(memory_space=pltpu.SMEM),
            pl.BlockSpec((count, wide), lambda i: (0, 0)),
            pl.BlockSpec((1, feat), lambda i: (0, 0)),
            w_spec,
            w_spec,
        ],
        out_specs=[
            pl.BlockSpec((count, hidden), lambda i: (0, i)),
            pl.BlockSpec((count, LANES), lambda i: (0, 0)),
        ],
        out_shape=[
            jax.ShapeDtypeStruct((count, local * hidden), jnp.bfloat16),
            jax.ShapeDtypeStruct((count, LANES), jnp.float32),
        ],
        compiler_params=pltpu.CompilerParams(vmem_limit_bytes=VMEM_LIMIT),
        cost_estimate=pl.CostEstimate(
            flops=4 * count * local * feat * hidden,
            bytes_accessed=4 * local * feat * hidden,
            transcendentals=count * local * hidden,
        ),
        name="expert_in",
    )(first, x, scale.reshape(1, feat), gate, up)


def expert_out_kernel(first, width, act_ref, down_ref, keep_ref, send_ref, buf, sems):
    local, hidden, columns = buf.shape
    copies = stream(down_ref, buf, sems, width, first)
    act = act_ref[...]
    half = act.shape[0] // 2
    for j, copy in enumerate(copies):
        at = pl.ds(j * width, width)
        copy.wait()
        sums = jnp.dot(
            act, buf[:, :, at].reshape(local * hidden, width), preferred_element_type=jnp.float32
        )
        keep_ref[:, at] = sums[:half]
        send_ref[:, at] = sums[half:].astype(jnp.bfloat16)


def expert_out(act, down, first, columns):
    count = act.shape[0]
    local, hidden, _ = down.shape
    width = chunk_of(columns, 256)
    whole = pl.BlockSpec(memory_space=pltpu.VMEM)
    return pl.pallas_call(
        functools.partial(expert_out_kernel, first, width),
        in_specs=[whole, pl.BlockSpec(memory_space=pl.ANY)],
        out_specs=[whole, whole],
        out_shape=[
            jax.ShapeDtypeStruct((count // 2, columns), jnp.float32),
            jax.ShapeDtypeStruct((count // 2, columns), jnp.bfloat16),
        ],
        scratch_shapes=[
            pltpu.VMEM((local, hidden, columns), down.dtype),
            pltpu.SemaphoreType.DMA((columns // width,)),
        ],
        compiler_params=pltpu.CompilerParams(vmem_limit_bytes=VMEM_LIMIT),
        cost_estimate=pl.CostEstimate(
            flops=2 * count * local * hidden * columns,
            bytes_accessed=2 * local * hidden * columns,
            transcendentals=0,
        ),
        name="expert_out",
    )(act, down)


def shared_out_kernel(sizes, branch_ref, down_ref, *refs):
    outer, spread, rows = sizes
    act_refs, (keep_ref, send_ref) = refs[:spread], refs[spread:]
    act = jnp.concatenate([ref[...] for ref in act_refs], axis=0)
    sums = jnp.dot(act, down_ref[...], preferred_element_type=jnp.float32)
    width = sums.shape[1]
    sums = jnp.swapaxes(sums.reshape(spread, outer, rows, width), 0, 1)
    sums = sums.reshape(outer * spread * rows, width) * branch_ref[:, :1]
    half = sums.shape[0] // 2
    keep_ref[...] = sums[:half]
    send_ref[...] = sums[half:]


def shared_out(branch, down, acts, rows):
    count, spread = branch.shape[0], len(acts)
    outer = count // (spread * rows)
    out = jax.ShapeDtypeStruct((count // 2, down.shape[1]), jnp.float32)
    return pl.pallas_call(
        functools.partial(shared_out_kernel, (outer, spread, rows)),
        out_shape=[out, out],
        compiler_params=pltpu.CompilerParams(vmem_limit_bytes=VMEM_LIMIT),
        cost_estimate=pl.CostEstimate(
            flops=2 * count * down.shape[0] * down.shape[1],
            bytes_accessed=2 * down.shape[0] * down.shape[1],
            transcendentals=0,
        ),
        name="shared_out",
    )(branch, down, *acts)


def narrow_sum(keep, send, kind):
    chips = lax.axis_size("narrow") // 2
    total = keep + core_swap(send).astype(jnp.float32)
    part = total.shape[0] // chips
    result = total[:part]
    for d in range(1, chips):
        result = result + x_shift(total[d * part : (d + 1) * part].astype(kind), -d).astype(
            jnp.float32
        )
    return result


def body(
    tokens,
    expert_ids,
    route_weights,
    expert_gate,
    expert_up,
    expert_down,
    shared_gate,
    shared_up,
    shared_down,
    shared_scale,
):
    rows, feat = tokens.shape
    spread = lax.axis_size("expert")
    here = lax.axis_index("expert")
    local = expert_gate.shape[0]
    depth = shared_gate.shape[0]
    own = prepare(tokens, expert_ids, route_weights)
    column = jnp.concatenate(gather_column([own] * spread), axis=0)
    part = lax.dynamic_slice_in_dim(column, here * depth, depth, axis=1)
    parts, (column,) = join(gather_plane(part), [column])
    parts = parts + [core_swap(piece) for piece in parts]
    hidden_parts = shared_in(parts, shared_gate, shared_up, rows)
    plane, hidden_parts = join(gather_plane(column), hidden_parts)
    x = both_cores(jnp.concatenate(plane, axis=0))

    first = (here * local).astype(jnp.int32).reshape(1)
    act, branch = expert_in(x, shared_scale, expert_gate, expert_up, first)
    middle = feat // LANES // 2 * LANES
    keep, send = expert_out(act, expert_down, 0, middle)
    arrived = [z_shift(hidden_parts[d], -d) for d in range(1, spread)]
    arrived, (keep, send) = join(arrived, [keep, send])
    hidden = hidden_parts[0].astype(jnp.float32)
    for piece in arrived:
        hidden = hidden + piece.astype(jnp.float32)
    shared_act = (jax.nn.silu(hidden[0]) * hidden[1]).astype(jnp.bfloat16)
    (act,), (shared_act,) = join([act], [shared_act])
    acts = gather_column([shared_act] * spread)
    left = narrow_sum(keep, send, jnp.bfloat16)
    right = expert_out(act, expert_down, middle, feat - middle)
    acts, right, (left,) = join(acts, right, [left])
    right = narrow_sum(*right, jnp.bfloat16)
    routed = jnp.concatenate([left, right], axis=1)

    part = narrow_sum(*shared_out(branch, shared_down, acts, rows), jnp.float32)
    both = jnp.concatenate([routed, part], axis=1)
    pieces = [both[:rows]] + [
        z_shift(both[d * rows : (d + 1) * rows].astype(jnp.bfloat16), -d).astype(jnp.float32)
        for d in range(1, spread)
    ]
    total = pieces[0][:, :feat]
    for piece in pieces[1:]:
        total = total + piece[:, :feat]
    width = part.shape[1]
    for d, piece in enumerate(pieces):
        at = lax.rem(here + d, spread) * width
        old = lax.dynamic_slice_in_dim(total, at, width, axis=1)
        total = lax.dynamic_update_slice_in_dim(total, old + piece[:, feat:], at, axis=1)
    return total.astype(jnp.bfloat16)


def solution(mesh):
    return jax.shard_map(
        body,
        mesh=mesh,
        in_specs=(
            P(("groups", "expert", "narrow"), None),
            P(("groups", "expert", "narrow"), None),
            P(("groups", "expert", "narrow"), None),
            P("expert", None, "narrow"),
            P("expert", None, "narrow"),
            P("expert", "narrow", None),
            P("expert", "narrow"),
            P("expert", "narrow"),
            P("narrow", "expert"),
            P(),
        ),
        out_specs=P(("groups", "expert", "narrow"), None),
        check_vma=False,
    )
```

time: 110 us -> 98 us (0.89)
  waiting for transfers between devices: 32.2 us -> 25.2 us
  other arithmetic: 4.25 us -> 2.14 us
  local copies, waits for them, and re-layouts: 2.51 us -> 1.19 us
    ppermute x15 -> x12, waiting for transfers between devices: 22 us -> 15.7 us  [z_shift(): lax.ppermute(value, 'expert', [(i, (i + step) % spread) for i in range(sp...]
    pallas_call x1, Pallas kernels: 5.34 us -> 0.86 us  [shared_out(): pl.pallas_call(functools.partial(shared_out_kernel, (outer, spread, rows)...]
    ppermute x15 -> x12, starting transfers between devices: 24 us -> 19.9 us  [z_shift(): lax.ppermute(value, 'expert', [(i, (i + step) % spread) for i in range(sp...]
    pallas_call x2 -> x4, Pallas kernels: 17.3 us -> 21.3 us  [the longest x2 13.3 us: expert_out(): pl.pallas_call(functools.partial(expert_out_kernel, first, width), in_spe...]
    ppermute x3 -> x6, waiting for transfers between devices: 3.44 us -> 1.33 us  [core_swap(): return lax.ppermute(value, 'narrow', [(i, i ^ 1) for i in range(size)])]
    ppermute x3 -> x5, starting transfers between devices: 3.43 us -> 5.39 us  [x_shift(): lax.ppermute(value, 'narrow', [(i, (i + 2 * step) % size) for i in range(...]
    ppermute x3 -> x5, waiting for transfers between devices: 6.78 us -> 8.19 us  [x_shift(): lax.ppermute(value, 'narrow', [(i, (i + 2 * step) % size) for i in range(...]
    unnamed x7 -> x16, local copies, waits for them, and re-layouts: 2.35 us -> 1.13 us
  transfers between devices with their start and end apart: 21 -> 23, of which waited for: 14 -> 13; matrix products, arithmetic and copies ran while one was open for 0% -> 1% of each run, Pallas kernels for 34% -> 42%
where the time goes in v2:
time: 98 us; the launch traced here: 97.7 us
  Pallas kernels  42.3 us (43%)
  starting transfers between devices  26.6 us (27%)
  waiting for transfers between devices  25.2 us (26%)
  other arithmetic  2.14 us (2%)
  local copies, waits for them, and re-layouts  1.19 us (1%)
    pallas_call x1, Pallas kernels, expert_in(): pl.pallas_call(functools.partial(expert_in_kernel, feat), grid=(local,),...  20.1 us
    ppermute x12, starting transfers between devices, z_shift(): lax.ppermute(value, 'expert', [(i, (i + step) % spread) for i in range(sp...  19.9 us
    ppermute x12, waiting for transfers between devices, z_shift(): lax.ppermute(value, 'expert', [(i, (i + step) % spread) for i in range(sp...  15.7 us
    pallas_call x2, Pallas kernels, expert_out(): pl.pallas_call(functools.partial(expert_out_kernel, first, width), in_spe...  13.3 us
    ppermute x5, waiting for transfers between devices, x_shift(): lax.ppermute(value, 'narrow', [(i, (i + 2 * step) % size) for i in range(...  8.19 us
    pallas_call x1, Pallas kernels, shared_in(): pl.pallas_call(functools.partial(shared_in_kernel, (outer, spread, rows),...  6.54 us
    ppermute x5, starting transfers between devices, x_shift(): lax.ppermute(value, 'narrow', [(i, (i + 2 * step) % size) for i in range(...  5.39 us
  transfers between devices with their start and end apart: 23, of which 13 were waited for; matrix products, arithmetic and copies ran while one was open for 1% of the time, Pallas kernels for 42%

profile of v2, /device:TPU:0, one launch (start us, length us, event | category | flops | bytes accessed | tf_op | source)
XLA Modules:
  0.0 97.7 jit_solution(14682379409593751839)
XLA Ops:
  0.0 1.6 %prepare.1 = bf16[8,3712]{1,0:T(8,128)(2,1)} custom-call(bf16[8,3584]{1,0:T(8,128)(2,1)} %tokens_ref.1, s32[8,8]{1,0:T(8,128)} %ids_ref.1, bf16[8,8]{1,0:T(8,128)(2,1)} %weights_ref.1), custom_call_target="tpu_custom_call" | custom-call | bytes 114688 | tf_op jit(solution)/shard_map/prepare/pallas_call | solution.py:86
  1.6 3.0 %collective-permute-start = (bf16[8,3712]{1,0:T(8,128)(2,1)}, bf16[8,3712]{1,0:T(8,128)(2,1)S(1)}, u32[]{:S(2)}, u32[]{:S(2)}) collective-permute-start(bf16[8,3712]{1,0:T(8,128)(2,1)} %prepare.1), channel_id=1, source_target_pairs={{0,4},{4,8},{8,12},{12,0},{1,5},{5,9},{9,13},{13,1},{2,6},{6,10},{... | collective-permute-start | bytes 178184 | tf_op jit(solution)/shard_map/ppermute | solution.py:26
  4.6 2.6 %collective-permute-start.1 = (bf16[8,3712]{1,0:T(8,128)(2,1)}, bf16[8,3712]{1,0:T(8,128)(2,1)S(1)}, u32[]{:S(2)}, u32[]{:S(2)}) collective-permute-start(bf16[8,3712]{1,0:T(8,128)(2,1)} %prepare.1), channel_id=1, source_target_pairs={{0,8},{4,12},{8,0},{12,4},{1,9},{5,13},{9,1},{13,5},{2,10},{6,14},... | collective-permute-start | bytes 178184 | tf_op jit(solution)/shard_map/ppermute | solution.py:26
  7.2 1.3 %collective-permute-start.2 = (bf16[8,3712]{1,0:T(8,128)(2,1)}, bf16[8,3712]{1,0:T(8,128)(2,1)S(1)}, u32[]{:S(2)}, u32[]{:S(2)}) collective-permute-start(bf16[8,3712]{1,0:T(8,128)(2,1)} %prepare.1), channel_id=1, source_target_pairs={{0,12},{4,0},{8,4},{12,8},{1,13},{5,1},{9,5},{13,9},{2,14},{6,2},{... | collective-permute-start | bytes 178184 | tf_op jit(solution)/shard_map/ppermute | solution.py:26
  8.5 0.7 collective-permute-done
  9.2 2.3 %collective-permute-done.1 = bf16[8,3712]{1,0:T(8,128)(2,1)S(1)} collective-permute-done((bf16[8,3712]{1,0:T(8,128)(2,1)}, bf16[8,3712]{1,0:T(8,128)(2,1)S(1)}, u32[]{:S(2)}, u32[]{:S(2)}) %collective-permute-start.1) | collective-permute-done | bytes 59424 | tf_op jit(solution)/shard_map/ppermute | solution.py:26
  11.5 0.4 collective-permute-done.2
  11.9 0.8 pad_maximum_fusion.2
  12.8 0.0 copy-start.5
  12.8 1.5 %collective-permute-start.3 = (bf16[32,896]{1,0:T(8,128)(2,1)S(1)}, bf16[32,896]{1,0:T(8,128)(2,1)S(1)}, u32[]{:S(2)}, u32[]{:S(2)}) collective-permute-start(bf16[32,896]{1,0:T(8,128)(2,1)S(1)} %constant_dynamic-slice_fusion.refs_0_), channel_id=1, source_target_pairs={{0,2},{1,3},{2,0},{3,1},{4,6},{5,7},{6,4},{7,5},{8,10},{9,11},{10,... | collective-permute-start | bytes 172040 | tf_op jit(solution)/shard_map/ppermute | solution.py:31
  14.3 2.7 %collective-permute-done.3.refs_1_ = bf16[32,896]{1,0:T(8,128)(2,1)S(1)} collective-permute-done((bf16[32,896]{1,0:T(8,128)(2,1)S(1)}, bf16[32,896]{1,0:T(8,128)(2,1)S(1)}, u32[]{:S(2)}, u32[]{:S(2)}) %collective-permute-start.3) | collective-permute-done | bytes 57376 | tf_op jit(solution)/shard_map/ppermute | solution.py:31
  17.0 1.5 %collective-permute-start.4 = (bf16[32,3712]{1,0:T(8,128)(2,1)S(1)}, bf16[32,3712]{1,0:T(8,128)(2,1)S(1)}, u32[]{:S(2)}, u32[]{:S(2)}) collective-permute-start(bf16[32,3712]{1,0:T(8,128)(2,1)S(1)} %pad_maximum_fusion.2), channel_id=1, source_target_pairs={{0,2},{1,3},{2,0},{3,1},{4,6},{5,7},{6,4},{7,5},{8,10},{9,11},{10,... | collective-permute-start | bytes 712712 | tf_op jit(solution)/shard_map/ppermute | solution.py:31
  18.5 0.5 collective-permute-start.6
  19.0 0.7 collective-permute-done.5.refs_2_
  19.8 0.2 collective-permute-done.6.refs_3_
  19.9 0.5 copy-done.3
  20.4 0.6 copy-done.4
  21.0 6.5 %shared_in.1 = (bf16[2,32,2560]{2,1,0:T(8,128)(2,1)}, bf16[2,32,2560]{2,1,0:T(8,128)(2,1)}, bf16[2,32,2560]{2,1,0:T(8,128)(2,1)}, bf16[2,32,2560]{2,1,0:T(8,128)(2,1)}) custom-call(bf16[896,2560]{1,0:T(8,128)(2,1)} %gate_ref.2, bf16[896,2560]{1,0:T(8,128)(2,1)} %up_ref.2, bf16[32,896]{1,0:T(8,128)(2,1)} %copy-done.1, bf16[32,896]{1,0:T(8,128)(2,1)} %copy-done.2, ...), custom_call_target="tpu_custom_call" | custom-call | flops 1174405120 | bytes 10485760 | tf_op jit(solution)/shard_map/shared_in/pallas_call | solution.py:124
  27.6 0.2 collective-permute-start.7
  27.8 1.3 %collective-permute-start.10 = (bf16[2,32,2560]{2,1,0:T(8,128)(2,1)}, bf16[2,32,2560]{2,1,0:T(8,128)(2,1)S(1)}, u32[]{:S(2)}, u32[]{:S(2)}) collective-permute-start(bf16[2,32,2560]{2,1,0:T(8,128)(2,1)} %get-tuple-element.53), channel_id=1, source_target_pairs={{0,4},{4,8},{8,12},{12,0},{1,5},{5,9},{9,13},{13,1},{2,6},{6,10},{... | collective-permute-start | bytes 983048 | tf_op jit(solution)/shard_map/ppermute | solution.py:26
  29.2 2.5 %collective-permute-start.8 = (bf16[2,32,2560]{2,1,0:T(8,128)(2,1)}, bf16[2,32,2560]{2,1,0:T(8,128)(2,1)S(1)}, u32[]{:S(2)}, u32[]{:S(2)}) collective-permute-start(bf16[2,32,2560]{2,1,0:T(8,128)(2,1)} %get-tuple-element.51), channel_id=1, source_target_pairs={{0,12},{4,0},{8,4},{12,8},{1,13},{5,1},{9,5},{13,9},{2,14},{6,2},{... | collective-permute-start | bytes 983048 | tf_op jit(solution)/shard_map/ppermute | solution.py:26
  31.7 0.1 pad_maximum_fusion.x_ref
  31.8 20.1 %expert_in.1 = (bf16[128,4096]{1,0:T(8,128)(2,1)S(1)}, f32[128,128]{1,0:T(8,128)S(1)}) custom-call(s32[1]{0:T(128)} %bitcast.first_ref, bf16[128,3712]{1,0:T(8,128)(2,1)S(1)} %pad_maximum_fusion.x_ref, f32[1,3584]{1,0:T(1,128)S(1)} %reshape.7.scale_ref, bf16[8,3584,512]{2,1,0:T(8,128)(2,1)} %gate_ref.3, bf16[8,3584,512]{2,1,0:T(8,128)(2,1)} %up_ref.3), custom_call_target="tpu_custom_call" | custom-call | flops 7516192768 | bytes 58720256 | tf_op jit(solution)/shard_map/expert_in/pallas_call | solution.py:162
  51.9 6.5 %expert_out.2 = (f32[64,1792]{1,0:T(8,128)S(1)}, bf16[64,1792]{1,0:T(8,128)(2,1)S(1)}) custom-call(bf16[128,4096]{1,0:T(8,128)(2,1)S(1)} %get-tuple-element.60.act_ref, bf16[8,512,3584]{2,1,0:T(8,128)(2,1)} %down_ref.4), custom_call_target="tpu_custom_call" | custom-call | flops 1879048192 | bytes 14680064 | tf_op jit(solution)/shard_map/expert_out/pallas_call | solution.py:210
  58.4 2.2 %collective-permute-done.9 = bf16[2,32,2560]{2,1,0:T(8,128)(2,1)S(1)} collective-permute-done((bf16[2,32,2560]{2,1,0:T(8,128)(2,1)}, bf16[2,32,2560]{2,1,0:T(8,128)(2,1)S(1)}, u32[]{:S(2)}, u32[]{:S(2)}) %collective-permute-start.9) | collective-permute-done | bytes 327712 | tf_op jit(solution)/shard_map/ppermute | solution.py:26
  60.7 0.2 convert_add_fusion
  60.8 0.1 fusion.1.refs_0_
  60.9 0.1 collective-permute-start.11
  61.0 1.0 %collective-permute-start.12 = (bf16[32,2560]{1,0:T(8,128)(2,1)S(1)}, bf16[32,2560]{1,0:T(8,128)(2,1)S(1)}, u32[]{:S(2)}, u32[]{:S(2)}) collective-permute-start(bf16[32,2560]{1,0:T(8,128)(2,1)S(1)} %fusion.1.refs_0_), channel_id=1, source_target_pairs={{0,8},{4,12},{8,0},{12,4},{1,9},{5,13},{9,1},{13,5},{2,10},{6,14},... | collective-permute-start | bytes 491528 | tf_op jit(solution)/shard_map/ppermute | solution.py:26
  62.0 2.8 %collective-permute-start.13 = (bf16[32,2560]{1,0:T(8,128)(2,1)S(1)}, bf16[32,2560]{1,0:T(8,128)(2,1)S(1)}, u32[]{:S(2)}, u32[]{:S(2)}) collective-permute-start(bf16[32,2560]{1,0:T(8,128)(2,1)S(1)} %fusion.1.refs_0_), channel_id=1, source_target_pairs={{0,12},{4,0},{8,4},{12,8},{1,13},{5,1},{9,5},{13,9},{2,14},{6,2},{... | collective-permute-start | bytes 491528 | tf_op jit(solution)/shard_map/ppermute | solution.py:26
  64.8 0.0 slice-start
  64.9 0.0 slice-start.1
  64.9 0.6 collective-permute-start.15
  65.5 6.8 %expert_out.3 = (f32[64,1792]{1,0:T(8,128)S(1)}, bf16[64,1792]{1,0:T(8,128)(2,1)S(1)}) custom-call(bf16[128,4096]{1,0:T(8,128)(2,1)S(1)} %get-tuple-element.60.act_ref, bf16[8,512,3584]{2,1,0:T(8,128)(2,1)} %down_ref.4), custom_call_target="tpu_custom_call" | custom-call | flops 1879048192 | bytes 14680064 | tf_op jit(solution)/shard_map/expert_out/pallas_call | solution.py:210
  72.3 3.7 %collective-permute-done.12.refs_2_ = bf16[32,2560]{1,0:T(8,128)(2,1)S(1)} collective-permute-done((bf16[32,2560]{1,0:T(8,128)(2,1)S(1)}, bf16[32,2560]{1,0:T(8,128)(2,1)S(1)}, u32[]{:S(2)}, u32[]{:S(2)}) %collective-permute-start.12) | collective-permute-done | bytes 163872 | tf_op jit(solution)/shard_map/ppermute | solution.py:26
  76.0 0.9 shared_out.1
  76.9 0.5 collective-permute-start.18
  77.5 0.0 collective-permute-done.16
  77.6 0.6 collective-permute-start.17
  78.2 0.4 collective-permute-done.18
  78.6 1.2 %collective-permute-start.19 = (f32[32,896]{1,0:T(8,128)S(1)}, f32[32,896]{1,0:T(8,128)S(1)}, u32[]{:S(2)}, u32[]{:S(2)}) collective-permute-start(f32[32,896]{1,0:T(8,128)S(1)} %slice.93), channel_id=1, source_target_pairs={{0,2},{1,3},{2,0},{3,1},{4,6},{5,7},{6,4},{7,5},{8,10},{9,11},{10,... | collective-permute-start | bytes 344072 | tf_op jit(solution)/shard_map/ppermute | solution.py:31
  79.8 3.8 %collective-permute-done.17 = bf16[32,1792]{1,0:T(8,128)(2,1)S(1)} collective-permute-done((bf16[32,1792]{1,0:T(8,128)(2,1)S(1)}, bf16[32,1792]{1,0:T(8,128)(2,1)S(1)}, u32[]{:S(2)}, u32[]{:S(2)}) %collective-permute-start.17) | collective-permute-done | bytes 114720 | tf_op jit(solution)/shard_map/ppermute | solution.py:31
  83.6 1.6 %collective-permute-done.19 = f32[32,896]{1,0:T(8,128)S(1)} collective-permute-done((f32[32,896]{1,0:T(8,128)S(1)}, f32[32,896]{1,0:T(8,128)S(1)}, u32[]{:S(2)}, u32[]{:S(2)}) %collective-permute-start.19) | collective-permute-done | bytes 114720 | tf_op jit(solution)/shard_map/ppermute | solution.py:31
  85.3 3.8 %collective-permute-start.20 = (bf16[8,4480]{1,0:T(8,128)(2,1)S(1)}, bf16[8,4480]{1,0:T(8,128)(2,1)S(1)}, u32[]{:S(2)}, u32[]{:S(2)}) collective-permute-start(bf16[8,4480]{1,0:T(8,128)(2,1)S(1)} %get-tuple-element.75), channel_id=1, source_target_pairs={{0,12},{4,0},{8,4},{12,8},{1,13},{5,1},{9,5},{13,9},{2,14},{6,2},{... | collective-permute-start | bytes 215048 | tf_op jit(solution)/shard_map/ppermute | solution.py:26
  89.2 1.4 %collective-permute-start.21 = (bf16[8,4480]{1,0:T(8,128)(2,1)S(1)}, bf16[8,4480]{1,0:T(8,128)(2,1)S(1)}, u32[]{:S(2)}, u32[]{:S(2)}) collective-permute-start(bf16[8,4480]{1,0:T(8,128)(2,1)S(1)} %get-tuple-element.76), channel_id=1, source_target_pairs={{0,8},{4,12},{8,0},{12,4},{1,9},{5,13},{9,1},{13,5},{2,10},{6,14},... | collective-permute-start | bytes 215048 | tf_op jit(solution)/shard_map/ppermute | solution.py:26
  90.5 1.2 %collective-permute-done.20 = bf16[8,4480]{1,0:T(8,128)(2,1)S(1)} collective-permute-done((bf16[8,4480]{1,0:T(8,128)(2,1)S(1)}, bf16[8,4480]{1,0:T(8,128)(2,1)S(1)}, u32[]{:S(2)}, u32[]{:S(2)}) %collective-permute-start.20) | collective-permute-done | bytes 71712 | tf_op jit(solution)/shard_map/ppermute | solution.py:26
  91.7 5.2 %collective-permute-done.21 = bf16[8,4480]{1,0:T(8,128)(2,1)S(1)} collective-permute-done((bf16[8,4480]{1,0:T(8,128)(2,1)S(1)}, bf16[8,4480]{1,0:T(8,128)(2,1)S(1)}, u32[]{:S(2)}, u32[]{:S(2)}) %collective-permute-start.21) | collective-permute-done | bytes 71712 | tf_op jit(solution)/shard_map/ppermute | solution.py:26
  97.1 0.6 convert_element_type.56
  (47 shorter events, 0.5 us)
Async XLA Ops:
  1.6 7.6 %collective-permute-start = (bf16[8,3712]{1,0:T(8,128)(2,1)}, bf16[8,3712]{1,0:T(8,128)(2,1)S(1)}, u32[]{:S(2)}, u32[]{:S(2)}) collective-permute-start(bf16[8,3712]{1,0:T(8,128)(2,1)} %prepare.1), channel_id=1, source_target_pairs={{0,4},{4,8},{8,12},{12,0},{1,5},{5,9},{9,13},{13,1},{2,6},{6,10},{... | collective-permute-start | bytes 178184 | tf_op jit(solution)/shard_map/ppermute | solution.py:26
  4.6 7.0 %collective-permute-start.1 = (bf16[8,3712]{1,0:T(8,128)(2,1)}, bf16[8,3712]{1,0:T(8,128)(2,1)S(1)}, u32[]{:S(2)}, u32[]{:S(2)}) collective-permute-start(bf16[8,3712]{1,0:T(8,128)(2,1)} %prepare.1), channel_id=1, source_target_pairs={{0,8},{4,12},{8,0},{12,4},{1,9},{5,13},{9,1},{13,5},{2,10},{6,14},... | collective-permute-start | bytes 178184 | tf_op jit(solution)/shard_map/ppermute | solution.py:26
  7.2 4.7 %collective-permute-start.2 = (bf16[8,3712]{1,0:T(8,128)(2,1)}, bf16[8,3712]{1,0:T(8,128)(2,1)S(1)}, u32[]{:S(2)}, u32[]{:S(2)}) collective-permute-start(bf16[8,3712]{1,0:T(8,128)(2,1)} %prepare.1), channel_id=1, source_target_pairs={{0,12},{4,0},{8,4},{12,8},{1,13},{5,1},{9,5},{13,9},{2,14},{6,2},{... | collective-permute-start | bytes 178184 | tf_op jit(solution)/shard_map/ppermute | solution.py:26
  12.8 7.2 %copy-start.1 = (bf16[32,896]{1,0:T(8,128)(2,1)}, bf16[32,896]{1,0:T(8,128)(2,1)S(1)}, u32[]{:S(2)}) copy-start(bf16[32,896]{1,0:T(8,128)(2,1)S(1)} %constant_dynamic-slice_fusion.refs_0_) | copy-start | bytes 172036
  12.8 15.1 %copy-start.5 = (f32[3584]{0:T(1024)S(1)}, f32[3584]{0:T(1024)}, u32[]{:S(2)}) copy-start(f32[3584]{0:T(1024)} %param.19) | copy-start | bytes 43012
  12.8 4.2 %collective-permute-start.3 = (bf16[32,896]{1,0:T(8,128)(2,1)S(1)}, bf16[32,896]{1,0:T(8,128)(2,1)S(1)}, u32[]{:S(2)}, u32[]{:S(2)}) collective-permute-start(bf16[32,896]{1,0:T(8,128)(2,1)S(1)} %constant_dynamic-slice_fusion.refs_0_), channel_id=1, source_target_pairs={{0,2},{1,3},{2,0},{3,1},{4,6},{5,7},{6,4},{7,5},{8,10},{9,11},{10,... | collective-permute-start | bytes 172040 | tf_op jit(solution)/shard_map/ppermute | solution.py:31
  17.0 2.9 %copy-start.2 = (bf16[32,896]{1,0:T(8,128)(2,1)}, bf16[32,896]{1,0:T(8,128)(2,1)S(1)}, u32[]{:S(2)}) copy-start(bf16[32,896]{1,0:T(8,128)(2,1)S(1)} %collective-permute-done.3.refs_1_) | copy-start | bytes 172036
  17.0 10.5 %collective-permute-start.4 = (bf16[32,3712]{1,0:T(8,128)(2,1)S(1)}, bf16[32,3712]{1,0:T(8,128)(2,1)S(1)}, u32[]{:S(2)}, u32[]{:S(2)}) collective-permute-start(bf16[32,3712]{1,0:T(8,128)(2,1)S(1)} %pad_maximum_fusion.2), channel_id=1, source_target_pairs={{0,2},{1,3},{2,0},{3,1},{4,6},{5,7},{6,4},{7,5},{8,10},{9,11},{10,... | collective-permute-start | bytes 712712 | tf_op jit(solution)/shard_map/ppermute | solution.py:31
  18.5 1.2 %collective-permute-start.5 = (bf16[32,896]{1,0:T(8,128)(2,1)S(1)}, bf16[32,896]{1,0:T(8,128)(2,1)S(1)}, u32[]{:S(2)}, u32[]{:S(2)}) collective-permute-start(bf16[32,896]{1,0:T(8,128)(2,1)S(1)} %constant_dynamic-slice_fusion.refs_0_), channel_id=1, source_target_pairs={{0,1},{1,0},{2,3},{3,2},{4,5},{5,4},{6,7},{7,6},{8,9},{9,8},{10,11... | collective-permute-start | bytes 172040 | tf_op jit(solution)/shard_map/ppermute | solution.py:36
  18.5 1.4 %collective-permute-start.6 = (bf16[32,896]{1,0:T(8,128)(2,1)S(1)}, bf16[32,896]{1,0:T(8,128)(2,1)S(1)}, u32[]{:S(2)}, u32[]{:S(2)}) collective-permute-start(bf16[32,896]{1,0:T(8,128)(2,1)S(1)} %collective-permute-done.3.refs_1_), channel_id=1, source_target_pairs={{0,1},{1,0},{2,3},{3,2},{4,5},{5,4},{6,7},{7,6},{8,9},{9,8},{10,11... | collective-permute-start | bytes 172040 | tf_op jit(solution)/shard_map/ppermute | solution.py:36
  19.7 0.6 copy-start.3
  20.4 0.6 copy-start.4
  27.6 4.1 %collective-permute-start.7 = (bf16[64,3712]{1,0:T(8,128)(2,1)S(1)}, bf16[64,3712]{1,0:T(8,128)(2,1)S(1)}, u32[]{:S(2)}, u32[]{:S(2)}) collective-permute-start(bf16[64,3712]{1,0:T(8,128)(2,1)S(1)} %pad_maximum_fusion.1), channel_id=1, source_target_pairs={{0,1},{1,0},{2,3},{3,2},{4,5},{5,4},{6,7},{7,6},{8,9},{9,8},{10,11... | collective-permute-start | bytes 1425416 | tf_op jit(solution)/shard_map/ppermute | solution.py:36
  27.8 30.6 %collective-permute-start.10 = (bf16[2,32,2560]{2,1,0:T(8,128)(2,1)}, bf16[2,32,2560]{2,1,0:T(8,128)(2,1)S(1)}, u32[]{:S(2)}, u32[]{:S(2)}) collective-permute-start(bf16[2,32,2560]{2,1,0:T(8,128)(2,1)} %get-tuple-element.53), channel_id=1, source_target_pairs={{0,4},{4,8},{8,12},{12,0},{1,5},{5,9},{9,13},{13,1},{2,6},{6,10},{... | collective-permute-start | bytes 983048 | tf_op jit(solution)/shard_map/ppermute | solution.py:26
  29.2 29.2 %collective-permute-start.8 = (bf16[2,32,2560]{2,1,0:T(8,128)(2,1)}, bf16[2,32,2560]{2,1,0:T(8,128)(2,1)S(1)}, u32[]{:S(2)}, u32[]{:S(2)}) collective-permute-start(bf16[2,32,2560]{2,1,0:T(8,128)(2,1)} %get-tuple-element.51), channel_id=1, source_target_pairs={{0,12},{4,0},{8,4},{12,8},{1,13},{5,1},{9,5},{13,9},{2,14},{6,2},{... | collective-permute-start | bytes 983048 | tf_op jit(solution)/shard_map/ppermute | solution.py:26
  31.7 28.9 %collective-permute-start.9 = (bf16[2,32,2560]{2,1,0:T(8,128)(2,1)}, bf16[2,32,2560]{2,1,0:T(8,128)(2,1)S(1)}, u32[]{:S(2)}, u32[]{:S(2)}) collective-permute-start(bf16[2,32,2560]{2,1,0:T(8,128)(2,1)} %get-tuple-element.52), channel_id=1, source_target_pairs={{0,8},{4,12},{8,0},{12,4},{1,9},{5,13},{9,1},{13,5},{2,10},{6,14},... | collective-permute-start | bytes 983048 | tf_op jit(solution)/shard_map/ppermute | solution.py:26
  51.9 8.8 %copy-start = (bf16[2,32,2560]{2,1,0:T(8,128)(2,1)S(1)}, bf16[2,32,2560]{2,1,0:T(8,128)(2,1)}, u32[]{:S(2)}) copy-start(bf16[2,32,2560]{2,1,0:T(8,128)(2,1)} %get-tuple-element.50) | copy-start | bytes 983044
  60.7 4.2 %collective-permute-start.14 = (bf16[64,1792]{1,0:T(8,128)(2,1)S(1)}, bf16[64,1792]{1,0:T(8,128)(2,1)S(1)}, u32[]{:S(2)}, u32[]{:S(2)}) collective-permute-start(bf16[64,1792]{1,0:T(8,128)(2,1)S(1)} %get-tuple-element.64), channel_id=1, source_target_pairs={{0,1},{1,0},{2,3},{3,2},{4,5},{5,4},{6,7},{7,6},{8,9},{9,8},{10,11... | collective-permute-start | bytes 688136 | tf_op jit(solution)/shard_map/ppermute | solution.py:36
  60.9 11.4 %collective-permute-start.11 = (bf16[32,2560]{1,0:T(8,128)(2,1)S(1)}, bf16[32,2560]{1,0:T(8,128)(2,1)S(1)}, u32[]{:S(2)}, u32[]{:S(2)}) collective-permute-start(bf16[32,2560]{1,0:T(8,128)(2,1)S(1)} %fusion.1.refs_0_), channel_id=1, source_target_pairs={{0,4},{4,8},{8,12},{12,0},{1,5},{5,9},{9,13},{13,1},{2,6},{6,10},{... | collective-permute-start | bytes 491528 | tf_op jit(solution)/shard_map/ppermute | solution.py:26
  61.0 15.0 %collective-permute-start.12 = (bf16[32,2560]{1,0:T(8,128)(2,1)S(1)}, bf16[32,2560]{1,0:T(8,128)(2,1)S(1)}, u32[]{:S(2)}, u32[]{:S(2)}) collective-permute-start(bf16[32,2560]{1,0:T(8,128)(2,1)S(1)} %fusion.1.refs_0_), channel_id=1, source_target_pairs={{0,8},{4,12},{8,0},{12,4},{1,9},{5,13},{9,1},{13,5},{2,10},{6,14},... | collective-permute-start | bytes 491528 | tf_op jit(solution)/shard_map/ppermute | solution.py:26
  62.0 14.0 %collective-permute-start.13 = (bf16[32,2560]{1,0:T(8,128)(2,1)S(1)}, bf16[32,2560]{1,0:T(8,128)(2,1)S(1)}, u32[]{:S(2)}, u32[]{:S(2)}) collective-permute-start(bf16[32,2560]{1,0:T(8,128)(2,1)S(1)} %fusion.1.refs_0_), channel_id=1, source_target_pairs={{0,12},{4,0},{8,4},{12,8},{1,13},{5,1},{9,5},{13,9},{2,14},{6,2},{... | collective-permute-start | bytes 491528 | tf_op jit(solution)/shard_map/ppermute | solution.py:26
  64.8 11.2 %slice-start = ((s8[4587520]{0:T(1024)(128)(4,1)}), s8[4194304]{0:T(1024)(128)(4,1)S(1)}, s32[]{:S(2)}) async-start(s8[4587520]{0:T(1024)(128)(4,1)} %bitcast.11), calls=%async_computation | async-start | bytes 8388608
  64.9 11.1 %slice-start.1 = ((s8[4587520]{0:T(1024)(128)(4,1)}), s8[393216]{0:T(1024)(128)(4,1)S(1)}, s32[]{:S(2)}) async-start(s8[4587520]{0:T(1024)(128)(4,1)} %bitcast.11), calls=%async_computation.1 | async-start | bytes 786432
  64.9 7.4 %collective-permute-start.15 = (bf16[32,1792]{1,0:T(8,128)(2,1)S(1)}, bf16[32,1792]{1,0:T(8,128)(2,1)S(1)}, u32[]{:S(2)}, u32[]{:S(2)}) collective-permute-start(bf16[32,1792]{1,0:T(8,128)(2,1)S(1)} %slice.134), channel_id=1, source_target_pairs={{0,2},{1,3},{2,0},{3,1},{4,6},{5,7},{6,4},{7,5},{8,10},{9,11},{10,... | collective-permute-start | bytes 344072 | tf_op jit(solution)/shard_map/ppermute | solution.py:31
  76.0 1.5 %collective-permute-start.16 = (bf16[64,1792]{1,0:T(8,128)(2,1)S(1)}, bf16[64,1792]{1,0:T(8,128)(2,1)S(1)}, u32[]{:S(2)}, u32[]{:S(2)}) collective-permute-start(bf16[64,1792]{1,0:T(8,128)(2,1)S(1)} %get-tuple-element.67), channel_id=1, source_target_pairs={{0,1},{1,0},{2,3},{3,2},{4,5},{5,4},{6,7},{7,6},{8,9},{9,8},{10,11... | collective-permute-start | bytes 688136 | tf_op jit(solution)/shard_map/ppermute | solution.py:36
  76.9 1.7 %collective-permute-start.18 = (f32[64,896]{1,0:T(8,128)S(1)}, f32[64,896]{1,0:T(8,128)S(1)}, u32[]{:S(2)}, u32[]{:S(2)}) collective-permute-start(f32[64,896]{1,0:T(8,128)S(1)} %get-tuple-element.74), channel_id=1, source_target_pairs={{0,1},{1,0},{2,3},{3,2},{4,5},{5,4},{6,7},{7,6},{8,9},{9,8},{10,11... | collective-permute-start | bytes 688136 | tf_op jit(solution)/shard_map/ppermute | solution.py:36
  77.6 6.1 %collective-permute-start.17 = (bf16[32,1792]{1,0:T(8,128)(2,1)S(1)}, bf16[32,1792]{1,0:T(8,128)(2,1)S(1)}, u32[]{:S(2)}, u32[]{:S(2)}) collective-permute-start(bf16[32,1792]{1,0:T(8,128)(2,1)S(1)} %slice.133), channel_id=1, source_target_pairs={{0,2},{1,3},{2,0},{3,1},{4,6},{5,7},{6,4},{7,5},{8,10},{9,11},{10,... | collective-permute-start | bytes 344072 | tf_op jit(solution)/shard_map/ppermute | solution.py:31
  78.6 6.7 %collective-permute-start.19 = (f32[32,896]{1,0:T(8,128)S(1)}, f32[32,896]{1,0:T(8,128)S(1)}, u32[]{:S(2)}, u32[]{:S(2)}) collective-permute-start(f32[32,896]{1,0:T(8,128)S(1)} %slice.93), channel_id=1, source_target_pairs={{0,2},{1,3},{2,0},{3,1},{4,6},{5,7},{6,4},{7,5},{8,10},{9,11},{10,... | collective-permute-start | bytes 344072 | tf_op jit(solution)/shard_map/ppermute | solution.py:31
  85.3 6.4 %collective-permute-start.20 = (bf16[8,4480]{1,0:T(8,128)(2,1)S(1)}, bf16[8,4480]{1,0:T(8,128)(2,1)S(1)}, u32[]{:S(2)}, u32[]{:S(2)}) collective-permute-start(bf16[8,4480]{1,0:T(8,128)(2,1)S(1)} %get-tuple-element.75), channel_id=1, source_target_pairs={{0,12},{4,0},{8,4},{12,8},{1,13},{5,1},{9,5},{13,9},{2,14},{6,2},{... | collective-permute-start | bytes 215048 | tf_op jit(solution)/shard_map/ppermute | solution.py:26
  89.2 7.8 %collective-permute-start.21 = (bf16[8,4480]{1,0:T(8,128)(2,1)S(1)}, bf16[8,4480]{1,0:T(8,128)(2,1)S(1)}, u32[]{:S(2)}, u32[]{:S(2)}) collective-permute-start(bf16[8,4480]{1,0:T(8,128)(2,1)S(1)} %get-tuple-element.76), channel_id=1, source_target_pairs={{0,8},{4,12},{8,0},{12,4},{1,9},{5,13},{9,1},{13,5},{2,10},{6,14},... | collective-permute-start | bytes 215048 | tf_op jit(solution)/shard_map/ppermute | solution.py:26
  90.5 6.4 %collective-permute-start.22 = (bf16[8,4480]{1,0:T(8,128)(2,1)S(1)}, bf16[8,4480]{1,0:T(8,128)(2,1)S(1)}, u32[]{:S(2)}, u32[]{:S(2)}) collective-permute-start(bf16[8,4480]{1,0:T(8,128)(2,1)S(1)} %get-tuple-element.77), channel_id=1, source_target_pairs={{0,4},{4,8},{8,12},{12,0},{1,5},{5,9},{9,13},{13,1},{2,6},{6,10},{... | collective-permute-start | bytes 215048 | tf_op jit(solution)/shard_map/ppermute | solution.py:26

commit v3 on v2

v3 whole, which is shorter than its diff:
```python
import functools
import math

import jax
import jax.numpy as jnp
from jax import lax
from jax.experimental import pallas as pl
from jax.experimental.pallas import tpu as pltpu
from jax.sharding import PartitionSpec as P

EXPERTS = 32
LANES = 128
VMEM_LIMIT = 48 * 2**20
VMEM_SMALL = 8 * 2**20


def chunk_of(width, most):
    best = width
    for size in range(LANES, most + 1, LANES):
        if width % size == 0:
            best = size
    return best


def z_shift(value, step):
    spread = lax.axis_size("expert")
    return lax.ppermute(value, "expert", [(i, (i + step) % spread) for i in range(spread)])


def x_shift(value, step):
    size = lax.axis_size("narrow")
    return lax.ppermute(value, "narrow", [(i, (i + 2 * step) % size) for i in range(size)])


def core_swap(value):
    size = lax.axis_size("narrow")
    return lax.ppermute(value, "narrow", [(i, i ^ 1) for i in range(size)])


def gather_column(pieces):
    return [pieces[0]] + [z_shift(piece, d) for d, piece in enumerate(pieces) if d > 0]


def gather_plane(column):
    chips = lax.axis_size("narrow") // 2
    return [column] + [x_shift(column, d) for d in range(1, chips)]


def both_cores(plane):
    return jnp.concatenate([plane, core_swap(plane)], axis=0)


def join(*lists):
    values = iter(lax.optimization_barrier([value for part in lists for value in part]))
    return [[next(values) for _ in part] for part in lists]


def load_kernel(*refs):
    count = len(refs) // 2
    sources, targets, sems = refs[:count], refs[count:-1], refs[-1]
    copies = [
        pltpu.make_async_copy(source.at[pl.ds(0, target.shape[0])], target, sems.at[i])
        for i, (source, target) in enumerate(zip(sources, targets))
    ]
    for copy in copies:
        copy.start()
    for copy in copies:
        copy.wait()


def load(arrays, taken):
    shapes = [(taken, *value.shape[1:]) for value in arrays]
    return pl.pallas_call(
        load_kernel,
        in_specs=[pl.BlockSpec(memory_space=pl.ANY)] * len(arrays),
        out_shape=[
            jax.ShapeDtypeStruct(shape, value.dtype) for shape, value in zip(shapes, arrays)
        ],
        scratch_shapes=[pltpu.SemaphoreType.DMA((len(arrays),))],
        compiler_params=pltpu.CompilerParams(vmem_limit_bytes=VMEM_SMALL),
        cost_estimate=pl.CostEstimate(
            flops=0,
            bytes_accessed=sum(2 * math.prod(shape) for shape in shapes),
            transcendentals=0,
        ),
        name="load",
    )(*arrays)


def shared_in_kernel(sizes, width, gate_ref, up_ref, *refs):
    outer, spread, rows = sizes
    x_refs, out_refs = refs[:outer], refs[outer : outer + spread]
    x_buf, sems = refs[outer + spread :]
    copies = [
        pltpu.make_async_copy(ref, x_buf.at[i], sems.at[i]) for i, ref in enumerate(x_refs)
    ]
    for copy in copies:
        copy.start()
    for copy in copies:
        copy.wait()
    x = x_buf[...].reshape(outer * spread * rows, x_buf.shape[2])
    for half, ref in enumerate((gate_ref, up_ref)):
        for j in range(ref.shape[1] // width):
            columns = pl.ds(j * width, width)
            sums = jnp.dot(x, ref[:, columns], preferred_element_type=jnp.float32)
            sums = sums.reshape(outer, spread, rows, width)
            for d in range(spread):
                block = sums[:, d].reshape(outer * rows, width)
                out_refs[d][half, :, columns] = block.astype(jnp.bfloat16)


def shared_in(pieces, gate, up, rows):
    depth, hidden = gate.shape
    outer, spread = len(pieces), lax.axis_size("expert")
    count = outer * spread * rows
    whole = pl.BlockSpec(memory_space=pltpu.VMEM)
    apart = pl.BlockSpec(memory_space=pl.ANY)
    return pl.pallas_call(
        functools.partial(shared_in_kernel, (outer, spread, rows), chunk_of(hidden, 512)),
        in_specs=[whole, whole] + [apart] * outer,
        out_shape=[jax.ShapeDtypeStruct((2, outer * rows, hidden), jnp.bfloat16)] * spread,
        scratch_shapes=[
            pltpu.VMEM((outer, spread * rows, depth), gate.dtype),
            pltpu.SemaphoreType.DMA((outer,)),
        ],
        compiler_params=pltpu.CompilerParams(vmem_limit_bytes=VMEM_SMALL),
        cost_estimate=pl.CostEstimate(
            flops=4 * count * depth * hidden,
            bytes_accessed=4 * count * hidden,
            transcendentals=0,
        ),
        name="shared_in",
    )(gate, up, *pieces)


def experts_kernel(chosen, first_ref, x_ref, scale_ref, gate_ref, up_ref, down_ref, *refs):
    branch_ref, keep_ref, send_ref = refs[:3]
    act_buf, gate_buf, up_buf, down_buf, sems, down_sems = refs[3:]
    local, feat, hidden = gate_ref.shape
    slots, (down_slots, _, _, width) = gate_buf.shape[0], down_buf.shape
    blocks = feat // width

    def copies(i):
        slot = i % slots
        return [
            pltpu.make_async_copy(ref.at[i], buf.at[slot], sems.at[half, slot])
            for half, (ref, buf) in enumerate(((gate_ref, gate_buf), (up_ref, up_buf)))
        ]

    def down_copy(j):
        slot = j % down_slots
        return pltpu.make_async_copy(
            down_ref.at[:, :, pl.ds(j * width, width)], down_buf.at[slot], down_sems.at[slot]
        )

    for i in range(slots):
        for copy in copies(i):
            copy.start()
    inner = jnp.sum(x_ref[:, :feat].astype(jnp.float32) * scale_ref[...], axis=1, keepdims=True)
    branch_ref[...] = jnp.broadcast_to(1.0 / (1.0 + jnp.exp(-inner)), branch_ref.shape)
    route = x_ref[:, feat:].astype(jnp.float32)
    named, weights = route[:, :chosen], route[:, chosen : 2 * chosen]
    x = x_ref[:, :feat]
    for i in range(local):
        slot = i % slots
        gate_copy, up_copy = copies(i)
        gate_copy.wait()
        gate = jnp.dot(x, gate_buf[slot], preferred_element_type=jnp.float32)
        up_copy.wait()
        up = jnp.dot(x, up_buf[slot], preferred_element_type=jnp.float32)
        if i + slots < local:
            for copy in copies(i + slots):
                copy.start()
        if i == max(local - slots, 0):
            for j in range(down_slots):
                down_copy(j).start()
        expert = (first_ref[0] + i).astype(jnp.float32)
        weight = jnp.sum(jnp.where(named == expert, weights, 0.0), axis=1, keepdims=True)
        value = gate / (1.0 + jnp.exp(-gate)) * up * weight
        act_buf[:, i * hidden : (i + 1) * hidden] = jnp.where(
            weight == 0.0, 0.0, value
        ).astype(jnp.bfloat16)
    half = act_buf.shape[0] // 2
    for j in range(blocks):
        down_copy(j).wait()
        sums = jnp.dot(
            act_buf[...],
            down_buf[j % down_slots].reshape(local * hidden, width),
            preferred_element_type=jnp.float32,
        )
        if j + down_slots < blocks:
            down_copy(j + down_slots).start()
        at = pl.ds(j * width, width)
        keep_ref[:, at] = sums[:half]
        send_ref[:, at] = sums[half:].astype(jnp.bfloat16)


def experts(x, scale, gate, up, down, first, chosen):
    count = x.shape[0]
    local, feat, hidden = gate.shape
    whole = pl.BlockSpec(memory_space=pltpu.VMEM)
    apart = pl.BlockSpec(memory_space=pl.ANY)
    slots = min(3, local)
    width = chunk_of(feat, 256)
    down_slots = (feat // width + 1) // 2
    buffer = pltpu.VMEM((slots, feat, hidden), gate.dtype)
    return pl.pallas_call(
        functools.partial(experts_kernel, chosen),
        in_specs=[pl.BlockSpec(memory_space=pltpu.SMEM), whole, whole, apart, apart, apart],
        out_shape=[
            jax.ShapeDtypeStruct((count, LANES), jnp.float32),
            jax.ShapeDtypeStruct((count // 2, feat), jnp.float32),
            jax.ShapeDtypeStruct((count // 2, feat), jnp.bfloat16),
        ],
        scratch_shapes=[
            pltpu.VMEM((count, local * hidden), jnp.bfloat16),
            buffer,
            buffer,
            pltpu.VMEM((down_slots, local, hidden, width), down.dtype),
            pltpu.SemaphoreType.DMA((2, slots)),
            pltpu.SemaphoreType.DMA((down_slots,)),
        ],
        compiler_params=pltpu.CompilerParams(vmem_limit_bytes=VMEM_LIMIT),
        cost_estimate=pl.CostEstimate(
            flops=6 * count * local * feat * hidden,
            bytes_accessed=6 * local * feat * hidden,
            transcendentals=count * local * hidden,
        ),
        name="experts",
    )(first, x, scale.reshape(1, feat), gate, up, down)


def shared_out_kernel(sizes, branch_ref, down_ref, *refs):
    outer, spread, rows = sizes
    act_refs, (keep_ref, send_ref) = refs[:spread], refs[spread:]
    act = jnp.concatenate([ref[...] for ref in act_refs], axis=0)
    sums = jnp.dot(act, down_ref[...], preferred_element_type=jnp.float32)
    width = sums.shape[1]
    sums = jnp.swapaxes(sums.reshape(spread, outer, rows, width), 0, 1)
    sums = sums.reshape(outer * spread * rows, width) * branch_ref[:, :1]
    half = sums.shape[0] // 2
    keep_ref[...] = sums[:half]
    send_ref[...] = sums[half:].astype(jnp.bfloat16)


def shared_out(branch, down, acts, rows):
    count, spread = branch.shape[0], len(acts)
    outer = count // (spread * rows)
    shape = (count // 2, down.shape[1])
    return pl.pallas_call(
        functools.partial(shared_out_kernel, (outer, spread, rows)),
        out_shape=[
            jax.ShapeDtypeStruct(shape, jnp.float32),
            jax.ShapeDtypeStruct(shape, jnp.bfloat16),
        ],
        compiler_params=pltpu.CompilerParams(vmem_limit_bytes=VMEM_LIMIT),
        cost_estimate=pl.CostEstimate(
            flops=2 * count * down.shape[0] * down.shape[1],
            bytes_accessed=2 * down.shape[0] * down.shape[1],
            transcendentals=0,
        ),
        name="shared_out",
    )(branch, down, *acts)


def narrow_sum(keep, send):
    return chip_sum(keep + core_swap(send).astype(jnp.float32))


def chip_sum(total):
    chips = lax.axis_size("narrow") // 2
    part = total.shape[0] // chips
    result = total[:part]
    for d in range(1, chips):
        piece = total[d * part : (d + 1) * part].astype(jnp.bfloat16)
        result = result + x_shift(piece, -d).astype(jnp.float32)
    return result


def body(
    tokens,
    expert_ids,
    route_weights,
    expert_gate,
    expert_up,
    expert_down,
    shared_gate,
    shared_up,
    shared_down,
    shared_scale,
):
    rows, feat = tokens.shape
    spread = lax.axis_size("expert")
    here = lax.axis_index("expert")
    local = expert_gate.shape[0]
    depth = shared_gate.shape[0]
    chosen = expert_ids.shape[1]
    own = jnp.concatenate(
        [
            tokens,
            expert_ids.astype(jnp.bfloat16),
            route_weights,
            jnp.zeros((rows, LANES - 2 * chosen), jnp.bfloat16),
        ],
        axis=1,
    )
    column = jnp.concatenate(gather_column([own] * spread), axis=0)
    part = lax.dynamic_slice_in_dim(column, here * depth, depth, axis=1)
    parts, (column,), up = join(gather_plane(part), [column], load([shared_up], shared_up.shape[0]))
    parts = parts + [core_swap(piece) for piece in parts]
    hidden_own, *hidden_parts = shared_in(parts, shared_gate, *up, rows)
    plane, (hidden_own,) = join(gather_plane(column), [hidden_own])
    x = both_cores(jnp.concatenate(plane, axis=0))

    first = (here * local).astype(jnp.int32).reshape(1)
    branch, keep, send = experts(
        x, shared_scale, expert_gate, expert_up, expert_down, first, chosen
    )
    arrived = [z_shift(piece, -d) for d, piece in enumerate(hidden_parts, 1)]
    arrived, (keep, send) = join(arrived, [keep, send])
    hidden = hidden_own.astype(jnp.float32)
    for piece in arrived:
        hidden = hidden + piece.astype(jnp.float32)
    shared_act = (jax.nn.silu(hidden[0]) * hidden[1]).astype(jnp.bfloat16)
    acts = gather_column([shared_act] * spread)
    routed = keep + core_swap(send).astype(jnp.float32)
    middle = feat // LANES // 2 * LANES
    routed = [chip_sum(routed[:, :middle]), chip_sum(routed[:, middle:])]
    down = join([shared_down, shared_act])[0][:1]
    acts, down = join(acts, load(down, shared_down.shape[0]))
    part = shared_out(branch, *down, acts, rows)
    part, routed = join(part, routed)
    both = jnp.concatenate([*routed, narrow_sum(*part)], axis=1)
    pieces = [both[:rows]] + [
        z_shift(both[d * rows : (d + 1) * rows].astype(jnp.bfloat16), -d).astype(jnp.float32)
        for d in range(1, spread)
    ]
    total = pieces[0][:, :feat]
    for piece in pieces[1:]:
        total = total + piece[:, :feat]
    width = shared_down.shape[1]
    for d, piece in enumerate(pieces):
        at = lax.rem(here + d, spread) * width
        old = lax.dynamic_slice_in_dim(total, at, width, axis=1)
        total = lax.dynamic_update_slice_in_dim(total, old + piece[:, feat:], at, axis=1)
    return total.astype(jnp.bfloat16)


def solution(mesh):
    return jax.shard_map(
        body,
        mesh=mesh,
        in_specs=(
            P(("groups", "expert", "narrow"), None),
            P(("groups", "expert", "narrow"), None),
            P(("groups", "expert", "narrow"), None),
            P("expert", None, "narrow"),
            P("expert", None, "narrow"),
            P("expert", "narrow", None),
            P("expert", "narrow"),
            P("expert", "narrow"),
            P("narrow", "expert"),
            P(),
        ),
        out_specs=P(("groups", "expert", "narrow"), None),
        check_vma=False,
    )
```

time: 98 us -> 90.7 us (0.926)
  Pallas kernels: 42.3 us -> 32.4 us
  starting transfers between devices: 26.6 us -> 29.5 us
  waiting for transfers between devices: 25.2 us -> 22.9 us
  local copies, waits for them, and re-layouts: 1.19 us -> 3.29 us
    pallas_call x4 -> x3, Pallas kernels: 34.9 us -> 29.7 us  [the longest x1 28.8 us: experts(): pl.pallas_call(functools.partial(experts_kernel, chosen), in_specs=[pl.Bl...]
    pallas_call x1, Pallas kernels: 6.54 us -> 1.85 us  [shared_in(): pl.pallas_call(functools.partial(shared_in_kernel, (outer, spread, rows),...]
    ppermute x5, waiting for transfers between devices: 8.19 us -> 4.63 us  [x_shift(): lax.ppermute(value, 'narrow', [(i, (i + 2 * step) % size) for i in range(...]
    ppermute x12, starting transfers between devices: 19.9 us -> 22.6 us  [z_shift(): lax.ppermute(value, 'expert', [(i, (i + step) % spread) for i in range(sp...]
    unnamed x16 -> x10, local copies, waits for them, and re-layouts: 1.13 us -> 2.32 us
    ppermute x6 -> x5, waiting for transfers between devices: 1.33 us -> 2.21 us  [core_swap(): return lax.ppermute(value, 'narrow', [(i, i ^ 1) for i in range(size)])]
  transfers between devices with their start and end apart: 23 -> 22, of which waited for: 13 -> 14; matrix products, arithmetic and copies ran while one was open for 1% -> 1% of each run, Pallas kernels for 42% -> 36%
where the time goes in v3:
time: 90.7 us; the launch traced here: 90.4 us
  Pallas kernels  32.4 us (36%)
  starting transfers between devices  29.5 us (33%)
  waiting for transfers between devices  22.9 us (25%)
  local copies, waits for them, and re-layouts  3.29 us (4%)
  other arithmetic  2.03 us (2%)
    pallas_call x1, Pallas kernels, experts(): pl.pallas_call(functools.partial(experts_kernel, chosen), in_specs=[pl.Bl...  28.8 us
    ppermute x12, starting transfers between devices, z_shift(): lax.ppermute(value, 'expert', [(i, (i + step) % spread) for i in range(sp...  22.6 us
    ppermute x12, waiting for transfers between devices, z_shift(): lax.ppermute(value, 'expert', [(i, (i + step) % spread) for i in range(sp...  16.1 us
    ppermute x5, starting transfers between devices, x_shift(): lax.ppermute(value, 'narrow', [(i, (i + 2 * step) % size) for i in range(...  6.18 us
    ppermute x5, waiting for transfers between devices, x_shift(): lax.ppermute(value, 'narrow', [(i, (i + 2 * step) % size) for i in range(...  4.63 us
    unnamed x10, local copies, waits for them, and re-layouts  2.32 us
    ppermute x5, waiting for transfers between devices, core_swap(): return lax.ppermute(value, 'narrow', [(i, i ^ 1) for i in range(size)])  2.21 us
    pallas_call x1, Pallas kernels, shared_in(): pl.pallas_call(functools.partial(shared_in_kernel, (outer, spread, rows),...  1.85 us
  transfers between devices with their start and end apart: 22, of which 14 were waited for; matrix products, arithmetic and copies ran while one was open for 1% of the time, Pallas kernels for 36%

profile of v3, /device:TPU:0, one launch (start us, length us, event | category | flops | bytes accessed | tf_op | source)
XLA Modules:
  0.0 90.4 jit_solution(17488212703798757299)
XLA Ops:
  0.0 0.7 convert_element_type.51
  0.7 0.9 %concatenate.19 = bf16[8,3712]{1,0:T(8,128)(2,1)S(1)} concatenate(bf16[8,3584]{1,0:T(8,128)(2,1)} %param.10, bf16[8,8]{1,0:T(8,128)(2,1)S(1)} %convert_element_type.51, bf16[8,8]{1,0:T(8,128)(2,1)} %param.12, bf16[8,112]{1,0:T(8,128)(2,1)S(1)} %broadcast_in_dim.3), dimensions={1} | concatenate | bytes 118784 | tf_op jit(solution)/shard_map/concatenate | solution.py:298
  1.6 3.0 %collective-permute-start = (bf16[8,3712]{1,0:T(8,128)(2,1)S(1)}, bf16[8,3712]{1,0:T(8,128)(2,1)S(1)}, u32[]{:S(2)}, u32[]{:S(2)}) collective-permute-start(bf16[8,3712]{1,0:T(8,128)(2,1)S(1)} %concatenate.19), channel_id=1, source_target_pairs={{0,4},{4,8},{8,12},{12,0},{1,5},{5,9},{9,13},{13,1},{2,6},{6,10},{... | collective-permute-start | bytes 178184 | tf_op jit(solution)/shard_map/ppermute | solution.py:27
  4.6 2.6 %collective-permute-start.1 = (bf16[8,3712]{1,0:T(8,128)(2,1)S(1)}, bf16[8,3712]{1,0:T(8,128)(2,1)S(1)}, u32[]{:S(2)}, u32[]{:S(2)}) collective-permute-start(bf16[8,3712]{1,0:T(8,128)(2,1)S(1)} %concatenate.19), channel_id=1, source_target_pairs={{0,8},{4,12},{8,0},{12,4},{1,9},{5,13},{9,1},{13,5},{2,10},{6,14},... | collective-permute-start | bytes 178184 | tf_op jit(solution)/shard_map/ppermute | solution.py:27
  7.2 1.3 %collective-permute-start.2 = (bf16[8,3712]{1,0:T(8,128)(2,1)S(1)}, bf16[8,3712]{1,0:T(8,128)(2,1)S(1)}, u32[]{:S(2)}, u32[]{:S(2)}) collective-permute-start(bf16[8,3712]{1,0:T(8,128)(2,1)S(1)} %concatenate.19), channel_id=1, source_target_pairs={{0,12},{4,0},{8,4},{12,8},{1,13},{5,1},{9,5},{13,9},{2,14},{6,2},{... | collective-permute-start | bytes 178184 | tf_op jit(solution)/shard_map/ppermute | solution.py:27
  8.6 0.5 collective-permute-done
  9.0 2.3 %collective-permute-done.1 = bf16[8,3712]{1,0:T(8,128)(2,1)S(1)} collective-permute-done((bf16[8,3712]{1,0:T(8,128)(2,1)S(1)}, bf16[8,3712]{1,0:T(8,128)(2,1)S(1)}, u32[]{:S(2)}, u32[]{:S(2)}) %collective-permute-start.1) | collective-permute-done | bytes 59424 | tf_op jit(solution)/shard_map/ppermute | solution.py:27
  11.4 0.4 collective-permute-done.2
  11.8 1.5 %collective-permute-start.3 = (bf16[32,896]{1,0:T(8,128)(2,1)S(1)}, bf16[32,896]{1,0:T(8,128)(2,1)S(1)}, u32[]{:S(2)}, u32[]{:S(2)}) collective-permute-start(bf16[32,896]{1,0:T(8,128)(2,1)S(1)} %constant_dynamic-slice_fusion.refs_0_), channel_id=1, source_target_pairs={{0,2},{1,3},{2,0},{3,1},{4,6},{5,7},{6,4},{7,5},{8,10},{9,11},{10,... | collective-permute-start | bytes 172040 | tf_op jit(solution)/shard_map/ppermute | solution.py:32
  13.3 2.3 %copy-done = bf16[896,2560]{1,0:T(8,128)(2,1)S(1)} copy-done((bf16[896,2560]{1,0:T(8,128)(2,1)S(1)}, bf16[896,2560]{1,0:T(8,128)(2,1)}, u32[]{:S(2)}) %copy-start) | copy-done | bytes 4587544
  15.6 0.5 load.2.up_ref
  16.1 1.4 %collective-permute-start.4 = (bf16[32,3712]{1,0:T(8,128)(2,1)S(1)}, bf16[32,3712]{1,0:T(8,128)(2,1)S(1)}, u32[]{:S(2)}, u32[]{:S(2)}) collective-permute-start(bf16[32,3712]{1,0:T(8,128)(2,1)S(1)} %pad_maximum_fusion.2), channel_id=1, source_target_pairs={{0,2},{1,3},{2,0},{3,1},{4,6},{5,7},{6,4},{7,5},{8,10},{9,11},{10,... | collective-permute-start | bytes 712712 | tf_op jit(solution)/shard_map/ppermute | solution.py:32
  17.5 0.5 collective-permute-start.6
  18.0 0.7 collective-permute-done.5.refs_2_
  18.7 0.2 collective-permute-done.6.refs_3_
  18.9 1.9 %shared_in.1 = (bf16[2,32,2560]{2,1,0:T(8,128)(2,1)S(1)}, bf16[2,32,2560]{2,1,0:T(8,128)(2,1)S(1)}, bf16[2,32,2560]{2,1,0:T(8,128)(2,1)S(1)}, bf16[2,32,2560]{2,1,0:T(8,128)(2,1)S(1)}) custom-call(bf16[896,2560]{1,0:T(8,128)(2,1)S(1)} %copy-done.1, bf16[896,2560]{1,0:T(8,128)(2,1)S(1)} %load.2.up_ref, ...), custom_call_target="tpu_custom_call" | custom-call | flops 1174405120 | bytes 1310720 | tf_op jit(solution)/shard_map/shared_in/pallas_call | solution.py:118
  20.8 1.6 %collective-permute-done.4 = bf16[32,3712]{1,0:T(8,128)(2,1)S(1)} collective-permute-done((bf16[32,3712]{1,0:T(8,128)(2,1)S(1)}, bf16[32,3712]{1,0:T(8,128)(2,1)S(1)}, u32[]{:S(2)}, u32[]{:S(2)}) %collective-permute-start.4) | collective-permute-done | bytes 237600 | tf_op jit(solution)/shard_map/ppermute | solution.py:32
  22.4 0.1 collective-permute-start.7
  22.5 2.2 %collective-permute-start.10 = (bf16[2,32,2560]{2,1,0:T(8,128)(2,1)S(1)}, bf16[2,32,2560]{2,1,0:T(8,128)(2,1)S(1)}, u32[]{:S(2)}, u32[]{:S(2)}) collective-permute-start(bf16[2,32,2560]{2,1,0:T(8,128)(2,1)S(1)} %get-tuple-element.47), channel_id=1, source_target_pairs={{0,4},{4,8},{8,12},{12,0},{1,5},{5,9},{9,13},{13,1},{2,6},{6,10},{... | collective-permute-start | bytes 983048 | tf_op jit(solution)/shard_map/ppermute | solution.py:27
  24.7 1.7 %collective-permute-start.8 = (bf16[2,32,2560]{2,1,0:T(8,128)(2,1)S(1)}, bf16[2,32,2560]{2,1,0:T(8,128)(2,1)S(1)}, u32[]{:S(2)}, u32[]{:S(2)}) collective-permute-start(bf16[2,32,2560]{2,1,0:T(8,128)(2,1)S(1)} %get-tuple-element.45), channel_id=1, source_target_pairs={{0,12},{4,0},{8,4},{12,8},{1,13},{5,1},{9,5},{13,9},{2,14},{6,2},{... | collective-permute-start | bytes 983048 | tf_op jit(solution)/shard_map/ppermute | solution.py:27
  26.4 0.0 collective-permute-start.9
  26.4 0.1 pad_maximum_fusion.x_ref
  26.5 28.8 %experts.1 = (f32[128,128]{1,0:T(8,128)S(1)}, f32[64,3584]{1,0:T(8,128)S(1)}, bf16[64,3584]{1,0:T(8,128)(2,1)S(1)}) custom-call(s32[1]{0:T(128)} %bitcast.first_ref, bf16[128,3712]{1,0:T(8,128)(2,1)S(1)} %pad_maximum_fusion.x_ref, f32[1,3584]{1,0:T(1,128)S(1)} %reshape.7.scale_ref, bf16[8,3584,512]{2,1,0:T(8,128)(2,1)} %gate_ref.3, ...), custom_call_target="tpu_custom_call" | custom-call | flops 11274289152 | bytes 88080384 | tf_op jit(solution)/shard_map/experts/pallas_call | solution.py:207
  55.3 0.2 collective-permute-done.9
  55.5 0.1 collective-permute-start.14
  55.6 0.2 convert_add_fusion.1
  55.7 0.1 fusion.1.refs_0_
  55.8 1.4 %collective-permute-start.11 = (bf16[32,2560]{1,0:T(8,128)(2,1)S(1)}, bf16[32,2560]{1,0:T(8,128)(2,1)S(1)}, u32[]{:S(2)}, u32[]{:S(2)}) collective-permute-start(bf16[32,2560]{1,0:T(8,128)(2,1)S(1)} %fusion.1.refs_0_), channel_id=1, source_target_pairs={{0,4},{4,8},{8,12},{12,0},{1,5},{5,9},{9,13},{13,1},{2,6},{6,10},{... | collective-permute-start | bytes 491528 | tf_op jit(solution)/shard_map/ppermute | solution.py:27
  57.3 1.7 %collective-permute-start.12 = (bf16[32,2560]{1,0:T(8,128)(2,1)S(1)}, bf16[32,2560]{1,0:T(8,128)(2,1)S(1)}, u32[]{:S(2)}, u32[]{:S(2)}) collective-permute-start(bf16[32,2560]{1,0:T(8,128)(2,1)S(1)} %fusion.1.refs_0_), channel_id=1, source_target_pairs={{0,8},{4,12},{8,0},{12,4},{1,9},{5,13},{9,1},{13,5},{2,10},{6,14},... | collective-permute-start | bytes 491528 | tf_op jit(solution)/shard_map/ppermute | solution.py:27
  59.0 2.6 %collective-permute-start.13 = (bf16[32,2560]{1,0:T(8,128)(2,1)S(1)}, bf16[32,2560]{1,0:T(8,128)(2,1)S(1)}, u32[]{:S(2)}, u32[]{:S(2)}) collective-permute-start(bf16[32,2560]{1,0:T(8,128)(2,1)S(1)} %fusion.1.refs_0_), channel_id=1, source_target_pairs={{0,12},{4,0},{8,4},{12,8},{1,13},{5,1},{9,5},{13,9},{2,14},{6,2},{... | collective-permute-start | bytes 491528 | tf_op jit(solution)/shard_map/ppermute | solution.py:27
  61.5 0.1 fusion.7
  61.7 1.3 %collective-permute-start.15 = (bf16[32,1792]{1,0:T(8,128)(2,1)S(1)}, bf16[32,1792]{1,0:T(8,128)(2,1)S(1)}, u32[]{:S(2)}, u32[]{:S(2)}) collective-permute-start(bf16[32,1792]{1,0:T(8,128)(2,1)S(1)} %get-tuple-element.75), channel_id=1, source_target_pairs={{0,2},{1,3},{2,0},{3,1},{4,6},{5,7},{6,4},{7,5},{8,10},{9,11},{10,... | collective-permute-start | bytes 344072 | tf_op jit(solution)/shard_map/ppermute | solution.py:32
  63.0 0.8 collective-permute-start.16
  63.8 0.5 load.3.down_ref
  64.3 0.6 collective-permute-done.11.refs_1_
  64.8 6.5 %collective-permute-done.12.refs_2_ = bf16[32,2560]{1,0:T(8,128)(2,1)S(1)} collective-permute-done((bf16[32,2560]{1,0:T(8,128)(2,1)S(1)}, bf16[32,2560]{1,0:T(8,128)(2,1)S(1)}, u32[]{:S(2)}, u32[]{:S(2)}) %collective-permute-start.12) | collective-permute-done | bytes 163872 | tf_op jit(solution)/shard_map/ppermute | solution.py:27
  71.4 0.9 shared_out.1
  72.3 0.1 collective-permute-start.17
  72.4 1.3 %collective-permute-done.17 = bf16[64,896]{1,0:T(8,128)(2,1)S(1)} collective-permute-done((bf16[64,896]{1,0:T(8,128)(2,1)S(1)}, bf16[64,896]{1,0:T(8,128)(2,1)S(1)}, u32[]{:S(2)}, u32[]{:S(2)}) %collective-permute-start.17) | collective-permute-done | bytes 114720 | tf_op jit(solution)/shard_map/ppermute | solution.py:37
  73.7 1.2 %collective-permute-start.18 = (bf16[32,896]{1,0:T(8,128)(2,1)S(1)}, bf16[32,896]{1,0:T(8,128)(2,1)S(1)}, u32[]{:S(2)}, u32[]{:S(2)}) collective-permute-start(bf16[32,896]{1,0:T(8,128)(2,1)S(1)} %slice.139), channel_id=1, source_target_pairs={{0,2},{1,3},{2,0},{3,1},{4,6},{5,7},{6,4},{7,5},{8,10},{9,11},{10,... | collective-permute-start | bytes 172040 | tf_op jit(solution)/shard_map/ppermute | solution.py:32
  74.9 3.1 %collective-permute-done.18 = bf16[32,896]{1,0:T(8,128)(2,1)S(1)} collective-permute-done((bf16[32,896]{1,0:T(8,128)(2,1)S(1)}, bf16[32,896]{1,0:T(8,128)(2,1)S(1)}, u32[]{:S(2)}, u32[]{:S(2)}) %collective-permute-start.18) | collective-permute-done | bytes 57376 | tf_op jit(solution)/shard_map/ppermute | solution.py:32
  78.0 5.3 %collective-permute-start.19 = (bf16[8,4480]{1,0:T(8,128)(2,1)S(1)}, bf16[8,4480]{1,0:T(8,128)(2,1)S(1)}, u32[]{:S(2)}, u32[]{:S(2)}) collective-permute-start(bf16[8,4480]{1,0:T(8,128)(2,1)S(1)} %get-tuple-element.71), channel_id=1, source_target_pairs={{0,12},{4,0},{8,4},{12,8},{1,13},{5,1},{9,5},{13,9},{2,14},{6,2},{... | collective-permute-start | bytes 215048 | tf_op jit(solution)/shard_map/ppermute | solution.py:27
  83.4 0.2 collective-permute-start.20
  83.5 0.5 collective-permute-start.21
  84.0 1.5 %collective-permute-done.19 = bf16[8,4480]{1,0:T(8,128)(2,1)S(1)} collective-permute-done((bf16[8,4480]{1,0:T(8,128)(2,1)S(1)}, bf16[8,4480]{1,0:T(8,128)(2,1)S(1)}, u32[]{:S(2)}, u32[]{:S(2)}) %collective-permute-start.19) | collective-permute-done | bytes 71712 | tf_op jit(solution)/shard_map/ppermute | solution.py:27
  85.6 3.4 %collective-permute-done.20 = bf16[8,4480]{1,0:T(8,128)(2,1)S(1)} collective-permute-done((bf16[8,4480]{1,0:T(8,128)(2,1)S(1)}, bf16[8,4480]{1,0:T(8,128)(2,1)S(1)}, u32[]{:S(2)}, u32[]{:S(2)}) %collective-permute-start.20) | collective-permute-done | bytes 71712 | tf_op jit(solution)/shard_map/ppermute | solution.py:27
  88.9 0.7 collective-permute-done.21
  89.8 0.6 convert_element_type.65
  (38 shorter events, 0.4 us)
Async XLA Ops:
  1.6 7.4 %collective-permute-start = (bf16[8,3712]{1,0:T(8,128)(2,1)S(1)}, bf16[8,3712]{1,0:T(8,128)(2,1)S(1)}, u32[]{:S(2)}, u32[]{:S(2)}) collective-permute-start(bf16[8,3712]{1,0:T(8,128)(2,1)S(1)} %concatenate.19), channel_id=1, source_target_pairs={{0,4},{4,8},{8,12},{12,0},{1,5},{5,9},{9,13},{13,1},{2,6},{6,10},{... | collective-permute-start | bytes 178184 | tf_op jit(solution)/shard_map/ppermute | solution.py:27
  4.6 6.7 %collective-permute-start.1 = (bf16[8,3712]{1,0:T(8,128)(2,1)S(1)}, bf16[8,3712]{1,0:T(8,128)(2,1)S(1)}, u32[]{:S(2)}, u32[]{:S(2)}) collective-permute-start(bf16[8,3712]{1,0:T(8,128)(2,1)S(1)} %concatenate.19), channel_id=1, source_target_pairs={{0,8},{4,12},{8,0},{12,4},{1,9},{5,13},{9,1},{13,5},{2,10},{6,14},... | collective-permute-start | bytes 178184 | tf_op jit(solution)/shard_map/ppermute | solution.py:27
  7.2 4.5 %collective-permute-start.2 = (bf16[8,3712]{1,0:T(8,128)(2,1)S(1)}, bf16[8,3712]{1,0:T(8,128)(2,1)S(1)}, u32[]{:S(2)}, u32[]{:S(2)}) collective-permute-start(bf16[8,3712]{1,0:T(8,128)(2,1)S(1)} %concatenate.19), channel_id=1, source_target_pairs={{0,12},{4,0},{8,4},{12,8},{1,13},{5,1},{9,5},{13,9},{2,14},{6,2},{... | collective-permute-start | bytes 178184 | tf_op jit(solution)/shard_map/ppermute | solution.py:27
  11.8 4.3 %collective-permute-start.3 = (bf16[32,896]{1,0:T(8,128)(2,1)S(1)}, bf16[32,896]{1,0:T(8,128)(2,1)S(1)}, u32[]{:S(2)}, u32[]{:S(2)}) collective-permute-start(bf16[32,896]{1,0:T(8,128)(2,1)S(1)} %constant_dynamic-slice_fusion.refs_0_), channel_id=1, source_target_pairs={{0,2},{1,3},{2,0},{3,1},{4,6},{5,7},{6,4},{7,5},{8,10},{9,11},{10,... | collective-permute-start | bytes 172040 | tf_op jit(solution)/shard_map/ppermute | solution.py:32
  13.3 2.3 %copy-start = (bf16[896,2560]{1,0:T(8,128)(2,1)S(1)}, bf16[896,2560]{1,0:T(8,128)(2,1)}, u32[]{:S(2)}) copy-start(bf16[896,2560]{1,0:T(8,128)(2,1)} %refs_0_.1) | copy-start | bytes 13762564
  15.6 3.3 %copy-start.1 = (bf16[896,2560]{1,0:T(8,128)(2,1)S(1)}, bf16[896,2560]{1,0:T(8,128)(2,1)}, u32[]{:S(2)}) copy-start(bf16[896,2560]{1,0:T(8,128)(2,1)} %gate_ref.2) | copy-start | bytes 13762564
  16.1 6.4 %copy-start.2 = (f32[3584]{0:T(1024)S(1)}, f32[3584]{0:T(1024)}, u32[]{:S(2)}) copy-start(f32[3584]{0:T(1024)} %param.19) | copy-start | bytes 43012
  16.1 6.2 %collective-permute-start.4 = (bf16[32,3712]{1,0:T(8,128)(2,1)S(1)}, bf16[32,3712]{1,0:T(8,128)(2,1)S(1)}, u32[]{:S(2)}, u32[]{:S(2)}) collective-permute-start(bf16[32,3712]{1,0:T(8,128)(2,1)S(1)} %pad_maximum_fusion.2), channel_id=1, source_target_pairs={{0,2},{1,3},{2,0},{3,1},{4,6},{5,7},{6,4},{7,5},{8,10},{9,11},{10,... | collective-permute-start | bytes 712712 | tf_op jit(solution)/shard_map/ppermute | solution.py:32
  17.5 1.2 %collective-permute-start.5 = (bf16[32,896]{1,0:T(8,128)(2,1)S(1)}, bf16[32,896]{1,0:T(8,128)(2,1)S(1)}, u32[]{:S(2)}, u32[]{:S(2)}) collective-permute-start(bf16[32,896]{1,0:T(8,128)(2,1)S(1)} %constant_dynamic-slice_fusion.refs_0_), channel_id=1, source_target_pairs={{0,1},{1,0},{2,3},{3,2},{4,5},{5,4},{6,7},{7,6},{8,9},{9,8},{10,11... | collective-permute-start | bytes 172040 | tf_op jit(solution)/shard_map/ppermute | solution.py:37
  17.5 1.4 %collective-permute-start.6 = (bf16[32,896]{1,0:T(8,128)(2,1)S(1)}, bf16[32,896]{1,0:T(8,128)(2,1)S(1)}, u32[]{:S(2)}, u32[]{:S(2)}) collective-permute-start(bf16[32,896]{1,0:T(8,128)(2,1)S(1)} %collective-permute-done.3.refs_1_), channel_id=1, source_target_pairs={{0,1},{1,0},{2,3},{3,2},{4,5},{5,4},{6,7},{7,6},{8,9},{9,8},{10,11... | collective-permute-start | bytes 172040 | tf_op jit(solution)/shard_map/ppermute | solution.py:37
  22.4 4.0 %collective-permute-start.7 = (bf16[64,3712]{1,0:T(8,128)(2,1)S(1)}, bf16[64,3712]{1,0:T(8,128)(2,1)S(1)}, u32[]{:S(2)}, u32[]{:S(2)}) collective-permute-start(bf16[64,3712]{1,0:T(8,128)(2,1)S(1)} %pad_maximum_fusion.1), channel_id=1, source_target_pairs={{0,1},{1,0},{2,3},{3,2},{4,5},{5,4},{6,7},{7,6},{8,9},{9,8},{10,11... | collective-permute-start | bytes 1425416 | tf_op jit(solution)/shard_map/ppermute | solution.py:37
  22.5 32.8 %collective-permute-start.10 = (bf16[2,32,2560]{2,1,0:T(8,128)(2,1)S(1)}, bf16[2,32,2560]{2,1,0:T(8,128)(2,1)S(1)}, u32[]{:S(2)}, u32[]{:S(2)}) collective-permute-start(bf16[2,32,2560]{2,1,0:T(8,128)(2,1)S(1)} %get-tuple-element.47), channel_id=1, source_target_pairs={{0,4},{4,8},{8,12},{12,0},{1,5},{5,9},{9,13},{13,1},{2,6},{6,10},{... | collective-permute-start | bytes 983048 | tf_op jit(solution)/shard_map/ppermute | solution.py:27
  24.7 30.6 %collective-permute-start.8 = (bf16[2,32,2560]{2,1,0:T(8,128)(2,1)S(1)}, bf16[2,32,2560]{2,1,0:T(8,128)(2,1)S(1)}, u32[]{:S(2)}, u32[]{:S(2)}) collective-permute-start(bf16[2,32,2560]{2,1,0:T(8,128)(2,1)S(1)} %get-tuple-element.45), channel_id=1, source_target_pairs={{0,12},{4,0},{8,4},{12,8},{1,13},{5,1},{9,5},{13,9},{2,14},{6,2},{... | collective-permute-start | bytes 983048 | tf_op jit(solution)/shard_map/ppermute | solution.py:27
  26.4 29.1 %collective-permute-start.9 = (bf16[2,32,2560]{2,1,0:T(8,128)(2,1)S(1)}, bf16[2,32,2560]{2,1,0:T(8,128)(2,1)S(1)}, u32[]{:S(2)}, u32[]{:S(2)}) collective-permute-start(bf16[2,32,2560]{2,1,0:T(8,128)(2,1)S(1)} %get-tuple-element.46), channel_id=1, source_target_pairs={{0,8},{4,12},{8,0},{12,4},{1,9},{5,13},{9,1},{13,5},{2,10},{6,14},... | collective-permute-start | bytes 983048 | tf_op jit(solution)/shard_map/ppermute | solution.py:27
  26.5 37.3 %slice-start = ((s8[4587520]{0:T(1024)(128)(4,1)}), s8[4194304]{0:T(1024)(128)(4,1)S(1)}, s32[]{:S(2)}) async-start(s8[4587520]{0:T(1024)(128)(4,1)} %bitcast.11), calls=%async_computation | async-start | bytes 8388608
  26.5 37.3 %slice-start.1 = ((s8[4587520]{0:T(1024)(128)(4,1)}), s8[393216]{0:T(1024)(128)(4,1)S(1)}, s32[]{:S(2)}) async-start(s8[4587520]{0:T(1024)(128)(4,1)} %bitcast.11), calls=%async_computation.1 | async-start | bytes 786432
  55.5 6.0 %collective-permute-start.14 = (bf16[64,3584]{1,0:T(8,128)(2,1)S(1)}, bf16[64,3584]{1,0:T(8,128)(2,1)S(1)}, u32[]{:S(2)}, u32[]{:S(2)}) collective-permute-start(bf16[64,3584]{1,0:T(8,128)(2,1)S(1)} %get-tuple-element.62), channel_id=1, source_target_pairs={{0,1},{1,0},{2,3},{3,2},{4,5},{5,4},{6,7},{7,6},{8,9},{9,8},{10,11... | collective-permute-start | bytes 1376264 | tf_op jit(solution)/shard_map/ppermute | solution.py:37
  55.8 9.0 %collective-permute-start.11 = (bf16[32,2560]{1,0:T(8,128)(2,1)S(1)}, bf16[32,2560]{1,0:T(8,128)(2,1)S(1)}, u32[]{:S(2)}, u32[]{:S(2)}) collective-permute-start(bf16[32,2560]{1,0:T(8,128)(2,1)S(1)} %fusion.1.refs_0_), channel_id=1, source_target_pairs={{0,4},{4,8},{8,12},{12,0},{1,5},{5,9},{9,13},{13,1},{2,6},{6,10},{... | collective-permute-start | bytes 491528 | tf_op jit(solution)/shard_map/ppermute | solution.py:27
  57.3 14.1 %collective-permute-start.12 = (bf16[32,2560]{1,0:T(8,128)(2,1)S(1)}, bf16[32,2560]{1,0:T(8,128)(2,1)S(1)}, u32[]{:S(2)}, u32[]{:S(2)}) collective-permute-start(bf16[32,2560]{1,0:T(8,128)(2,1)S(1)} %fusion.1.refs_0_), channel_id=1, source_target_pairs={{0,8},{4,12},{8,0},{12,4},{1,9},{5,13},{9,1},{13,5},{2,10},{6,14},... | collective-permute-start | bytes 491528 | tf_op jit(solution)/shard_map/ppermute | solution.py:27
  59.0 12.4 %collective-permute-start.13 = (bf16[32,2560]{1,0:T(8,128)(2,1)S(1)}, bf16[32,2560]{1,0:T(8,128)(2,1)S(1)}, u32[]{:S(2)}, u32[]{:S(2)}) collective-permute-start(bf16[32,2560]{1,0:T(8,128)(2,1)S(1)} %fusion.1.refs_0_), channel_id=1, source_target_pairs={{0,12},{4,0},{8,4},{12,8},{1,13},{5,1},{9,5},{13,9},{2,14},{6,2},{... | collective-permute-start | bytes 491528 | tf_op jit(solution)/shard_map/ppermute | solution.py:27
  61.7 10.5 %collective-permute-start.15 = (bf16[32,1792]{1,0:T(8,128)(2,1)S(1)}, bf16[32,1792]{1,0:T(8,128)(2,1)S(1)}, u32[]{:S(2)}, u32[]{:S(2)}) collective-permute-start(bf16[32,1792]{1,0:T(8,128)(2,1)S(1)} %get-tuple-element.75), channel_id=1, source_target_pairs={{0,2},{1,3},{2,0},{3,1},{4,6},{5,7},{6,4},{7,5},{8,10},{9,11},{10,... | collective-permute-start | bytes 344072 | tf_op jit(solution)/shard_map/ppermute | solution.py:32
  63.0 9.2 %collective-permute-start.16 = (bf16[32,1792]{1,0:T(8,128)(2,1)S(1)}, bf16[32,1792]{1,0:T(8,128)(2,1)S(1)}, u32[]{:S(2)}, u32[]{:S(2)}) collective-permute-start(bf16[32,1792]{1,0:T(8,128)(2,1)S(1)} %get-tuple-element.74), channel_id=1, source_target_pairs={{0,2},{1,3},{2,0},{3,1},{4,6},{5,7},{6,4},{7,5},{8,10},{9,11},{10,... | collective-permute-start | bytes 344072 | tf_op jit(solution)/shard_map/ppermute | solution.py:32
  72.3 1.4 %collective-permute-start.17 = (bf16[64,896]{1,0:T(8,128)(2,1)S(1)}, bf16[64,896]{1,0:T(8,128)(2,1)S(1)}, u32[]{:S(2)}, u32[]{:S(2)}) collective-permute-start(bf16[64,896]{1,0:T(8,128)(2,1)S(1)} %get-tuple-element.66), channel_id=1, source_target_pairs={{0,1},{1,0},{2,3},{3,2},{4,5},{5,4},{6,7},{7,6},{8,9},{9,8},{10,11... | collective-permute-start | bytes 344072 | tf_op jit(solution)/shard_map/ppermute | solution.py:37
  73.7 4.2 %collective-permute-start.18 = (bf16[32,896]{1,0:T(8,128)(2,1)S(1)}, bf16[32,896]{1,0:T(8,128)(2,1)S(1)}, u32[]{:S(2)}, u32[]{:S(2)}) collective-permute-start(bf16[32,896]{1,0:T(8,128)(2,1)S(1)} %slice.139), channel_id=1, source_target_pairs={{0,2},{1,3},{2,0},{3,1},{4,6},{5,7},{6,4},{7,5},{8,10},{9,11},{10,... | collective-permute-start | bytes 172040 | tf_op jit(solution)/shard_map/ppermute | solution.py:32
  78.0 7.5 %collective-permute-start.19 = (bf16[8,4480]{1,0:T(8,128)(2,1)S(1)}, bf16[8,4480]{1,0:T(8,128)(2,1)S(1)}, u32[]{:S(2)}, u32[]{:S(2)}) collective-permute-start(bf16[8,4480]{1,0:T(8,128)(2,1)S(1)} %get-tuple-element.71), channel_id=1, source_target_pairs={{0,12},{4,0},{8,4},{12,8},{1,13},{5,1},{9,5},{13,9},{2,14},{6,2},{... | collective-permute-start | bytes 215048 | tf_op jit(solution)/shard_map/ppermute | solution.py:27
  83.4 5.6 %collective-permute-start.20 = (bf16[8,4480]{1,0:T(8,128)(2,1)S(1)}, bf16[8,4480]{1,0:T(8,128)(2,1)S(1)}, u32[]{:S(2)}, u32[]{:S(2)}) collective-permute-start(bf16[8,4480]{1,0:T(8,128)(2,1)S(1)} %get-tuple-element.72), channel_id=1, source_target_pairs={{0,8},{4,12},{8,0},{12,4},{1,9},{5,13},{9,1},{13,5},{2,10},{6,14},... | collective-permute-start | bytes 215048 | tf_op jit(solution)/shard_map/ppermute | solution.py:27
  83.5 6.1 %collective-permute-start.21 = (bf16[8,4480]{1,0:T(8,128)(2,1)S(1)}, bf16[8,4480]{1,0:T(8,128)(2,1)S(1)}, u32[]{:S(2)}, u32[]{:S(2)}) collective-permute-start(bf16[8,4480]{1,0:T(8,128)(2,1)S(1)} %get-tuple-element.73), channel_id=1, source_target_pairs={{0,4},{4,8},{8,12},{12,0},{1,5},{5,9},{9,13},{13,1},{2,6},{6,10},{... | collective-permute-start | bytes 215048 | tf_op jit(solution)/shard_map/ppermute | solution.py:27

commit v4 on v3

--- a/solution.py
+++ b/solution.py
@@ -306,10 +306,15 @@
     )
     column = jnp.concatenate(gather_column([own] * spread), axis=0)
     part = lax.dynamic_slice_in_dim(column, here * depth, depth, axis=1)
-    parts, (column,), up = join(gather_plane(part), [column], load([shared_up], shared_up.shape[0]))
+    early = jnp.concatenate([part, column[:, feat:]], axis=1)
+    early, up = join(gather_plane(early), load([shared_up], shared_up.shape[0]))
+    parts = [piece[:, :depth] for piece in early]
     parts = parts + [core_swap(piece) for piece in parts]
     hidden_own, *hidden_parts = shared_in(parts, shared_gate, *up, rows)
-    plane, (hidden_own,) = join(gather_plane(column), [hidden_own])
+    plane, (hidden_own,) = join(gather_plane(column[:, :feat]), [hidden_own])
+    plane = [
+        jnp.concatenate([piece, rest[:, depth:]], axis=1) for piece, rest in zip(plane, early)
+    ]
     x = both_cores(jnp.concatenate(plane, axis=0))
 
     first = (here * local).astype(jnp.int32).reshape(1)

time: 90.7 us -> 88.7 us (0.978)
  waiting for transfers between devices: 22.9 us -> 20.7 us
    ppermute x5, waiting for transfers between devices: 4.63 us -> 2.88 us  [x_shift(): lax.ppermute(value, 'narrow', [(i, (i + 2 * step) % size) for i in range(...]
  transfers between devices with their start and end apart: 22 -> 22, of which waited for: 14 -> 13; matrix products, arithmetic and copies ran while one was open for 1% -> 1% of each run, Pallas kernels for 36% -> 37%
where the time goes in v4:
time: 88.7 us; the launch traced here: 88.5 us
  Pallas kernels  32.4 us (37%)
  starting transfers between devices  29.4 us (33%)
  waiting for transfers between devices  20.7 us (23%)
  local copies, waits for them, and re-layouts  3.59 us (4%)
  other arithmetic  2.04 us (2%)
    pallas_call x1, Pallas kernels, experts(): pl.pallas_call(functools.partial(experts_kernel, chosen), in_specs=[pl.Bl...  28.8 us
    ppermute x12, starting transfers between devices, z_shift(): lax.ppermute(value, 'expert', [(i, (i + step) % spread) for i in range(sp...  22.9 us
    ppermute x12, waiting for transfers between devices, z_shift(): lax.ppermute(value, 'expert', [(i, (i + step) % spread) for i in range(sp...  15.6 us
    ppermute x5, starting transfers between devices, x_shift(): lax.ppermute(value, 'narrow', [(i, (i + 2 * step) % size) for i in range(...  5.75 us
    ppermute x5, waiting for transfers between devices, x_shift(): lax.ppermute(value, 'narrow', [(i, (i + 2 * step) % size) for i in range(...  2.88 us
    unnamed x10, local copies, waits for them, and re-layouts  2.58 us
    ppermute x5, waiting for transfers between devices, core_swap(): return lax.ppermute(value, 'narrow', [(i, i ^ 1) for i in range(size)])  2.18 us
    pallas_call x1, Pallas kernels, shared_in(): pl.pallas_call(functools.partial(shared_in_kernel, (outer, spread, rows),...  1.84 us
  transfers between devices with their start and end apart: 22, of which 13 were waited for; matrix products, arithmetic and copies ran while one was open for 1% of the time, Pallas kernels for 37%

profile of v4, /device:TPU:0, one launch (start us, length us, event | category | flops | bytes accessed | tf_op | source)
XLA Modules:
  0.0 88.5 jit_solution(4277716645791619865)
XLA Ops:
  0.0 0.7 convert_element_type.51
  0.7 0.9 %concatenate.28 = bf16[8,3712]{1,0:T(8,128)(2,1)S(1)} concatenate(bf16[8,3584]{1,0:T(8,128)(2,1)} %param.10, bf16[8,8]{1,0:T(8,128)(2,1)S(1)} %convert_element_type.51, bf16[8,8]{1,0:T(8,128)(2,1)} %param.12, bf16[8,112]{1,0:T(8,128)(2,1)S(1)} %broadcast_in_dim.3), dimensions={1} | concatenate | bytes 118784 | tf_op jit(solution)/shard_map/concatenate | solution.py:298
  1.6 3.0 %collective-permute-start = (bf16[8,3712]{1,0:T(8,128)(2,1)S(1)}, bf16[8,3712]{1,0:T(8,128)(2,1)S(1)}, u32[]{:S(2)}, u32[]{:S(2)}) collective-permute-start(bf16[8,3712]{1,0:T(8,128)(2,1)S(1)} %concatenate.28), channel_id=1, source_target_pairs={{0,4},{4,8},{8,12},{12,0},{1,5},{5,9},{9,13},{13,1},{2,6},{6,10},{... | collective-permute-start | bytes 178184 | tf_op jit(solution)/shard_map/ppermute | solution.py:27
  4.6 2.6 %collective-permute-start.1 = (bf16[8,3712]{1,0:T(8,128)(2,1)S(1)}, bf16[8,3712]{1,0:T(8,128)(2,1)S(1)}, u32[]{:S(2)}, u32[]{:S(2)}) collective-permute-start(bf16[8,3712]{1,0:T(8,128)(2,1)S(1)} %concatenate.28), channel_id=1, source_target_pairs={{0,8},{4,12},{8,0},{12,4},{1,9},{5,13},{9,1},{13,5},{2,10},{6,14},... | collective-permute-start | bytes 178184 | tf_op jit(solution)/shard_map/ppermute | solution.py:27
  7.2 1.3 %collective-permute-start.2 = (bf16[8,3712]{1,0:T(8,128)(2,1)S(1)}, bf16[8,3712]{1,0:T(8,128)(2,1)S(1)}, u32[]{:S(2)}, u32[]{:S(2)}) collective-permute-start(bf16[8,3712]{1,0:T(8,128)(2,1)S(1)} %concatenate.28), channel_id=1, source_target_pairs={{0,12},{4,0},{8,4},{12,8},{1,13},{5,1},{9,5},{13,9},{2,14},{6,2},{... | collective-permute-start | bytes 178184 | tf_op jit(solution)/shard_map/ppermute | solution.py:27
  8.6 0.5 collective-permute-done
  9.0 2.3 %collective-permute-done.1 = bf16[8,3712]{1,0:T(8,128)(2,1)S(1)} collective-permute-done((bf16[8,3712]{1,0:T(8,128)(2,1)S(1)}, bf16[8,3712]{1,0:T(8,128)(2,1)S(1)}, u32[]{:S(2)}, u32[]{:S(2)}) %collective-permute-start.1) | collective-permute-done | bytes 59424 | tf_op jit(solution)/shard_map/ppermute | solution.py:27
  11.4 0.4 collective-permute-done.2
  11.8 1.5 %collective-permute-start.4 = (bf16[32,1024]{1,0:T(8,128)(2,1)S(1)}, bf16[32,1024]{1,0:T(8,128)(2,1)S(1)}, u32[]{:S(2)}, u32[]{:S(2)}) collective-permute-start(bf16[32,1024]{1,0:T(8,128)(2,1)S(1)} %pad_maximum_fusion.5), channel_id=1, source_target_pairs={{0,2},{1,3},{2,0},{3,1},{4,6},{5,7},{6,4},{7,5},{8,10},{9,11},{10,... | collective-permute-start | bytes 196616 | tf_op jit(solution)/shard_map/ppermute | solution.py:32
  13.4 0.6 collective-permute-start.3
  14.0 2.3 %copy-done = bf16[896,2560]{1,0:T(8,128)(2,1)S(1)} copy-done((bf16[896,2560]{1,0:T(8,128)(2,1)S(1)}, bf16[896,2560]{1,0:T(8,128)(2,1)}, u32[]{:S(2)}) %copy-start) | copy-done | bytes 4587544
  16.3 0.5 load.2.up_ref
  16.8 0.1 collective-permute-done.4
  16.9 0.5 collective-permute-start.6
  17.4 0.7 collective-permute-done.5.refs_2_
  18.2 0.2 collective-permute-done.6.refs_3_
  18.3 0.3 copy-done.1
  18.6 1.8 %shared_in.1 = (bf16[2,32,2560]{2,1,0:T(8,128)(2,1)S(1)}, bf16[2,32,2560]{2,1,0:T(8,128)(2,1)S(1)}, bf16[2,32,2560]{2,1,0:T(8,128)(2,1)S(1)}, bf16[2,32,2560]{2,1,0:T(8,128)(2,1)S(1)}) custom-call(bf16[896,2560]{1,0:T(8,128)(2,1)S(1)} %copy-done.1, bf16[896,2560]{1,0:T(8,128)(2,1)S(1)} %load.2.up_ref, bf16[32,896]{1,0:T(8,128)(2,1)S(1)} %slice.94.refs_0_, ...), custom_call_target="tpu_custom_call" | custom-call | flops 1174405120 | bytes 1310720 | tf_op jit(solution)/shard_map/shared_in/pallas_call | solution.py:118
  20.5 0.2 collective-permute-start.7
  20.7 1.8 %collective-permute-start.10 = (bf16[2,32,2560]{2,1,0:T(8,128)(2,1)S(1)}, bf16[2,32,2560]{2,1,0:T(8,128)(2,1)S(1)}, u32[]{:S(2)}, u32[]{:S(2)}) collective-permute-start(bf16[2,32,2560]{2,1,0:T(8,128)(2,1)S(1)} %get-tuple-element.45), channel_id=1, source_target_pairs={{0,4},{4,8},{8,12},{12,0},{1,5},{5,9},{9,13},{13,1},{2,6},{6,10},{... | collective-permute-start | bytes 983048 | tf_op jit(solution)/shard_map/ppermute | solution.py:27
  22.5 2.1 %collective-permute-start.8 = (bf16[2,32,2560]{2,1,0:T(8,128)(2,1)S(1)}, bf16[2,32,2560]{2,1,0:T(8,128)(2,1)S(1)}, u32[]{:S(2)}, u32[]{:S(2)}) collective-permute-start(bf16[2,32,2560]{2,1,0:T(8,128)(2,1)S(1)} %get-tuple-element.43), channel_id=1, source_target_pairs={{0,12},{4,0},{8,4},{12,8},{1,13},{5,1},{9,5},{13,9},{2,14},{6,2},{... | collective-permute-start | bytes 983048 | tf_op jit(solution)/shard_map/ppermute | solution.py:27
  24.5 0.1 pad_maximum_fusion.x_ref
  24.6 0.0 slice-start
  24.6 28.8 %experts.1 = (f32[128,128]{1,0:T(8,128)S(1)}, f32[64,3584]{1,0:T(8,128)S(1)}, bf16[64,3584]{1,0:T(8,128)(2,1)S(1)}) custom-call(s32[1]{0:T(128)} %bitcast.first_ref, bf16[128,3712]{1,0:T(8,128)(2,1)S(1)} %pad_maximum_fusion.x_ref, f32[1,3584]{1,0:T(1,128)S(1)} %reshape.7.scale_ref, bf16[8,3584,512]{2,1,0:T(8,128)(2,1)} %gate_ref.3, ...), custom_call_target="tpu_custom_call" | custom-call | flops 11274289152 | bytes 88080384 | tf_op jit(solution)/shard_map/experts/pallas_call | solution.py:207
  53.5 0.1 collective-permute-start.14
  53.5 0.2 convert_add_fusion.1
  53.7 0.1 fusion.1.refs_0_
  53.8 1.6 %collective-permute-start.11 = (bf16[32,2560]{1,0:T(8,128)(2,1)S(1)}, bf16[32,2560]{1,0:T(8,128)(2,1)S(1)}, u32[]{:S(2)}, u32[]{:S(2)}) collective-permute-start(bf16[32,2560]{1,0:T(8,128)(2,1)S(1)} %fusion.1.refs_0_), channel_id=1, source_target_pairs={{0,4},{4,8},{8,12},{12,0},{1,5},{5,9},{9,13},{13,1},{2,6},{6,10},{... | collective-permute-start | bytes 491528 | tf_op jit(solution)/shard_map/ppermute | solution.py:27
  55.4 1.4 %collective-permute-start.12 = (bf16[32,2560]{1,0:T(8,128)(2,1)S(1)}, bf16[32,2560]{1,0:T(8,128)(2,1)S(1)}, u32[]{:S(2)}, u32[]{:S(2)}) collective-permute-start(bf16[32,2560]{1,0:T(8,128)(2,1)S(1)} %fusion.1.refs_0_), channel_id=1, source_target_pairs={{0,8},{4,12},{8,0},{12,4},{1,9},{5,13},{9,1},{13,5},{2,10},{6,14},... | collective-permute-start | bytes 491528 | tf_op jit(solution)/shard_map/ppermute | solution.py:27
  56.9 2.8 %collective-permute-start.13 = (bf16[32,2560]{1,0:T(8,128)(2,1)S(1)}, bf16[32,2560]{1,0:T(8,128)(2,1)S(1)}, u32[]{:S(2)}, u32[]{:S(2)}) collective-permute-start(bf16[32,2560]{1,0:T(8,128)(2,1)S(1)} %fusion.1.refs_0_), channel_id=1, source_target_pairs={{0,12},{4,0},{8,4},{12,8},{1,13},{5,1},{9,5},{13,9},{2,14},{6,2},{... | collective-permute-start | bytes 491528 | tf_op jit(solution)/shard_map/ppermute | solution.py:27
  59.7 0.1 fusion.7
  59.9 1.5 %collective-permute-start.15 = (bf16[32,1792]{1,0:T(8,128)(2,1)S(1)}, bf16[32,1792]{1,0:T(8,128)(2,1)S(1)}, u32[]{:S(2)}, u32[]{:S(2)}) collective-permute-start(bf16[32,1792]{1,0:T(8,128)(2,1)S(1)} %get-tuple-element.73), channel_id=1, source_target_pairs={{0,2},{1,3},{2,0},{3,1},{4,6},{5,7},{6,4},{7,5},{8,10},{9,11},{10,... | collective-permute-start | bytes 344072 | tf_op jit(solution)/shard_map/ppermute | solution.py:32
  61.4 0.6 collective-permute-start.16
  62.0 0.5 load.3.down_ref
  62.4 0.4 collective-permute-done.11.refs_1_
  62.8 6.6 %collective-permute-done.12.refs_2_ = bf16[32,2560]{1,0:T(8,128)(2,1)S(1)} collective-permute-done((bf16[32,2560]{1,0:T(8,128)(2,1)S(1)}, bf16[32,2560]{1,0:T(8,128)(2,1)S(1)}, u32[]{:S(2)}, u32[]{:S(2)}) %collective-permute-start.12) | collective-permute-done | bytes 163872 | tf_op jit(solution)/shard_map/ppermute | solution.py:27
  69.4 0.9 shared_out.1
  70.3 0.1 collective-permute-start.17
  70.4 1.3 %collective-permute-done.17 = bf16[64,896]{1,0:T(8,128)(2,1)S(1)} collective-permute-done((bf16[64,896]{1,0:T(8,128)(2,1)S(1)}, bf16[64,896]{1,0:T(8,128)(2,1)S(1)}, u32[]{:S(2)}, u32[]{:S(2)}) %collective-permute-start.17) | collective-permute-done | bytes 114720 | tf_op jit(solution)/shard_map/ppermute | solution.py:37
  71.8 1.5 %collective-permute-start.18 = (bf16[32,896]{1,0:T(8,128)(2,1)S(1)}, bf16[32,896]{1,0:T(8,128)(2,1)S(1)}, u32[]{:S(2)}, u32[]{:S(2)}) collective-permute-start(bf16[32,896]{1,0:T(8,128)(2,1)S(1)} %slice.165), channel_id=1, source_target_pairs={{0,2},{1,3},{2,0},{3,1},{4,6},{5,7},{6,4},{7,5},{8,10},{9,11},{10,... | collective-permute-start | bytes 172040 | tf_op jit(solution)/shard_map/ppermute | solution.py:32
  73.3 2.7 %collective-permute-done.18 = bf16[32,896]{1,0:T(8,128)(2,1)S(1)} collective-permute-done((bf16[32,896]{1,0:T(8,128)(2,1)S(1)}, bf16[32,896]{1,0:T(8,128)(2,1)S(1)}, u32[]{:S(2)}, u32[]{:S(2)}) %collective-permute-start.18) | collective-permute-done | bytes 57376 | tf_op jit(solution)/shard_map/ppermute | solution.py:32
  76.1 5.5 %collective-permute-start.19 = (bf16[8,4480]{1,0:T(8,128)(2,1)S(1)}, bf16[8,4480]{1,0:T(8,128)(2,1)S(1)}, u32[]{:S(2)}, u32[]{:S(2)}) collective-permute-start(bf16[8,4480]{1,0:T(8,128)(2,1)S(1)} %get-tuple-element.69), channel_id=1, source_target_pairs={{0,12},{4,0},{8,4},{12,8},{1,13},{5,1},{9,5},{13,9},{2,14},{6,2},{... | collective-permute-start | bytes 215048 | tf_op jit(solution)/shard_map/ppermute | solution.py:27
  81.5 0.0 collective-permute-start.20
  81.6 0.6 collective-permute-start.21
  82.2 1.5 %collective-permute-done.19 = bf16[8,4480]{1,0:T(8,128)(2,1)S(1)} collective-permute-done((bf16[8,4480]{1,0:T(8,128)(2,1)S(1)}, bf16[8,4480]{1,0:T(8,128)(2,1)S(1)}, u32[]{:S(2)}, u32[]{:S(2)}) %collective-permute-start.19) | collective-permute-done | bytes 71712 | tf_op jit(solution)/shard_map/ppermute | solution.py:27
  83.7 3.2 %collective-permute-done.20 = bf16[8,4480]{1,0:T(8,128)(2,1)S(1)} collective-permute-done((bf16[8,4480]{1,0:T(8,128)(2,1)S(1)}, bf16[8,4480]{1,0:T(8,128)(2,1)S(1)}, u32[]{:S(2)}, u32[]{:S(2)}) %collective-permute-start.20) | collective-permute-done | bytes 71712 | tf_op jit(solution)/shard_map/ppermute | solution.py:27
  87.0 0.7 collective-permute-done.21
  87.9 0.6 convert_element_type.65
  (45 shorter events, 0.4 us)
Async XLA Ops:
  1.6 7.4 %collective-permute-start = (bf16[8,3712]{1,0:T(8,128)(2,1)S(1)}, bf16[8,3712]{1,0:T(8,128)(2,1)S(1)}, u32[]{:S(2)}, u32[]{:S(2)}) collective-permute-start(bf16[8,3712]{1,0:T(8,128)(2,1)S(1)} %concatenate.28), channel_id=1, source_target_pairs={{0,4},{4,8},{8,12},{12,0},{1,5},{5,9},{9,13},{13,1},{2,6},{6,10},{... | collective-permute-start | bytes 178184 | tf_op jit(solution)/shard_map/ppermute | solution.py:27
  4.6 6.7 %collective-permute-start.1 = (bf16[8,3712]{1,0:T(8,128)(2,1)S(1)}, bf16[8,3712]{1,0:T(8,128)(2,1)S(1)}, u32[]{:S(2)}, u32[]{:S(2)}) collective-permute-start(bf16[8,3712]{1,0:T(8,128)(2,1)S(1)} %concatenate.28), channel_id=1, source_target_pairs={{0,8},{4,12},{8,0},{12,4},{1,9},{5,13},{9,1},{13,5},{2,10},{6,14},... | collective-permute-start | bytes 178184 | tf_op jit(solution)/shard_map/ppermute | solution.py:27
  7.2 4.5 %collective-permute-start.2 = (bf16[8,3712]{1,0:T(8,128)(2,1)S(1)}, bf16[8,3712]{1,0:T(8,128)(2,1)S(1)}, u32[]{:S(2)}, u32[]{:S(2)}) collective-permute-start(bf16[8,3712]{1,0:T(8,128)(2,1)S(1)} %concatenate.28), channel_id=1, source_target_pairs={{0,12},{4,0},{8,4},{12,8},{1,13},{5,1},{9,5},{13,9},{2,14},{6,2},{... | collective-permute-start | bytes 178184 | tf_op jit(solution)/shard_map/ppermute | solution.py:27
  11.8 5.1 %collective-permute-start.4 = (bf16[32,1024]{1,0:T(8,128)(2,1)S(1)}, bf16[32,1024]{1,0:T(8,128)(2,1)S(1)}, u32[]{:S(2)}, u32[]{:S(2)}) collective-permute-start(bf16[32,1024]{1,0:T(8,128)(2,1)S(1)} %pad_maximum_fusion.5), channel_id=1, source_target_pairs={{0,2},{1,3},{2,0},{3,1},{4,6},{5,7},{6,4},{7,5},{8,10},{9,11},{10,... | collective-permute-start | bytes 196616 | tf_op jit(solution)/shard_map/ppermute | solution.py:32
  13.4 7.1 %collective-permute-start.3 = (bf16[32,3584]{1,0:T(8,128)(2,1)S(1)}, bf16[32,3584]{1,0:T(8,128)(2,1)S(1)}, u32[]{:S(2)}, u32[]{:S(2)}) collective-permute-start(bf16[32,3584]{1,0:T(8,128)(2,1)S(1)} %slice.117), channel_id=1, source_target_pairs={{0,2},{1,3},{2,0},{3,1},{4,6},{5,7},{6,4},{7,5},{8,10},{9,11},{10,... | collective-permute-start | bytes 688136 | tf_op jit(solution)/shard_map/ppermute | solution.py:32
  14.0 2.3 %copy-start = (bf16[896,2560]{1,0:T(8,128)(2,1)S(1)}, bf16[896,2560]{1,0:T(8,128)(2,1)}, u32[]{:S(2)}) copy-start(bf16[896,2560]{1,0:T(8,128)(2,1)} %refs_0_.1) | copy-start | bytes 13762564
  16.3 2.3 %copy-start.1 = (bf16[896,2560]{1,0:T(8,128)(2,1)S(1)}, bf16[896,2560]{1,0:T(8,128)(2,1)}, u32[]{:S(2)}) copy-start(bf16[896,2560]{1,0:T(8,128)(2,1)} %gate_ref.2) | copy-start | bytes 13762564
  16.9 1.2 %collective-permute-start.5 = (bf16[32,896]{1,0:T(8,128)(2,1)S(1)}, bf16[32,896]{1,0:T(8,128)(2,1)S(1)}, u32[]{:S(2)}, u32[]{:S(2)}) collective-permute-start(bf16[32,896]{1,0:T(8,128)(2,1)S(1)} %slice.94.refs_0_), channel_id=1, source_target_pairs={{0,1},{1,0},{2,3},{3,2},{4,5},{5,4},{6,7},{7,6},{8,9},{9,8},{10,11... | collective-permute-start | bytes 172040 | tf_op jit(solution)/shard_map/ppermute | solution.py:37
  16.9 1.4 %collective-permute-start.6 = (bf16[32,896]{1,0:T(8,128)(2,1)S(1)}, bf16[32,896]{1,0:T(8,128)(2,1)S(1)}, u32[]{:S(2)}, u32[]{:S(2)}) collective-permute-start(bf16[32,896]{1,0:T(8,128)(2,1)S(1)} %slice.95.refs_1_), channel_id=1, source_target_pairs={{0,1},{1,0},{2,3},{3,2},{4,5},{5,4},{6,7},{7,6},{8,9},{9,8},{10,11... | collective-permute-start | bytes 172040 | tf_op jit(solution)/shard_map/ppermute | solution.py:37
  17.4 3.2 %copy-start.2 = (f32[3584]{0:T(1024)S(1)}, f32[3584]{0:T(1024)}, u32[]{:S(2)}) copy-start(f32[3584]{0:T(1024)} %param.19) | copy-start | bytes 43012
  20.5 4.1 %collective-permute-start.7 = (bf16[64,3712]{1,0:T(8,128)(2,1)S(1)}, bf16[64,3712]{1,0:T(8,128)(2,1)S(1)}, u32[]{:S(2)}, u32[]{:S(2)}) collective-permute-start(bf16[64,3712]{1,0:T(8,128)(2,1)S(1)} %maximum_maximum_fusion), channel_id=1, source_target_pairs={{0,1},{1,0},{2,3},{3,2},{4,5},{5,4},{6,7},{7,6},{8,9},{9,8},{10,11... | collective-permute-start | bytes 1425416 | tf_op jit(solution)/shard_map/ppermute | solution.py:37
  20.7 32.8 %collective-permute-start.10 = (bf16[2,32,2560]{2,1,0:T(8,128)(2,1)S(1)}, bf16[2,32,2560]{2,1,0:T(8,128)(2,1)S(1)}, u32[]{:S(2)}, u32[]{:S(2)}) collective-permute-start(bf16[2,32,2560]{2,1,0:T(8,128)(2,1)S(1)} %get-tuple-element.45), channel_id=1, source_target_pairs={{0,4},{4,8},{8,12},{12,0},{1,5},{5,9},{9,13},{13,1},{2,6},{6,10},{... | collective-permute-start | bytes 983048 | tf_op jit(solution)/shard_map/ppermute | solution.py:27
  22.5 31.0 %collective-permute-start.8 = (bf16[2,32,2560]{2,1,0:T(8,128)(2,1)S(1)}, bf16[2,32,2560]{2,1,0:T(8,128)(2,1)S(1)}, u32[]{:S(2)}, u32[]{:S(2)}) collective-permute-start(bf16[2,32,2560]{2,1,0:T(8,128)(2,1)S(1)} %get-tuple-element.43), channel_id=1, source_target_pairs={{0,12},{4,0},{8,4},{12,8},{1,13},{5,1},{9,5},{13,9},{2,14},{6,2},{... | collective-permute-start | bytes 983048 | tf_op jit(solution)/shard_map/ppermute | solution.py:27
  24.5 28.9 %collective-permute-start.9 = (bf16[2,32,2560]{2,1,0:T(8,128)(2,1)S(1)}, bf16[2,32,2560]{2,1,0:T(8,128)(2,1)S(1)}, u32[]{:S(2)}, u32[]{:S(2)}) collective-permute-start(bf16[2,32,2560]{2,1,0:T(8,128)(2,1)S(1)} %get-tuple-element.44), channel_id=1, source_target_pairs={{0,8},{4,12},{8,0},{12,4},{1,9},{5,13},{9,1},{13,5},{2,10},{6,14},... | collective-permute-start | bytes 983048 | tf_op jit(solution)/shard_map/ppermute | solution.py:27
  24.6 37.3 %slice-start = ((s8[4587520]{0:T(1024)(128)(4,1)}), s8[4194304]{0:T(1024)(128)(4,1)S(1)}, s32[]{:S(2)}) async-start(s8[4587520]{0:T(1024)(128)(4,1)} %bitcast.11), calls=%async_computation | async-start | bytes 8388608
  24.6 37.3 %slice-start.1 = ((s8[4587520]{0:T(1024)(128)(4,1)}), s8[393216]{0:T(1024)(128)(4,1)S(1)}, s32[]{:S(2)}) async-start(s8[4587520]{0:T(1024)(128)(4,1)} %bitcast.11), calls=%async_computation.1 | async-start | bytes 786432
  53.5 6.2 %collective-permute-start.14 = (bf16[64,3584]{1,0:T(8,128)(2,1)S(1)}, bf16[64,3584]{1,0:T(8,128)(2,1)S(1)}, u32[]{:S(2)}, u32[]{:S(2)}) collective-permute-start(bf16[64,3584]{1,0:T(8,128)(2,1)S(1)} %get-tuple-element.60), channel_id=1, source_target_pairs={{0,1},{1,0},{2,3},{3,2},{4,5},{5,4},{6,7},{7,6},{8,9},{9,8},{10,11... | collective-permute-start | bytes 1376264 | tf_op jit(solution)/shard_map/ppermute | solution.py:37
  53.8 9.0 %collective-permute-start.11 = (bf16[32,2560]{1,0:T(8,128)(2,1)S(1)}, bf16[32,2560]{1,0:T(8,128)(2,1)S(1)}, u32[]{:S(2)}, u32[]{:S(2)}) collective-permute-start(bf16[32,2560]{1,0:T(8,128)(2,1)S(1)} %fusion.1.refs_0_), channel_id=1, source_target_pairs={{0,4},{4,8},{8,12},{12,0},{1,5},{5,9},{9,13},{13,1},{2,6},{6,10},{... | collective-permute-start | bytes 491528 | tf_op jit(solution)/shard_map/ppermute | solution.py:27
  55.4 14.0 %collective-permute-start.12 = (bf16[32,2560]{1,0:T(8,128)(2,1)S(1)}, bf16[32,2560]{1,0:T(8,128)(2,1)S(1)}, u32[]{:S(2)}, u32[]{:S(2)}) collective-permute-start(bf16[32,2560]{1,0:T(8,128)(2,1)S(1)} %fusion.1.refs_0_), channel_id=1, source_target_pairs={{0,8},{4,12},{8,0},{12,4},{1,9},{5,13},{9,1},{13,5},{2,10},{6,14},... | collective-permute-start | bytes 491528 | tf_op jit(solution)/shard_map/ppermute | solution.py:27
  56.9 12.5 %collective-permute-start.13 = (bf16[32,2560]{1,0:T(8,128)(2,1)S(1)}, bf16[32,2560]{1,0:T(8,128)(2,1)S(1)}, u32[]{:S(2)}, u32[]{:S(2)}) collective-permute-start(bf16[32,2560]{1,0:T(8,128)(2,1)S(1)} %fusion.1.refs_0_), channel_id=1, source_target_pairs={{0,12},{4,0},{8,4},{12,8},{1,13},{5,1},{9,5},{13,9},{2,14},{6,2},{... | collective-permute-start | bytes 491528 | tf_op jit(solution)/shard_map/ppermute | solution.py:27
  59.9 10.4 %collective-permute-start.15 = (bf16[32,1792]{1,0:T(8,128)(2,1)S(1)}, bf16[32,1792]{1,0:T(8,128)(2,1)S(1)}, u32[]{:S(2)}, u32[]{:S(2)}) collective-permute-start(bf16[32,1792]{1,0:T(8,128)(2,1)S(1)} %get-tuple-element.73), channel_id=1, source_target_pairs={{0,2},{1,3},{2,0},{3,1},{4,6},{5,7},{6,4},{7,5},{8,10},{9,11},{10,... | collective-permute-start | bytes 344072 | tf_op jit(solution)/shard_map/ppermute | solution.py:32
  61.4 8.9 %collective-permute-start.16 = (bf16[32,1792]{1,0:T(8,128)(2,1)S(1)}, bf16[32,1792]{1,0:T(8,128)(2,1)S(1)}, u32[]{:S(2)}, u32[]{:S(2)}) collective-permute-start(bf16[32,1792]{1,0:T(8,128)(2,1)S(1)} %get-tuple-element.72), channel_id=1, source_target_pairs={{0,2},{1,3},{2,0},{3,1},{4,6},{5,7},{6,4},{7,5},{8,10},{9,11},{10,... | collective-permute-start | bytes 344072 | tf_op jit(solution)/shard_map/ppermute | solution.py:32
  70.3 1.4 %collective-permute-start.17 = (bf16[64,896]{1,0:T(8,128)(2,1)S(1)}, bf16[64,896]{1,0:T(8,128)(2,1)S(1)}, u32[]{:S(2)}, u32[]{:S(2)}) collective-permute-start(bf16[64,896]{1,0:T(8,128)(2,1)S(1)} %get-tuple-element.64), channel_id=1, source_target_pairs={{0,1},{1,0},{2,3},{3,2},{4,5},{5,4},{6,7},{7,6},{8,9},{9,8},{10,11... | collective-permute-start | bytes 344072 | tf_op jit(solution)/shard_map/ppermute | solution.py:37
  71.8 4.2 %collective-permute-start.18 = (bf16[32,896]{1,0:T(8,128)(2,1)S(1)}, bf16[32,896]{1,0:T(8,128)(2,1)S(1)}, u32[]{:S(2)}, u32[]{:S(2)}) collective-permute-start(bf16[32,896]{1,0:T(8,128)(2,1)S(1)} %slice.165), channel_id=1, source_target_pairs={{0,2},{1,3},{2,0},{3,1},{4,6},{5,7},{6,4},{7,5},{8,10},{9,11},{10,... | collective-permute-start | bytes 172040 | tf_op jit(solution)/shard_map/ppermute | solution.py:32
  76.1 7.7 %collective-permute-start.19 = (bf16[8,4480]{1,0:T(8,128)(2,1)S(1)}, bf16[8,4480]{1,0:T(8,128)(2,1)S(1)}, u32[]{:S(2)}, u32[]{:S(2)}) collective-permute-start(bf16[8,4480]{1,0:T(8,128)(2,1)S(1)} %get-tuple-element.69), channel_id=1, source_target_pairs={{0,12},{4,0},{8,4},{12,8},{1,13},{5,1},{9,5},{13,9},{2,14},{6,2},{... | collective-permute-start | bytes 215048 | tf_op jit(solution)/shard_map/ppermute | solution.py:27
  81.5 5.4 %collective-permute-start.20 = (bf16[8,4480]{1,0:T(8,128)(2,1)S(1)}, bf16[8,4480]{1,0:T(8,128)(2,1)S(1)}, u32[]{:S(2)}, u32[]{:S(2)}) collective-permute-start(bf16[8,4480]{1,0:T(8,128)(2,1)S(1)} %get-tuple-element.70), channel_id=1, source_target_pairs={{0,8},{4,12},{8,0},{12,4},{1,9},{5,13},{9,1},{13,5},{2,10},{6,14},... | collective-permute-start | bytes 215048 | tf_op jit(solution)/shard_map/ppermute | solution.py:27
  81.6 6.1 %collective-permute-start.21 = (bf16[8,4480]{1,0:T(8,128)(2,1)S(1)}, bf16[8,4480]{1,0:T(8,128)(2,1)S(1)}, u32[]{:S(2)}, u32[]{:S(2)}) collective-permute-start(bf16[8,4480]{1,0:T(8,128)(2,1)S(1)} %get-tuple-element.71), channel_id=1, source_target_pairs={{0,4},{4,8},{8,12},{12,0},{1,5},{5,9},{9,13},{13,1},{2,6},{6,10},{... | collective-permute-start | bytes 215048 | tf_op jit(solution)/shard_map/ppermute | solution.py:27

commit v5 on v4

--- a/solution.py
+++ b/solution.py
@@ -335,20 +335,15 @@
     acts, down = join(acts, load(down, shared_down.shape[0]))
     part = shared_out(branch, *down, acts, rows)
     part, routed = join(part, routed)
-    both = jnp.concatenate([*routed, narrow_sum(*part)], axis=1)
-    pieces = [both[:rows]] + [
-        z_shift(both[d * rows : (d + 1) * rows].astype(jnp.bfloat16), -d).astype(jnp.float32)
-        for d in range(1, spread)
-    ]
-    total = pieces[0][:, :feat]
-    for piece in pieces[1:]:
-        total = total + piece[:, :feat]
-    width = shared_down.shape[1]
-    for d, piece in enumerate(pieces):
-        at = lax.rem(here + d, spread) * width
-        old = lax.dynamic_slice_in_dim(total, at, width, axis=1)
-        total = lax.dynamic_update_slice_in_dim(total, old + piece[:, feat:], at, axis=1)
-    return total.astype(jnp.bfloat16)
+    total, part = jnp.concatenate(routed, axis=1), narrow_sum(*part)
+    at = here * part.shape[1]
+    part = part + lax.dynamic_slice_in_dim(total, at, part.shape[1], axis=1)
+    total = lax.dynamic_update_slice_in_dim(total, part, at, axis=1)
+    out = total[:rows]
+    for d in range(1, spread):
+        piece = total[d * rows : (d + 1) * rows].astype(jnp.bfloat16)
+        out = out + z_shift(piece, -d).astype(jnp.float32)
+    return out.astype(jnp.bfloat16)
 
 
 def solution(mesh):

time: 88.7 us -> 88.4 us (level)
  waiting for transfers between devices: 20.7 us -> 18.2 us
  local copies, waits for them, and re-layouts: 3.59 us -> 5.92 us
    ppermute x12, waiting for transfers between devices: 15.6 us -> 13.2 us  [z_shift(): lax.ppermute(value, 'expert', [(i, (i + step) % spread) for i in range(sp...]
    unnamed x10 -> x9, local copies, waits for them, and re-layouts: 2.58 us -> 4.89 us
  transfers between devices with their start and end apart: 22 -> 22, of which waited for: 13 -> 12; matrix products, arithmetic and copies ran while one was open for 1% -> 1% of each run, Pallas kernels for 37% -> 37%
where the time goes in v5:
time: 88.4 us; the launch traced here: 88.1 us
  Pallas kernels  32.3 us (37%)
  starting transfers between devices  29.4 us (33%)
  waiting for transfers between devices  18.2 us (21%)
  local copies, waits for them, and re-layouts  5.92 us (7%)
  other arithmetic  1.95 us (2%)
    pallas_call x1, Pallas kernels, experts(): pl.pallas_call(functools.partial(experts_kernel, chosen), in_specs=[pl.Bl...  28.6 us
    ppermute x12, starting transfers between devices, z_shift(): lax.ppermute(value, 'expert', [(i, (i + step) % spread) for i in range(sp...  22.9 us
    ppermute x12, waiting for transfers between devices, z_shift(): lax.ppermute(value, 'expert', [(i, (i + step) % spread) for i in range(sp...  13.2 us
    ppermute x5, starting transfers between devices, x_shift(): lax.ppermute(value, 'narrow', [(i, (i + 2 * step) % size) for i in range(...  5.75 us
    unnamed x9, local copies, waits for them, and re-layouts  4.89 us
    ppermute x5, waiting for transfers between devices, x_shift(): lax.ppermute(value, 'narrow', [(i, (i + 2 * step) % size) for i in range(...  2.86 us
    ppermute x5, waiting for transfers between devices, core_swap(): return lax.ppermute(value, 'narrow', [(i, i ^ 1) for i in range(size)])  2.16 us
    pallas_call x1, Pallas kernels, shared_in(): pl.pallas_call(functools.partial(shared_in_kernel, (outer, spread, rows),...  1.84 us
  transfers between devices with their start and end apart: 22, of which 12 were waited for; matrix products, arithmetic and copies ran while one was open for 1% of the time, Pallas kernels for 37%

profile of v5, /device:TPU:0, one launch (start us, length us, event | category | flops | bytes accessed | tf_op | source)
XLA Modules:
  0.0 88.1 jit_solution(7656330176203794598)
XLA Ops:
  0.0 0.7 convert_element_type.51
  0.7 0.9 %concatenate.25 = bf16[8,3712]{1,0:T(8,128)(2,1)S(1)} concatenate(bf16[8,3584]{1,0:T(8,128)(2,1)} %param.10, bf16[8,8]{1,0:T(8,128)(2,1)S(1)} %convert_element_type.51, bf16[8,8]{1,0:T(8,128)(2,1)} %param.12, bf16[8,112]{1,0:T(8,128)(2,1)S(1)} %broadcast_in_dim.3), dimensions={1} | concatenate | bytes 118784 | tf_op jit(solution)/shard_map/concatenate | solution.py:298
  1.6 3.0 %collective-permute-start = (bf16[8,3712]{1,0:T(8,128)(2,1)S(1)}, bf16[8,3712]{1,0:T(8,128)(2,1)S(1)}, u32[]{:S(2)}, u32[]{:S(2)}) collective-permute-start(bf16[8,3712]{1,0:T(8,128)(2,1)S(1)} %concatenate.25), channel_id=1, source_target_pairs={{0,4},{4,8},{8,12},{12,0},{1,5},{5,9},{9,13},{13,1},{2,6},{6,10},{... | collective-permute-start | bytes 178184 | tf_op jit(solution)/shard_map/ppermute | solution.py:27
  4.6 2.6 %collective-permute-start.1 = (bf16[8,3712]{1,0:T(8,128)(2,1)S(1)}, bf16[8,3712]{1,0:T(8,128)(2,1)S(1)}, u32[]{:S(2)}, u32[]{:S(2)}) collective-permute-start(bf16[8,3712]{1,0:T(8,128)(2,1)S(1)} %concatenate.25), channel_id=1, source_target_pairs={{0,8},{4,12},{8,0},{12,4},{1,9},{5,13},{9,1},{13,5},{2,10},{6,14},... | collective-permute-start | bytes 178184 | tf_op jit(solution)/shard_map/ppermute | solution.py:27
  7.2 1.3 %collective-permute-start.2 = (bf16[8,3712]{1,0:T(8,128)(2,1)S(1)}, bf16[8,3712]{1,0:T(8,128)(2,1)S(1)}, u32[]{:S(2)}, u32[]{:S(2)}) collective-permute-start(bf16[8,3712]{1,0:T(8,128)(2,1)S(1)} %concatenate.25), channel_id=1, source_target_pairs={{0,12},{4,0},{8,4},{12,8},{1,13},{5,1},{9,5},{13,9},{2,14},{6,2},{... | collective-permute-start | bytes 178184 | tf_op jit(solution)/shard_map/ppermute | solution.py:27
  8.6 0.5 collective-permute-done
  9.0 2.3 %collective-permute-done.1 = bf16[8,3712]{1,0:T(8,128)(2,1)S(1)} collective-permute-done((bf16[8,3712]{1,0:T(8,128)(2,1)S(1)}, bf16[8,3712]{1,0:T(8,128)(2,1)S(1)}, u32[]{:S(2)}, u32[]{:S(2)}) %collective-permute-start.1) | collective-permute-done | bytes 59424 | tf_op jit(solution)/shard_map/ppermute | solution.py:27
  11.4 0.4 collective-permute-done.2
  11.8 1.5 %collective-permute-start.4 = (bf16[32,1024]{1,0:T(8,128)(2,1)S(1)}, bf16[32,1024]{1,0:T(8,128)(2,1)S(1)}, u32[]{:S(2)}, u32[]{:S(2)}) collective-permute-start(bf16[32,1024]{1,0:T(8,128)(2,1)S(1)} %pad_maximum_fusion.2), channel_id=1, source_target_pairs={{0,2},{1,3},{2,0},{3,1},{4,6},{5,7},{6,4},{7,5},{8,10},{9,11},{10,... | collective-permute-start | bytes 196616 | tf_op jit(solution)/shard_map/ppermute | solution.py:32
  13.4 0.6 collective-permute-start.3
  14.0 2.3 %copy-done = bf16[896,2560]{1,0:T(8,128)(2,1)S(1)} copy-done((bf16[896,2560]{1,0:T(8,128)(2,1)S(1)}, bf16[896,2560]{1,0:T(8,128)(2,1)}, u32[]{:S(2)}) %copy-start) | copy-done | bytes 4587544
  16.3 0.5 load.2.up_ref
  16.8 0.1 collective-permute-done.4
  16.9 0.5 collective-permute-start.6
  17.4 0.7 collective-permute-done.5.refs_2_
  18.2 0.2 collective-permute-done.6.refs_3_
  18.3 0.3 copy-done.1
  18.6 1.8 %shared_in.1 = (bf16[2,32,2560]{2,1,0:T(8,128)(2,1)S(1)}, bf16[2,32,2560]{2,1,0:T(8,128)(2,1)S(1)}, bf16[2,32,2560]{2,1,0:T(8,128)(2,1)S(1)}, bf16[2,32,2560]{2,1,0:T(8,128)(2,1)S(1)}) custom-call(bf16[896,2560]{1,0:T(8,128)(2,1)S(1)} %copy-done.1, bf16[896,2560]{1,0:T(8,128)(2,1)S(1)} %load.2.up_ref, bf16[32,896]{1,0:T(8,128)(2,1)S(1)} %slice.68.refs_0_, ...), custom_call_target="tpu_custom_call" | custom-call | flops 1174405120 | bytes 1310720 | tf_op jit(solution)/shard_map/shared_in/pallas_call | solution.py:118
  20.5 0.2 collective-permute-start.7
  20.7 1.8 %collective-permute-start.10 = (bf16[2,32,2560]{2,1,0:T(8,128)(2,1)S(1)}, bf16[2,32,2560]{2,1,0:T(8,128)(2,1)S(1)}, u32[]{:S(2)}, u32[]{:S(2)}) collective-permute-start(bf16[2,32,2560]{2,1,0:T(8,128)(2,1)S(1)} %get-tuple-element.45), channel_id=1, source_target_pairs={{0,4},{4,8},{8,12},{12,0},{1,5},{5,9},{9,13},{13,1},{2,6},{6,10},{... | collective-permute-start | bytes 983048 | tf_op jit(solution)/shard_map/ppermute | solution.py:27
  22.5 2.1 %collective-permute-start.8 = (bf16[2,32,2560]{2,1,0:T(8,128)(2,1)S(1)}, bf16[2,32,2560]{2,1,0:T(8,128)(2,1)S(1)}, u32[]{:S(2)}, u32[]{:S(2)}) collective-permute-start(bf16[2,32,2560]{2,1,0:T(8,128)(2,1)S(1)} %get-tuple-element.43), channel_id=1, source_target_pairs={{0,12},{4,0},{8,4},{12,8},{1,13},{5,1},{9,5},{13,9},{2,14},{6,2},{... | collective-permute-start | bytes 983048 | tf_op jit(solution)/shard_map/ppermute | solution.py:27
  24.5 0.1 pad_maximum_fusion.x_ref
  24.6 28.6 %experts.1 = (f32[128,128]{1,0:T(8,128)S(1)}, f32[64,3584]{1,0:T(8,128)S(1)}, bf16[64,3584]{1,0:T(8,128)(2,1)S(1)}) custom-call(s32[1]{0:T(128)} %bitcast.first_ref, bf16[128,3712]{1,0:T(8,128)(2,1)S(1)} %pad_maximum_fusion.x_ref, f32[1,3584]{1,0:T(1,128)S(1)} %reshape.7.scale_ref, bf16[8,3584,512]{2,1,0:T(8,128)(2,1)} %gate_ref.3, ...), custom_call_target="tpu_custom_call" | custom-call | flops 11274289152 | bytes 88080384 | tf_op jit(solution)/shard_map/experts/pallas_call | solution.py:207
  53.3 0.0 collective-permute-done.9
  53.3 0.1 collective-permute-start.14
  53.4 0.2 convert_add_fusion.1
  53.5 0.1 fusion.1.refs_0_
  53.6 1.6 %collective-permute-start.11 = (bf16[32,2560]{1,0:T(8,128)(2,1)S(1)}, bf16[32,2560]{1,0:T(8,128)(2,1)S(1)}, u32[]{:S(2)}, u32[]{:S(2)}) collective-permute-start(bf16[32,2560]{1,0:T(8,128)(2,1)S(1)} %fusion.1.refs_0_), channel_id=1, source_target_pairs={{0,4},{4,8},{8,12},{12,0},{1,5},{5,9},{9,13},{13,1},{2,6},{6,10},{... | collective-permute-start | bytes 491528 | tf_op jit(solution)/shard_map/ppermute | solution.py:27
  55.3 1.4 %collective-permute-start.12 = (bf16[32,2560]{1,0:T(8,128)(2,1)S(1)}, bf16[32,2560]{1,0:T(8,128)(2,1)S(1)}, u32[]{:S(2)}, u32[]{:S(2)}) collective-permute-start(bf16[32,2560]{1,0:T(8,128)(2,1)S(1)} %fusion.1.refs_0_), channel_id=1, source_target_pairs={{0,8},{4,12},{8,0},{12,4},{1,9},{5,13},{9,1},{13,5},{2,10},{6,14},... | collective-permute-start | bytes 491528 | tf_op jit(solution)/shard_map/ppermute | solution.py:27
  56.7 2.8 %collective-permute-start.13 = (bf16[32,2560]{1,0:T(8,128)(2,1)S(1)}, bf16[32,2560]{1,0:T(8,128)(2,1)S(1)}, u32[]{:S(2)}, u32[]{:S(2)}) collective-permute-start(bf16[32,2560]{1,0:T(8,128)(2,1)S(1)} %fusion.1.refs_0_), channel_id=1, source_target_pairs={{0,12},{4,0},{8,4},{12,8},{1,13},{5,1},{9,5},{13,9},{2,14},{6,2},{... | collective-permute-start | bytes 491528 | tf_op jit(solution)/shard_map/ppermute | solution.py:27
  59.5 0.1 fusion.7
  59.7 1.5 %collective-permute-start.15 = (bf16[32,1792]{1,0:T(8,128)(2,1)S(1)}, bf16[32,1792]{1,0:T(8,128)(2,1)S(1)}, u32[]{:S(2)}, u32[]{:S(2)}) collective-permute-start(bf16[32,1792]{1,0:T(8,128)(2,1)S(1)} %get-tuple-element.70), channel_id=1, source_target_pairs={{0,2},{1,3},{2,0},{3,1},{4,6},{5,7},{6,4},{7,5},{8,10},{9,11},{10,... | collective-permute-start | bytes 344072 | tf_op jit(solution)/shard_map/ppermute | solution.py:32
  61.2 0.6 collective-permute-start.16
  61.8 2.3 %copy-done.2 = bf16[2560,896]{1,0:T(8,128)(2,1)S(1)} copy-done((bf16[2560,896]{1,0:T(8,128)(2,1)S(1)}, bf16[2560,896]{1,0:T(8,128)(2,1)}, u32[]{:S(2)}) %copy-start.2) | copy-done | bytes 4587544
  64.1 0.5 load.3.down_ref
  64.6 4.6 %collective-permute-done.12.refs_2_ = bf16[32,2560]{1,0:T(8,128)(2,1)S(1)} collective-permute-done((bf16[32,2560]{1,0:T(8,128)(2,1)S(1)}, bf16[32,2560]{1,0:T(8,128)(2,1)S(1)}, u32[]{:S(2)}, u32[]{:S(2)}) %collective-permute-start.12) | collective-permute-done | bytes 163872 | tf_op jit(solution)/shard_map/ppermute | solution.py:27
  69.2 0.9 shared_out.1
  70.1 0.1 collective-permute-start.17
  70.3 1.3 %collective-permute-done.17 = bf16[64,896]{1,0:T(8,128)(2,1)S(1)} collective-permute-done((bf16[64,896]{1,0:T(8,128)(2,1)S(1)}, bf16[64,896]{1,0:T(8,128)(2,1)S(1)}, u32[]{:S(2)}, u32[]{:S(2)}) %collective-permute-start.17) | collective-permute-done | bytes 114720 | tf_op jit(solution)/shard_map/ppermute | solution.py:37
  71.6 1.5 %collective-permute-start.18 = (bf16[32,896]{1,0:T(8,128)(2,1)S(1)}, bf16[32,896]{1,0:T(8,128)(2,1)S(1)}, u32[]{:S(2)}, u32[]{:S(2)}) collective-permute-start(bf16[32,896]{1,0:T(8,128)(2,1)S(1)} %slice.121), channel_id=1, source_target_pairs={{0,2},{1,3},{2,0},{3,1},{4,6},{5,7},{6,4},{7,5},{8,10},{9,11},{10,... | collective-permute-start | bytes 172040 | tf_op jit(solution)/shard_map/ppermute | solution.py:32
  73.1 2.7 %collective-permute-done.18 = bf16[32,896]{1,0:T(8,128)(2,1)S(1)} collective-permute-done((bf16[32,896]{1,0:T(8,128)(2,1)S(1)}, bf16[32,896]{1,0:T(8,128)(2,1)S(1)}, u32[]{:S(2)}, u32[]{:S(2)}) %collective-permute-start.18) | collective-permute-done | bytes 57376 | tf_op jit(solution)/shard_map/ppermute | solution.py:32
  75.9 5.5 %collective-permute-start.19 = (bf16[8,3584]{1,0:T(8,128)(2,1)S(1)}, bf16[8,3584]{1,0:T(8,128)(2,1)S(1)}, u32[]{:S(2)}, u32[]{:S(2)}) collective-permute-start(bf16[8,3584]{1,0:T(8,128)(2,1)S(1)} %get-tuple-element.71), channel_id=1, source_target_pairs={{0,12},{4,0},{8,4},{12,8},{1,13},{5,1},{9,5},{13,9},{2,14},{6,2},{... | collective-permute-start | bytes 172040 | tf_op jit(solution)/shard_map/ppermute | solution.py:27
  81.4 0.0 collective-permute-start.20
  81.4 0.6 collective-permute-start.21
  82.0 1.2 %collective-permute-done.19 = bf16[8,3584]{1,0:T(8,128)(2,1)S(1)} collective-permute-done((bf16[8,3584]{1,0:T(8,128)(2,1)S(1)}, bf16[8,3584]{1,0:T(8,128)(2,1)S(1)}, u32[]{:S(2)}, u32[]{:S(2)}) %collective-permute-start.19) | collective-permute-done | bytes 57376 | tf_op jit(solution)/shard_map/ppermute | solution.py:27
  83.2 3.2 %collective-permute-done.20 = bf16[8,3584]{1,0:T(8,128)(2,1)S(1)} collective-permute-done((bf16[8,3584]{1,0:T(8,128)(2,1)S(1)}, bf16[8,3584]{1,0:T(8,128)(2,1)S(1)}, u32[]{:S(2)}, u32[]{:S(2)}) %collective-permute-start.20) | collective-permute-done | bytes 57376 | tf_op jit(solution)/shard_map/ppermute | solution.py:27
  86.5 0.9 %collective-permute-done.21 = bf16[8,3584]{1,0:T(8,128)(2,1)S(1)} collective-permute-done((bf16[8,3584]{1,0:T(8,128)(2,1)S(1)}, bf16[8,3584]{1,0:T(8,128)(2,1)S(1)}, u32[]{:S(2)}, u32[]{:S(2)}) %collective-permute-start.21) | collective-permute-done | bytes 57376 | tf_op jit(solution)/shard_map/ppermute | solution.py:27
  87.4 0.7 fusion.4
  (37 shorter events, 0.4 us)
Async XLA Ops:
  1.6 7.4 %collective-permute-start = (bf16[8,3712]{1,0:T(8,128)(2,1)S(1)}, bf16[8,3712]{1,0:T(8,128)(2,1)S(1)}, u32[]{:S(2)}, u32[]{:S(2)}) collective-permute-start(bf16[8,3712]{1,0:T(8,128)(2,1)S(1)} %concatenate.25), channel_id=1, source_target_pairs={{0,4},{4,8},{8,12},{12,0},{1,5},{5,9},{9,13},{13,1},{2,6},{6,10},{... | collective-permute-start | bytes 178184 | tf_op jit(solution)/shard_map/ppermute | solution.py:27
  4.6 6.7 %collective-permute-start.1 = (bf16[8,3712]{1,0:T(8,128)(2,1)S(1)}, bf16[8,3712]{1,0:T(8,128)(2,1)S(1)}, u32[]{:S(2)}, u32[]{:S(2)}) collective-permute-start(bf16[8,3712]{1,0:T(8,128)(2,1)S(1)} %concatenate.25), channel_id=1, source_target_pairs={{0,8},{4,12},{8,0},{12,4},{1,9},{5,13},{9,1},{13,5},{2,10},{6,14},... | collective-permute-start | bytes 178184 | tf_op jit(solution)/shard_map/ppermute | solution.py:27
  7.2 4.5 %collective-permute-start.2 = (bf16[8,3712]{1,0:T(8,128)(2,1)S(1)}, bf16[8,3712]{1,0:T(8,128)(2,1)S(1)}, u32[]{:S(2)}, u32[]{:S(2)}) collective-permute-start(bf16[8,3712]{1,0:T(8,128)(2,1)S(1)} %concatenate.25), channel_id=1, source_target_pairs={{0,12},{4,0},{8,4},{12,8},{1,13},{5,1},{9,5},{13,9},{2,14},{6,2},{... | collective-permute-start | bytes 178184 | tf_op jit(solution)/shard_map/ppermute | solution.py:27
  11.8 5.1 %collective-permute-start.4 = (bf16[32,1024]{1,0:T(8,128)(2,1)S(1)}, bf16[32,1024]{1,0:T(8,128)(2,1)S(1)}, u32[]{:S(2)}, u32[]{:S(2)}) collective-permute-start(bf16[32,1024]{1,0:T(8,128)(2,1)S(1)} %pad_maximum_fusion.2), channel_id=1, source_target_pairs={{0,2},{1,3},{2,0},{3,1},{4,6},{5,7},{6,4},{7,5},{8,10},{9,11},{10,... | collective-permute-start | bytes 196616 | tf_op jit(solution)/shard_map/ppermute | solution.py:32
  13.4 7.1 %collective-permute-start.3 = (bf16[32,3584]{1,0:T(8,128)(2,1)S(1)}, bf16[32,3584]{1,0:T(8,128)(2,1)S(1)}, u32[]{:S(2)}, u32[]{:S(2)}) collective-permute-start(bf16[32,3584]{1,0:T(8,128)(2,1)S(1)} %slice.84), channel_id=1, source_target_pairs={{0,2},{1,3},{2,0},{3,1},{4,6},{5,7},{6,4},{7,5},{8,10},{9,11},{10,... | collective-permute-start | bytes 688136 | tf_op jit(solution)/shard_map/ppermute | solution.py:32
  14.0 2.3 %copy-start = (bf16[896,2560]{1,0:T(8,128)(2,1)S(1)}, bf16[896,2560]{1,0:T(8,128)(2,1)}, u32[]{:S(2)}) copy-start(bf16[896,2560]{1,0:T(8,128)(2,1)} %refs_0_.1) | copy-start | bytes 13762564
  16.3 2.3 %copy-start.1 = (bf16[896,2560]{1,0:T(8,128)(2,1)S(1)}, bf16[896,2560]{1,0:T(8,128)(2,1)}, u32[]{:S(2)}) copy-start(bf16[896,2560]{1,0:T(8,128)(2,1)} %gate_ref.2) | copy-start | bytes 13762564
  16.9 1.2 %collective-permute-start.5 = (bf16[32,896]{1,0:T(8,128)(2,1)S(1)}, bf16[32,896]{1,0:T(8,128)(2,1)S(1)}, u32[]{:S(2)}, u32[]{:S(2)}) collective-permute-start(bf16[32,896]{1,0:T(8,128)(2,1)S(1)} %slice.68.refs_0_), channel_id=1, source_target_pairs={{0,1},{1,0},{2,3},{3,2},{4,5},{5,4},{6,7},{7,6},{8,9},{9,8},{10,11... | collective-permute-start | bytes 172040 | tf_op jit(solution)/shard_map/ppermute | solution.py:37
  16.9 1.4 %collective-permute-start.6 = (bf16[32,896]{1,0:T(8,128)(2,1)S(1)}, bf16[32,896]{1,0:T(8,128)(2,1)S(1)}, u32[]{:S(2)}, u32[]{:S(2)}) collective-permute-start(bf16[32,896]{1,0:T(8,128)(2,1)S(1)} %slice.69.refs_1_), channel_id=1, source_target_pairs={{0,1},{1,0},{2,3},{3,2},{4,5},{5,4},{6,7},{7,6},{8,9},{9,8},{10,11... | collective-permute-start | bytes 172040 | tf_op jit(solution)/shard_map/ppermute | solution.py:37
  17.4 3.2 %copy-start.3 = (f32[3584]{0:T(1024)S(1)}, f32[3584]{0:T(1024)}, u32[]{:S(2)}) copy-start(f32[3584]{0:T(1024)} %param.19) | copy-start | bytes 43012
  20.5 4.1 %collective-permute-start.7 = (bf16[64,3712]{1,0:T(8,128)(2,1)S(1)}, bf16[64,3712]{1,0:T(8,128)(2,1)S(1)}, u32[]{:S(2)}, u32[]{:S(2)}) collective-permute-start(bf16[64,3712]{1,0:T(8,128)(2,1)S(1)} %maximum_maximum_fusion), channel_id=1, source_target_pairs={{0,1},{1,0},{2,3},{3,2},{4,5},{5,4},{6,7},{7,6},{8,9},{9,8},{10,11... | collective-permute-start | bytes 1425416 | tf_op jit(solution)/shard_map/ppermute | solution.py:37
  20.7 32.6 %collective-permute-start.10 = (bf16[2,32,2560]{2,1,0:T(8,128)(2,1)S(1)}, bf16[2,32,2560]{2,1,0:T(8,128)(2,1)S(1)}, u32[]{:S(2)}, u32[]{:S(2)}) collective-permute-start(bf16[2,32,2560]{2,1,0:T(8,128)(2,1)S(1)} %get-tuple-element.45), channel_id=1, source_target_pairs={{0,4},{4,8},{8,12},{12,0},{1,5},{5,9},{9,13},{13,1},{2,6},{6,10},{... | collective-permute-start | bytes 983048 | tf_op jit(solution)/shard_map/ppermute | solution.py:27
  22.5 30.8 %collective-permute-start.8 = (bf16[2,32,2560]{2,1,0:T(8,128)(2,1)S(1)}, bf16[2,32,2560]{2,1,0:T(8,128)(2,1)S(1)}, u32[]{:S(2)}, u32[]{:S(2)}) collective-permute-start(bf16[2,32,2560]{2,1,0:T(8,128)(2,1)S(1)} %get-tuple-element.43), channel_id=1, source_target_pairs={{0,12},{4,0},{8,4},{12,8},{1,13},{5,1},{9,5},{13,9},{2,14},{6,2},{... | collective-permute-start | bytes 983048 | tf_op jit(solution)/shard_map/ppermute | solution.py:27
  24.5 28.8 %collective-permute-start.9 = (bf16[2,32,2560]{2,1,0:T(8,128)(2,1)S(1)}, bf16[2,32,2560]{2,1,0:T(8,128)(2,1)S(1)}, u32[]{:S(2)}, u32[]{:S(2)}) collective-permute-start(bf16[2,32,2560]{2,1,0:T(8,128)(2,1)S(1)} %get-tuple-element.44), channel_id=1, source_target_pairs={{0,8},{4,12},{8,0},{12,4},{1,9},{5,13},{9,1},{13,5},{2,10},{6,14},... | collective-permute-start | bytes 983048 | tf_op jit(solution)/shard_map/ppermute | solution.py:27
  53.3 6.2 %collective-permute-start.14 = (bf16[64,3584]{1,0:T(8,128)(2,1)S(1)}, bf16[64,3584]{1,0:T(8,128)(2,1)S(1)}, u32[]{:S(2)}, u32[]{:S(2)}) collective-permute-start(bf16[64,3584]{1,0:T(8,128)(2,1)S(1)} %get-tuple-element.60), channel_id=1, source_target_pairs={{0,1},{1,0},{2,3},{3,2},{4,5},{5,4},{6,7},{7,6},{8,9},{9,8},{10,11... | collective-permute-start | bytes 1376264 | tf_op jit(solution)/shard_map/ppermute | solution.py:37
  53.6 10.9 %collective-permute-start.11 = (bf16[32,2560]{1,0:T(8,128)(2,1)S(1)}, bf16[32,2560]{1,0:T(8,128)(2,1)S(1)}, u32[]{:S(2)}, u32[]{:S(2)}) collective-permute-start(bf16[32,2560]{1,0:T(8,128)(2,1)S(1)} %fusion.1.refs_0_), channel_id=1, source_target_pairs={{0,4},{4,8},{8,12},{12,0},{1,5},{5,9},{9,13},{13,1},{2,6},{6,10},{... | collective-permute-start | bytes 491528 | tf_op jit(solution)/shard_map/ppermute | solution.py:27
  55.3 14.0 %collective-permute-start.12 = (bf16[32,2560]{1,0:T(8,128)(2,1)S(1)}, bf16[32,2560]{1,0:T(8,128)(2,1)S(1)}, u32[]{:S(2)}, u32[]{:S(2)}) collective-permute-start(bf16[32,2560]{1,0:T(8,128)(2,1)S(1)} %fusion.1.refs_0_), channel_id=1, source_target_pairs={{0,8},{4,12},{8,0},{12,4},{1,9},{5,13},{9,1},{13,5},{2,10},{6,14},... | collective-permute-start | bytes 491528 | tf_op jit(solution)/shard_map/ppermute | solution.py:27
  56.7 12.5 %collective-permute-start.13 = (bf16[32,2560]{1,0:T(8,128)(2,1)S(1)}, bf16[32,2560]{1,0:T(8,128)(2,1)S(1)}, u32[]{:S(2)}, u32[]{:S(2)}) collective-permute-start(bf16[32,2560]{1,0:T(8,128)(2,1)S(1)} %fusion.1.refs_0_), channel_id=1, source_target_pairs={{0,12},{4,0},{8,4},{12,8},{1,13},{5,1},{9,5},{13,9},{2,14},{6,2},{... | collective-permute-start | bytes 491528 | tf_op jit(solution)/shard_map/ppermute | solution.py:27
  59.7 10.4 %collective-permute-start.15 = (bf16[32,1792]{1,0:T(8,128)(2,1)S(1)}, bf16[32,1792]{1,0:T(8,128)(2,1)S(1)}, u32[]{:S(2)}, u32[]{:S(2)}) collective-permute-start(bf16[32,1792]{1,0:T(8,128)(2,1)S(1)} %get-tuple-element.70), channel_id=1, source_target_pairs={{0,2},{1,3},{2,0},{3,1},{4,6},{5,7},{6,4},{7,5},{8,10},{9,11},{10,... | collective-permute-start | bytes 344072 | tf_op jit(solution)/shard_map/ppermute | solution.py:32
  61.2 8.9 %collective-permute-start.16 = (bf16[32,1792]{1,0:T(8,128)(2,1)S(1)}, bf16[32,1792]{1,0:T(8,128)(2,1)S(1)}, u32[]{:S(2)}, u32[]{:S(2)}) collective-permute-start(bf16[32,1792]{1,0:T(8,128)(2,1)S(1)} %get-tuple-element.69), channel_id=1, source_target_pairs={{0,2},{1,3},{2,0},{3,1},{4,6},{5,7},{6,4},{7,5},{8,10},{9,11},{10,... | collective-permute-start | bytes 344072 | tf_op jit(solution)/shard_map/ppermute | solution.py:32
  61.8 2.3 %copy-start.2 = (bf16[2560,896]{1,0:T(8,128)(2,1)S(1)}, bf16[2560,896]{1,0:T(8,128)(2,1)}, u32[]{:S(2)}) copy-start(bf16[2560,896]{1,0:T(8,128)(2,1)} %refs_0_.2) | copy-start | bytes 13762564
  70.1 1.4 %collective-permute-start.17 = (bf16[64,896]{1,0:T(8,128)(2,1)S(1)}, bf16[64,896]{1,0:T(8,128)(2,1)S(1)}, u32[]{:S(2)}, u32[]{:S(2)}) collective-permute-start(bf16[64,896]{1,0:T(8,128)(2,1)S(1)} %get-tuple-element.64), channel_id=1, source_target_pairs={{0,1},{1,0},{2,3},{3,2},{4,5},{5,4},{6,7},{7,6},{8,9},{9,8},{10,11... | collective-permute-start | bytes 344072 | tf_op jit(solution)/shard_map/ppermute | solution.py:37
  71.6 4.2 %collective-permute-start.18 = (bf16[32,896]{1,0:T(8,128)(2,1)S(1)}, bf16[32,896]{1,0:T(8,128)(2,1)S(1)}, u32[]{:S(2)}, u32[]{:S(2)}) collective-permute-start(bf16[32,896]{1,0:T(8,128)(2,1)S(1)} %slice.121), channel_id=1, source_target_pairs={{0,2},{1,3},{2,0},{3,1},{4,6},{5,7},{6,4},{7,5},{8,10},{9,11},{10,... | collective-permute-start | bytes 172040 | tf_op jit(solution)/shard_map/ppermute | solution.py:32
  75.9 7.3 %collective-permute-start.19 = (bf16[8,3584]{1,0:T(8,128)(2,1)S(1)}, bf16[8,3584]{1,0:T(8,128)(2,1)S(1)}, u32[]{:S(2)}, u32[]{:S(2)}) collective-permute-start(bf16[8,3584]{1,0:T(8,128)(2,1)S(1)} %get-tuple-element.71), channel_id=1, source_target_pairs={{0,12},{4,0},{8,4},{12,8},{1,13},{5,1},{9,5},{13,9},{2,14},{6,2},{... | collective-permute-start | bytes 172040 | tf_op jit(solution)/shard_map/ppermute | solution.py:27
  81.4 5.1 %collective-permute-start.20 = (bf16[8,3584]{1,0:T(8,128)(2,1)S(1)}, bf16[8,3584]{1,0:T(8,128)(2,1)S(1)}, u32[]{:S(2)}, u32[]{:S(2)}) collective-permute-start(bf16[8,3584]{1,0:T(8,128)(2,1)S(1)} %get-tuple-element.73), channel_id=1, source_target_pairs={{0,8},{4,12},{8,0},{12,4},{1,9},{5,13},{9,1},{13,5},{2,10},{6,14},... | collective-permute-start | bytes 172040 | tf_op jit(solution)/shard_map/ppermute | solution.py:27
  81.4 6.0 %collective-permute-start.21 = (bf16[8,3584]{1,0:T(8,128)(2,1)S(1)}, bf16[8,3584]{1,0:T(8,128)(2,1)S(1)}, u32[]{:S(2)}, u32[]{:S(2)}) collective-permute-start(bf16[8,3584]{1,0:T(8,128)(2,1)S(1)} %get-tuple-element.72), channel_id=1, source_target_pairs={{0,4},{4,8},{8,12},{12,0},{1,5},{5,9},{9,13},{13,1},{2,6},{6,10},{... | collective-permute-start | bytes 172040 | tf_op jit(solution)/shard_map/ppermute | solution.py:27

commit v6 on v5

--- a/solution.py
+++ b/solution.py
@@ -201,7 +201,7 @@
     whole = pl.BlockSpec(memory_space=pltpu.VMEM)
     apart = pl.BlockSpec(memory_space=pl.ANY)
     slots = min(3, local)
-    width = chunk_of(feat, 256)
+    width = chunk_of(feat, 512)
     down_slots = (feat // width + 1) // 2
     buffer = pltpu.VMEM((slots, feat, hidden), gate.dtype)
     return pl.pallas_call(

time: 88.4 us -> 87.5 us (0.990)
  waiting for transfers between devices: 18.2 us -> 21.1 us
  starting transfers between devices: 29.4 us -> 27.1 us
  Pallas kernels: 32.3 us -> 30.9 us
    ppermute x12, waiting for transfers between devices: 13.2 us -> 16.1 us  [z_shift(): lax.ppermute(value, 'expert', [(i, (i + step) % spread) for i in range(sp...]
    ppermute x12, starting transfers between devices: 22.9 us -> 20.5 us  [z_shift(): lax.ppermute(value, 'expert', [(i, (i + step) % spread) for i in range(sp...]
    pallas_call x1, Pallas kernels: 28.6 us -> 27.3 us  [experts(): pl.pallas_call(functools.partial(experts_kernel, chosen), in_specs=[pl.Bl...]
  transfers between devices with their start and end apart: 22 -> 22, of which waited for: 12 -> 13; matrix products, arithmetic and copies ran while one was open for 1% -> 1% of each run, Pallas kernels for 37% -> 35%
where the time goes in v6:
time: 87.5 us; the launch traced here: 87.2 us
  Pallas kernels  30.9 us (35%)
  starting transfers between devices  27.1 us (31%)
  waiting for transfers between devices  21.1 us (24%)
  local copies, waits for them, and re-layouts  5.92 us (7%)
  other arithmetic  1.95 us (2%)
    pallas_call x1, Pallas kernels, experts(): pl.pallas_call(functools.partial(experts_kernel, chosen), in_specs=[pl.Bl...  27.3 us
    ppermute x12, starting transfers between devices, z_shift(): lax.ppermute(value, 'expert', [(i, (i + step) % spread) for i in range(sp...  20.5 us
    ppermute x12, waiting for transfers between devices, z_shift(): lax.ppermute(value, 'expert', [(i, (i + step) % spread) for i in range(sp...  16.1 us
    ppermute x5, starting transfers between devices, x_shift(): lax.ppermute(value, 'narrow', [(i, (i + 2 * step) % size) for i in range(...  5.83 us
    unnamed x9, local copies, waits for them, and re-layouts  4.89 us
    ppermute x5, waiting for transfers between devices, x_shift(): lax.ppermute(value, 'narrow', [(i, (i + 2 * step) % size) for i in range(...  2.78 us
    ppermute x5, waiting for transfers between devices, core_swap(): return lax.ppermute(value, 'narrow', [(i, i ^ 1) for i in range(size)])  2.16 us
    pallas_call x1, Pallas kernels, shared_in(): pl.pallas_call(functools.partial(shared_in_kernel, (outer, spread, rows),...  1.84 us
  transfers between devices with their start and end apart: 22, of which 13 were waited for; matrix products, arithmetic and copies ran while one was open for 1% of the time, Pallas kernels for 35%

profile of v6, /device:TPU:0, one launch (start us, length us, event | category | flops | bytes accessed | tf_op | source)
XLA Modules:
  0.0 87.2 jit_solution(5091698951018343961)
XLA Ops:
  0.0 0.7 convert_element_type.51
  0.7 0.9 %concatenate.25 = bf16[8,3712]{1,0:T(8,128)(2,1)S(1)} concatenate(bf16[8,3584]{1,0:T(8,128)(2,1)} %param.10, bf16[8,8]{1,0:T(8,128)(2,1)S(1)} %convert_element_type.51, bf16[8,8]{1,0:T(8,128)(2,1)} %param.12, bf16[8,112]{1,0:T(8,128)(2,1)S(1)} %broadcast_in_dim.3), dimensions={1} | concatenate | bytes 118784 | tf_op jit(solution)/shard_map/concatenate | solution.py:298
  1.6 3.0 %collective-permute-start = (bf16[8,3712]{1,0:T(8,128)(2,1)S(1)}, bf16[8,3712]{1,0:T(8,128)(2,1)S(1)}, u32[]{:S(2)}, u32[]{:S(2)}) collective-permute-start(bf16[8,3712]{1,0:T(8,128)(2,1)S(1)} %concatenate.25), channel_id=1, source_target_pairs={{0,4},{4,8},{8,12},{12,0},{1,5},{5,9},{9,13},{13,1},{2,6},{6,10},{... | collective-permute-start | bytes 178184 | tf_op jit(solution)/shard_map/ppermute | solution.py:27
  4.6 2.6 %collective-permute-start.1 = (bf16[8,3712]{1,0:T(8,128)(2,1)S(1)}, bf16[8,3712]{1,0:T(8,128)(2,1)S(1)}, u32[]{:S(2)}, u32[]{:S(2)}) collective-permute-start(bf16[8,3712]{1,0:T(8,128)(2,1)S(1)} %concatenate.25), channel_id=1, source_target_pairs={{0,8},{4,12},{8,0},{12,4},{1,9},{5,13},{9,1},{13,5},{2,10},{6,14},... | collective-permute-start | bytes 178184 | tf_op jit(solution)/shard_map/ppermute | solution.py:27
  7.2 1.3 %collective-permute-start.2 = (bf16[8,3712]{1,0:T(8,128)(2,1)S(1)}, bf16[8,3712]{1,0:T(8,128)(2,1)S(1)}, u32[]{:S(2)}, u32[]{:S(2)}) collective-permute-start(bf16[8,3712]{1,0:T(8,128)(2,1)S(1)} %concatenate.25), channel_id=1, source_target_pairs={{0,12},{4,0},{8,4},{12,8},{1,13},{5,1},{9,5},{13,9},{2,14},{6,2},{... | collective-permute-start | bytes 178184 | tf_op jit(solution)/shard_map/ppermute | solution.py:27
  8.6 0.5 collective-permute-done
  9.0 2.3 %collective-permute-done.1 = bf16[8,3712]{1,0:T(8,128)(2,1)S(1)} collective-permute-done((bf16[8,3712]{1,0:T(8,128)(2,1)S(1)}, bf16[8,3712]{1,0:T(8,128)(2,1)S(1)}, u32[]{:S(2)}, u32[]{:S(2)}) %collective-permute-start.1) | collective-permute-done | bytes 59424 | tf_op jit(solution)/shard_map/ppermute | solution.py:27
  11.4 0.4 collective-permute-done.2
  11.8 1.5 %collective-permute-start.4 = (bf16[32,1024]{1,0:T(8,128)(2,1)S(1)}, bf16[32,1024]{1,0:T(8,128)(2,1)S(1)}, u32[]{:S(2)}, u32[]{:S(2)}) collective-permute-start(bf16[32,1024]{1,0:T(8,128)(2,1)S(1)} %pad_maximum_fusion.2), channel_id=1, source_target_pairs={{0,2},{1,3},{2,0},{3,1},{4,6},{5,7},{6,4},{7,5},{8,10},{9,11},{10,... | collective-permute-start | bytes 196616 | tf_op jit(solution)/shard_map/ppermute | solution.py:32
  13.4 0.6 collective-permute-start.3
  14.0 2.3 %copy-done = bf16[896,2560]{1,0:T(8,128)(2,1)S(1)} copy-done((bf16[896,2560]{1,0:T(8,128)(2,1)S(1)}, bf16[896,2560]{1,0:T(8,128)(2,1)}, u32[]{:S(2)}) %copy-start) | copy-done | bytes 4587544
  16.3 0.5 load.2.up_ref
  16.8 0.1 collective-permute-done.4
  16.9 0.5 collective-permute-start.6
  17.4 0.0 copy-start.3
  17.4 0.7 collective-permute-done.5.refs_2_
  18.2 0.2 collective-permute-done.6.refs_3_
  18.3 0.3 copy-done.1
  18.6 1.8 %shared_in.1 = (bf16[2,32,2560]{2,1,0:T(8,128)(2,1)S(1)}, bf16[2,32,2560]{2,1,0:T(8,128)(2,1)S(1)}, bf16[2,32,2560]{2,1,0:T(8,128)(2,1)S(1)}, bf16[2,32,2560]{2,1,0:T(8,128)(2,1)S(1)}) custom-call(bf16[896,2560]{1,0:T(8,128)(2,1)S(1)} %copy-done.1, bf16[896,2560]{1,0:T(8,128)(2,1)S(1)} %load.2.up_ref, bf16[32,896]{1,0:T(8,128)(2,1)S(1)} %slice.68.refs_0_, ...), custom_call_target="tpu_custom_call" | custom-call | flops 1174405120 | bytes 1310720 | tf_op jit(solution)/shard_map/shared_in/pallas_call | solution.py:118
  20.5 0.2 collective-permute-start.7
  20.7 1.8 %collective-permute-start.10 = (bf16[2,32,2560]{2,1,0:T(8,128)(2,1)S(1)}, bf16[2,32,2560]{2,1,0:T(8,128)(2,1)S(1)}, u32[]{:S(2)}, u32[]{:S(2)}) collective-permute-start(bf16[2,32,2560]{2,1,0:T(8,128)(2,1)S(1)} %get-tuple-element.45), channel_id=1, source_target_pairs={{0,4},{4,8},{8,12},{12,0},{1,5},{5,9},{9,13},{13,1},{2,6},{6,10},{... | collective-permute-start | bytes 983048 | tf_op jit(solution)/shard_map/ppermute | solution.py:27
  22.5 2.1 %collective-permute-start.8 = (bf16[2,32,2560]{2,1,0:T(8,128)(2,1)S(1)}, bf16[2,32,2560]{2,1,0:T(8,128)(2,1)S(1)}, u32[]{:S(2)}, u32[]{:S(2)}) collective-permute-start(bf16[2,32,2560]{2,1,0:T(8,128)(2,1)S(1)} %get-tuple-element.43), channel_id=1, source_target_pairs={{0,12},{4,0},{8,4},{12,8},{1,13},{5,1},{9,5},{13,9},{2,14},{6,2},{... | collective-permute-start | bytes 983048 | tf_op jit(solution)/shard_map/ppermute | solution.py:27
  24.5 0.1 pad_maximum_fusion.x_ref
  24.6 27.3 %experts.1 = (f32[128,128]{1,0:T(8,128)S(1)}, f32[64,3584]{1,0:T(8,128)S(1)}, bf16[64,3584]{1,0:T(8,128)(2,1)S(1)}) custom-call(s32[1]{0:T(128)} %bitcast.first_ref, bf16[128,3712]{1,0:T(8,128)(2,1)S(1)} %pad_maximum_fusion.x_ref, f32[1,3584]{1,0:T(1,128)S(1)} %reshape.7.scale_ref, bf16[8,3584,512]{2,1,0:T(8,128)(2,1)} %gate_ref.3, ...), custom_call_target="tpu_custom_call" | custom-call | flops 11274289152 | bytes 88080384 | tf_op jit(solution)/shard_map/experts/pallas_call | solution.py:207
  51.9 1.4 %collective-permute-done.9 = bf16[2,32,2560]{2,1,0:T(8,128)(2,1)S(1)} collective-permute-done((bf16[2,32,2560]{2,1,0:T(8,128)(2,1)S(1)}, bf16[2,32,2560]{2,1,0:T(8,128)(2,1)S(1)}, u32[]{:S(2)}, u32[]{:S(2)}) %collective-permute-start.9) | collective-permute-done | bytes 327712 | tf_op jit(solution)/shard_map/ppermute | solution.py:27
  53.3 0.2 convert_add_fusion.1
  53.5 0.1 fusion.1.refs_0_
  53.6 0.3 collective-permute-start.11
  53.9 1.5 %collective-permute-start.12 = (bf16[32,2560]{1,0:T(8,128)(2,1)S(1)}, bf16[32,2560]{1,0:T(8,128)(2,1)S(1)}, u32[]{:S(2)}, u32[]{:S(2)}) collective-permute-start(bf16[32,2560]{1,0:T(8,128)(2,1)S(1)} %fusion.1.refs_0_), channel_id=1, source_target_pairs={{0,8},{4,12},{8,0},{12,4},{1,9},{5,13},{9,1},{13,5},{2,10},{6,14},... | collective-permute-start | bytes 491528 | tf_op jit(solution)/shard_map/ppermute | solution.py:27
  55.3 2.8 %collective-permute-start.13 = (bf16[32,2560]{1,0:T(8,128)(2,1)S(1)}, bf16[32,2560]{1,0:T(8,128)(2,1)S(1)}, u32[]{:S(2)}, u32[]{:S(2)}) collective-permute-start(bf16[32,2560]{1,0:T(8,128)(2,1)S(1)} %fusion.1.refs_0_), channel_id=1, source_target_pairs={{0,12},{4,0},{8,4},{12,8},{1,13},{5,1},{9,5},{13,9},{2,14},{6,2},{... | collective-permute-start | bytes 491528 | tf_op jit(solution)/shard_map/ppermute | solution.py:27
  58.2 0.1 fusion.7
  58.3 1.5 %collective-permute-start.15 = (bf16[32,1792]{1,0:T(8,128)(2,1)S(1)}, bf16[32,1792]{1,0:T(8,128)(2,1)S(1)}, u32[]{:S(2)}, u32[]{:S(2)}) collective-permute-start(bf16[32,1792]{1,0:T(8,128)(2,1)S(1)} %get-tuple-element.70), channel_id=1, source_target_pairs={{0,2},{1,3},{2,0},{3,1},{4,6},{5,7},{6,4},{7,5},{8,10},{9,11},{10,... | collective-permute-start | bytes 344072 | tf_op jit(solution)/shard_map/ppermute | solution.py:32
  59.8 0.6 collective-permute-start.16
  60.4 2.3 %copy-done.2 = bf16[2560,896]{1,0:T(8,128)(2,1)S(1)} copy-done((bf16[2560,896]{1,0:T(8,128)(2,1)S(1)}, bf16[2560,896]{1,0:T(8,128)(2,1)}, u32[]{:S(2)}) %copy-start.2) | copy-done | bytes 4587544
  62.7 0.5 load.3.down_ref
  63.2 5.7 %collective-permute-done.12.refs_2_ = bf16[32,2560]{1,0:T(8,128)(2,1)S(1)} collective-permute-done((bf16[32,2560]{1,0:T(8,128)(2,1)S(1)}, bf16[32,2560]{1,0:T(8,128)(2,1)S(1)}, u32[]{:S(2)}, u32[]{:S(2)}) %collective-permute-start.12) | collective-permute-done | bytes 163872 | tf_op jit(solution)/shard_map/ppermute | solution.py:27
  68.9 0.9 shared_out.1
  69.8 0.1 collective-permute-start.17
  69.9 1.3 %collective-permute-done.17 = bf16[64,896]{1,0:T(8,128)(2,1)S(1)} collective-permute-done((bf16[64,896]{1,0:T(8,128)(2,1)S(1)}, bf16[64,896]{1,0:T(8,128)(2,1)S(1)}, u32[]{:S(2)}, u32[]{:S(2)}) %collective-permute-start.17) | collective-permute-done | bytes 114720 | tf_op jit(solution)/shard_map/ppermute | solution.py:37
  71.2 1.6 %collective-permute-start.18 = (bf16[32,896]{1,0:T(8,128)(2,1)S(1)}, bf16[32,896]{1,0:T(8,128)(2,1)S(1)}, u32[]{:S(2)}, u32[]{:S(2)}) collective-permute-start(bf16[32,896]{1,0:T(8,128)(2,1)S(1)} %slice.121), channel_id=1, source_target_pairs={{0,2},{1,3},{2,0},{3,1},{4,6},{5,7},{6,4},{7,5},{8,10},{9,11},{10,... | collective-permute-start | bytes 172040 | tf_op jit(solution)/shard_map/ppermute | solution.py:32
  72.8 2.6 %collective-permute-done.18 = bf16[32,896]{1,0:T(8,128)(2,1)S(1)} collective-permute-done((bf16[32,896]{1,0:T(8,128)(2,1)S(1)}, bf16[32,896]{1,0:T(8,128)(2,1)S(1)}, u32[]{:S(2)}, u32[]{:S(2)}) %collective-permute-start.18) | collective-permute-done | bytes 57376 | tf_op jit(solution)/shard_map/ppermute | solution.py:32
  75.5 4.5 %collective-permute-start.19 = (bf16[8,3584]{1,0:T(8,128)(2,1)S(1)}, bf16[8,3584]{1,0:T(8,128)(2,1)S(1)}, u32[]{:S(2)}, u32[]{:S(2)}) collective-permute-start(bf16[8,3584]{1,0:T(8,128)(2,1)S(1)} %get-tuple-element.71), channel_id=1, source_target_pairs={{0,12},{4,0},{8,4},{12,8},{1,13},{5,1},{9,5},{13,9},{2,14},{6,2},{... | collective-permute-start | bytes 172040 | tf_op jit(solution)/shard_map/ppermute | solution.py:27
  80.0 0.5 collective-permute-start.20
  80.6 0.1 collective-permute-start.21
  80.7 1.2 %collective-permute-done.19 = bf16[8,3584]{1,0:T(8,128)(2,1)S(1)} collective-permute-done((bf16[8,3584]{1,0:T(8,128)(2,1)S(1)}, bf16[8,3584]{1,0:T(8,128)(2,1)S(1)}, u32[]{:S(2)}, u32[]{:S(2)}) %collective-permute-start.19) | collective-permute-done | bytes 57376 | tf_op jit(solution)/shard_map/ppermute | solution.py:27
  81.8 3.3 %collective-permute-done.20 = bf16[8,3584]{1,0:T(8,128)(2,1)S(1)} collective-permute-done((bf16[8,3584]{1,0:T(8,128)(2,1)S(1)}, bf16[8,3584]{1,0:T(8,128)(2,1)S(1)}, u32[]{:S(2)}, u32[]{:S(2)}) %collective-permute-start.20) | collective-permute-done | bytes 57376 | tf_op jit(solution)/shard_map/ppermute | solution.py:27
  85.2 1.4 %collective-permute-done.21 = bf16[8,3584]{1,0:T(8,128)(2,1)S(1)} collective-permute-done((bf16[8,3584]{1,0:T(8,128)(2,1)S(1)}, bf16[8,3584]{1,0:T(8,128)(2,1)S(1)}, u32[]{:S(2)}, u32[]{:S(2)}) %collective-permute-start.21) | collective-permute-done | bytes 57376 | tf_op jit(solution)/shard_map/ppermute | solution.py:27
  86.5 0.7 fusion.4
  (37 shorter events, 0.4 us)
Async XLA Ops:
  1.6 7.4 %collective-permute-start = (bf16[8,3712]{1,0:T(8,128)(2,1)S(1)}, bf16[8,3712]{1,0:T(8,128)(2,1)S(1)}, u32[]{:S(2)}, u32[]{:S(2)}) collective-permute-start(bf16[8,3712]{1,0:T(8,128)(2,1)S(1)} %concatenate.25), channel_id=1, source_target_pairs={{0,4},{4,8},{8,12},{12,0},{1,5},{5,9},{9,13},{13,1},{2,6},{6,10},{... | collective-permute-start | bytes 178184 | tf_op jit(solution)/shard_map/ppermute | solution.py:27
  4.6 6.7 %collective-permute-start.1 = (bf16[8,3712]{1,0:T(8,128)(2,1)S(1)}, bf16[8,3712]{1,0:T(8,128)(2,1)S(1)}, u32[]{:S(2)}, u32[]{:S(2)}) collective-permute-start(bf16[8,3712]{1,0:T(8,128)(2,1)S(1)} %concatenate.25), channel_id=1, source_target_pairs={{0,8},{4,12},{8,0},{12,4},{1,9},{5,13},{9,1},{13,5},{2,10},{6,14},... | collective-permute-start | bytes 178184 | tf_op jit(solution)/shard_map/ppermute | solution.py:27
  7.2 4.5 %collective-permute-start.2 = (bf16[8,3712]{1,0:T(8,128)(2,1)S(1)}, bf16[8,3712]{1,0:T(8,128)(2,1)S(1)}, u32[]{:S(2)}, u32[]{:S(2)}) collective-permute-start(bf16[8,3712]{1,0:T(8,128)(2,1)S(1)} %concatenate.25), channel_id=1, source_target_pairs={{0,12},{4,0},{8,4},{12,8},{1,13},{5,1},{9,5},{13,9},{2,14},{6,2},{... | collective-permute-start | bytes 178184 | tf_op jit(solution)/shard_map/ppermute | solution.py:27
  11.8 5.1 %collective-permute-start.4 = (bf16[32,1024]{1,0:T(8,128)(2,1)S(1)}, bf16[32,1024]{1,0:T(8,128)(2,1)S(1)}, u32[]{:S(2)}, u32[]{:S(2)}) collective-permute-start(bf16[32,1024]{1,0:T(8,128)(2,1)S(1)} %pad_maximum_fusion.2), channel_id=1, source_target_pairs={{0,2},{1,3},{2,0},{3,1},{4,6},{5,7},{6,4},{7,5},{8,10},{9,11},{10,... | collective-permute-start | bytes 196616 | tf_op jit(solution)/shard_map/ppermute | solution.py:32
  13.4 7.1 %collective-permute-start.3 = (bf16[32,3584]{1,0:T(8,128)(2,1)S(1)}, bf16[32,3584]{1,0:T(8,128)(2,1)S(1)}, u32[]{:S(2)}, u32[]{:S(2)}) collective-permute-start(bf16[32,3584]{1,0:T(8,128)(2,1)S(1)} %slice.84), channel_id=1, source_target_pairs={{0,2},{1,3},{2,0},{3,1},{4,6},{5,7},{6,4},{7,5},{8,10},{9,11},{10,... | collective-permute-start | bytes 688136 | tf_op jit(solution)/shard_map/ppermute | solution.py:32
  14.0 2.3 %copy-start = (bf16[896,2560]{1,0:T(8,128)(2,1)S(1)}, bf16[896,2560]{1,0:T(8,128)(2,1)}, u32[]{:S(2)}) copy-start(bf16[896,2560]{1,0:T(8,128)(2,1)} %refs_0_.1) | copy-start | bytes 13762564
  16.3 2.3 %copy-start.1 = (bf16[896,2560]{1,0:T(8,128)(2,1)S(1)}, bf16[896,2560]{1,0:T(8,128)(2,1)}, u32[]{:S(2)}) copy-start(bf16[896,2560]{1,0:T(8,128)(2,1)} %gate_ref.2) | copy-start | bytes 13762564
  16.9 1.2 %collective-permute-start.5 = (bf16[32,896]{1,0:T(8,128)(2,1)S(1)}, bf16[32,896]{1,0:T(8,128)(2,1)S(1)}, u32[]{:S(2)}, u32[]{:S(2)}) collective-permute-start(bf16[32,896]{1,0:T(8,128)(2,1)S(1)} %slice.68.refs_0_), channel_id=1, source_target_pairs={{0,1},{1,0},{2,3},{3,2},{4,5},{5,4},{6,7},{7,6},{8,9},{9,8},{10,11... | collective-permute-start | bytes 172040 | tf_op jit(solution)/shard_map/ppermute | solution.py:37
  16.9 1.4 %collective-permute-start.6 = (bf16[32,896]{1,0:T(8,128)(2,1)S(1)}, bf16[32,896]{1,0:T(8,128)(2,1)S(1)}, u32[]{:S(2)}, u32[]{:S(2)}) collective-permute-start(bf16[32,896]{1,0:T(8,128)(2,1)S(1)} %slice.69.refs_1_), channel_id=1, source_target_pairs={{0,1},{1,0},{2,3},{3,2},{4,5},{5,4},{6,7},{7,6},{8,9},{9,8},{10,11... | collective-permute-start | bytes 172040 | tf_op jit(solution)/shard_map/ppermute | solution.py:37
  17.4 3.2 %copy-start.3 = (f32[3584]{0:T(1024)S(1)}, f32[3584]{0:T(1024)}, u32[]{:S(2)}) copy-start(f32[3584]{0:T(1024)} %param.19) | copy-start | bytes 43012
  20.5 4.1 %collective-permute-start.7 = (bf16[64,3712]{1,0:T(8,128)(2,1)S(1)}, bf16[64,3712]{1,0:T(8,128)(2,1)S(1)}, u32[]{:S(2)}, u32[]{:S(2)}) collective-permute-start(bf16[64,3712]{1,0:T(8,128)(2,1)S(1)} %maximum_maximum_fusion), channel_id=1, source_target_pairs={{0,1},{1,0},{2,3},{3,2},{4,5},{5,4},{6,7},{7,6},{8,9},{9,8},{10,11... | collective-permute-start | bytes 1425416 | tf_op jit(solution)/shard_map/ppermute | solution.py:37
  20.7 31.2 %collective-permute-start.10 = (bf16[2,32,2560]{2,1,0:T(8,128)(2,1)S(1)}, bf16[2,32,2560]{2,1,0:T(8,128)(2,1)S(1)}, u32[]{:S(2)}, u32[]{:S(2)}) collective-permute-start(bf16[2,32,2560]{2,1,0:T(8,128)(2,1)S(1)} %get-tuple-element.45), channel_id=1, source_target_pairs={{0,4},{4,8},{8,12},{12,0},{1,5},{5,9},{9,13},{13,1},{2,6},{6,10},{... | collective-permute-start | bytes 983048 | tf_op jit(solution)/shard_map/ppermute | solution.py:27
  22.5 29.4 %collective-permute-start.8 = (bf16[2,32,2560]{2,1,0:T(8,128)(2,1)S(1)}, bf16[2,32,2560]{2,1,0:T(8,128)(2,1)S(1)}, u32[]{:S(2)}, u32[]{:S(2)}) collective-permute-start(bf16[2,32,2560]{2,1,0:T(8,128)(2,1)S(1)} %get-tuple-element.43), channel_id=1, source_target_pairs={{0,12},{4,0},{8,4},{12,8},{1,13},{5,1},{9,5},{13,9},{2,14},{6,2},{... | collective-permute-start | bytes 983048 | tf_op jit(solution)/shard_map/ppermute | solution.py:27
  24.5 28.8 %collective-permute-start.9 = (bf16[2,32,2560]{2,1,0:T(8,128)(2,1)S(1)}, bf16[2,32,2560]{2,1,0:T(8,128)(2,1)S(1)}, u32[]{:S(2)}, u32[]{:S(2)}) collective-permute-start(bf16[2,32,2560]{2,1,0:T(8,128)(2,1)S(1)} %get-tuple-element.44), channel_id=1, source_target_pairs={{0,8},{4,12},{8,0},{12,4},{1,9},{5,13},{9,1},{13,5},{2,10},{6,14},... | collective-permute-start | bytes 983048 | tf_op jit(solution)/shard_map/ppermute | solution.py:27
  53.3 4.9 %collective-permute-start.14 = (bf16[64,3584]{1,0:T(8,128)(2,1)S(1)}, bf16[64,3584]{1,0:T(8,128)(2,1)S(1)}, u32[]{:S(2)}, u32[]{:S(2)}) collective-permute-start(bf16[64,3584]{1,0:T(8,128)(2,1)S(1)} %get-tuple-element.60), channel_id=1, source_target_pairs={{0,1},{1,0},{2,3},{3,2},{4,5},{5,4},{6,7},{7,6},{8,9},{9,8},{10,11... | collective-permute-start | bytes 1376264 | tf_op jit(solution)/shard_map/ppermute | solution.py:37
  53.6 9.6 %collective-permute-start.11 = (bf16[32,2560]{1,0:T(8,128)(2,1)S(1)}, bf16[32,2560]{1,0:T(8,128)(2,1)S(1)}, u32[]{:S(2)}, u32[]{:S(2)}) collective-permute-start(bf16[32,2560]{1,0:T(8,128)(2,1)S(1)} %fusion.1.refs_0_), channel_id=1, source_target_pairs={{0,4},{4,8},{8,12},{12,0},{1,5},{5,9},{9,13},{13,1},{2,6},{6,10},{... | collective-permute-start | bytes 491528 | tf_op jit(solution)/shard_map/ppermute | solution.py:27
  53.9 15.0 %collective-permute-start.12 = (bf16[32,2560]{1,0:T(8,128)(2,1)S(1)}, bf16[32,2560]{1,0:T(8,128)(2,1)S(1)}, u32[]{:S(2)}, u32[]{:S(2)}) collective-permute-start(bf16[32,2560]{1,0:T(8,128)(2,1)S(1)} %fusion.1.refs_0_), channel_id=1, source_target_pairs={{0,8},{4,12},{8,0},{12,4},{1,9},{5,13},{9,1},{13,5},{2,10},{6,14},... | collective-permute-start | bytes 491528 | tf_op jit(solution)/shard_map/ppermute | solution.py:27
  55.3 13.5 %collective-permute-start.13 = (bf16[32,2560]{1,0:T(8,128)(2,1)S(1)}, bf16[32,2560]{1,0:T(8,128)(2,1)S(1)}, u32[]{:S(2)}, u32[]{:S(2)}) collective-permute-start(bf16[32,2560]{1,0:T(8,128)(2,1)S(1)} %fusion.1.refs_0_), channel_id=1, source_target_pairs={{0,12},{4,0},{8,4},{12,8},{1,13},{5,1},{9,5},{13,9},{2,14},{6,2},{... | collective-permute-start | bytes 491528 | tf_op jit(solution)/shard_map/ppermute | solution.py:27
  58.3 11.4 %collective-permute-start.15 = (bf16[32,1792]{1,0:T(8,128)(2,1)S(1)}, bf16[32,1792]{1,0:T(8,128)(2,1)S(1)}, u32[]{:S(2)}, u32[]{:S(2)}) collective-permute-start(bf16[32,1792]{1,0:T(8,128)(2,1)S(1)} %get-tuple-element.70), channel_id=1, source_target_pairs={{0,2},{1,3},{2,0},{3,1},{4,6},{5,7},{6,4},{7,5},{8,10},{9,11},{10,... | collective-permute-start | bytes 344072 | tf_op jit(solution)/shard_map/ppermute | solution.py:32
  59.8 9.9 %collective-permute-start.16 = (bf16[32,1792]{1,0:T(8,128)(2,1)S(1)}, bf16[32,1792]{1,0:T(8,128)(2,1)S(1)}, u32[]{:S(2)}, u32[]{:S(2)}) collective-permute-start(bf16[32,1792]{1,0:T(8,128)(2,1)S(1)} %get-tuple-element.69), channel_id=1, source_target_pairs={{0,2},{1,3},{2,0},{3,1},{4,6},{5,7},{6,4},{7,5},{8,10},{9,11},{10,... | collective-permute-start | bytes 344072 | tf_op jit(solution)/shard_map/ppermute | solution.py:32
  60.4 2.3 %copy-start.2 = (bf16[2560,896]{1,0:T(8,128)(2,1)S(1)}, bf16[2560,896]{1,0:T(8,128)(2,1)}, u32[]{:S(2)}) copy-start(bf16[2560,896]{1,0:T(8,128)(2,1)} %refs_0_.2) | copy-start | bytes 13762564
  69.8 1.4 %collective-permute-start.17 = (bf16[64,896]{1,0:T(8,128)(2,1)S(1)}, bf16[64,896]{1,0:T(8,128)(2,1)S(1)}, u32[]{:S(2)}, u32[]{:S(2)}) collective-permute-start(bf16[64,896]{1,0:T(8,128)(2,1)S(1)} %get-tuple-element.64), channel_id=1, source_target_pairs={{0,1},{1,0},{2,3},{3,2},{4,5},{5,4},{6,7},{7,6},{8,9},{9,8},{10,11... | collective-permute-start | bytes 344072 | tf_op jit(solution)/shard_map/ppermute | solution.py:37
  71.2 4.2 %collective-permute-start.18 = (bf16[32,896]{1,0:T(8,128)(2,1)S(1)}, bf16[32,896]{1,0:T(8,128)(2,1)S(1)}, u32[]{:S(2)}, u32[]{:S(2)}) collective-permute-start(bf16[32,896]{1,0:T(8,128)(2,1)S(1)} %slice.121), channel_id=1, source_target_pairs={{0,2},{1,3},{2,0},{3,1},{4,6},{5,7},{6,4},{7,5},{8,10},{9,11},{10,... | collective-permute-start | bytes 172040 | tf_op jit(solution)/shard_map/ppermute | solution.py:32
  75.5 6.3 %collective-permute-start.19 = (bf16[8,3584]{1,0:T(8,128)(2,1)S(1)}, bf16[8,3584]{1,0:T(8,128)(2,1)S(1)}, u32[]{:S(2)}, u32[]{:S(2)}) collective-permute-start(bf16[8,3584]{1,0:T(8,128)(2,1)S(1)} %get-tuple-element.71), channel_id=1, source_target_pairs={{0,12},{4,0},{8,4},{12,8},{1,13},{5,1},{9,5},{13,9},{2,14},{6,2},{... | collective-permute-start | bytes 172040 | tf_op jit(solution)/shard_map/ppermute | solution.py:27
  80.0 5.2 %collective-permute-start.20 = (bf16[8,3584]{1,0:T(8,128)(2,1)S(1)}, bf16[8,3584]{1,0:T(8,128)(2,1)S(1)}, u32[]{:S(2)}, u32[]{:S(2)}) collective-permute-start(bf16[8,3584]{1,0:T(8,128)(2,1)S(1)} %get-tuple-element.73), channel_id=1, source_target_pairs={{0,8},{4,12},{8,0},{12,4},{1,9},{5,13},{9,1},{13,5},{2,10},{6,14},... | collective-permute-start | bytes 172040 | tf_op jit(solution)/shard_map/ppermute | solution.py:27
  80.6 6.0 %collective-permute-start.21 = (bf16[8,3584]{1,0:T(8,128)(2,1)S(1)}, bf16[8,3584]{1,0:T(8,128)(2,1)S(1)}, u32[]{:S(2)}, u32[]{:S(2)}) collective-permute-start(bf16[8,3584]{1,0:T(8,128)(2,1)S(1)} %get-tuple-element.72), channel_id=1, source_target_pairs={{0,4},{4,8},{8,12},{12,0},{1,5},{5,9},{9,13},{13,1},{2,6},{6,10},{... | collective-permute-start | bytes 172040 | tf_op jit(solution)/shard_map/ppermute | solution.py:27

commit v7 on v6

--- a/solution.py
+++ b/solution.py
@@ -263,8 +263,19 @@
     )(branch, down, *acts)
 
 
-def narrow_sum(keep, send):
-    return chip_sum(keep + core_swap(send).astype(jnp.float32))
+def peers_sum(keep, send):
+    size = lax.axis_size("narrow")
+    chips = size // 2
+    part = keep.shape[0] // chips
+    result = keep[:part]
+    for d in range(chips):
+        rows = slice(d * part, (d + 1) * part)
+        if d > 0:
+            piece = keep[rows].astype(jnp.bfloat16)
+            result = result + x_shift(piece, -d).astype(jnp.float32)
+        pairs = [(i, ((i - 2 * d) % size) ^ 1) for i in range(size)]
+        result = result + lax.ppermute(send[rows], "narrow", pairs).astype(jnp.float32)
+    return result
 
 
 def chip_sum(total):
@@ -335,7 +346,7 @@
     acts, down = join(acts, load(down, shared_down.shape[0]))
     part = shared_out(branch, *down, acts, rows)
     part, routed = join(part, routed)
-    total, part = jnp.concatenate(routed, axis=1), narrow_sum(*part)
+    total, part = jnp.concatenate(routed, axis=1), peers_sum(*part)
     at = here * part.shape[1]
     part = part + lax.dynamic_slice_in_dim(total, at, part.shape[1], axis=1)
     total = lax.dynamic_update_slice_in_dim(total, part, at, axis=1)

time: 87.5 us -> 87.7 us (level)
    ppermute x0 -> x2, starting transfers between devices: none -> 1.7 us  [peers_sum(): lax.ppermute(send[rows], 'narrow', pairs).astype(jnp.float32)]
    ppermute x0 -> x2, waiting for transfers between devices: none -> 1.63 us  [peers_sum(): lax.ppermute(send[rows], 'narrow', pairs).astype(jnp.float32)]
    ppermute x5 -> x4, waiting for transfers between devices: 2.16 us -> 0.87 us  [core_swap(): return lax.ppermute(value, 'narrow', [(i, i ^ 1) for i in range(size)])]
    ppermute x5, starting transfers between devices: 5.83 us -> 4.82 us  [x_shift(): lax.ppermute(value, 'narrow', [(i, (i + 2 * step) % size) for i in range(...]
  transfers between devices with their start and end apart: 22 -> 23, of which waited for: 13 -> 13; matrix products, arithmetic and copies ran while one was open for 1% -> 1% of each run, Pallas kernels for 35% -> 35%
where the time goes in v7:
time: 87.7 us; the launch traced here: 87.4 us
  Pallas kernels  30.9 us (35%)
  starting transfers between devices  27.7 us (32%)
  waiting for transfers between devices  20.7 us (24%)
  local copies, waits for them, and re-layouts  5.93 us (7%)
  other arithmetic  1.94 us (2%)
    pallas_call x1, Pallas kernels, experts(): pl.pallas_call(functools.partial(experts_kernel, chosen), in_specs=[pl.Bl...  27.3 us
    ppermute x12, starting transfers between devices, z_shift(): lax.ppermute(value, 'expert', [(i, (i + step) % spread) for i in range(sp...  20.5 us
    ppermute x12, waiting for transfers between devices, z_shift(): lax.ppermute(value, 'expert', [(i, (i + step) % spread) for i in range(sp...  16 us
    unnamed x9, local copies, waits for them, and re-layouts  4.89 us
    ppermute x5, starting transfers between devices, x_shift(): lax.ppermute(value, 'narrow', [(i, (i + 2 * step) % size) for i in range(...  4.82 us
    ppermute x5, waiting for transfers between devices, x_shift(): lax.ppermute(value, 'narrow', [(i, (i + 2 * step) % size) for i in range(...  2.14 us
    pallas_call x1, Pallas kernels, shared_in(): pl.pallas_call(functools.partial(shared_in_kernel, (outer, spread, rows),...  1.84 us
  transfers between devices with their start and end apart: 23, of which 13 were waited for; matrix products, arithmetic and copies ran while one was open for 1% of the time, Pallas kernels for 35%

profile of v7, /device:TPU:0, one launch (start us, length us, event | category | flops | bytes accessed | tf_op | source)
XLA Modules:
  0.0 87.4 jit_solution(11898908589399734581)
XLA Ops:
  0.0 0.7 convert_element_type.54
  0.7 0.9 %concatenate.25 = bf16[8,3712]{1,0:T(8,128)(2,1)S(1)} concatenate(bf16[8,3584]{1,0:T(8,128)(2,1)} %param.10, bf16[8,8]{1,0:T(8,128)(2,1)S(1)} %convert_element_type.54, bf16[8,8]{1,0:T(8,128)(2,1)} %param.12, bf16[8,112]{1,0:T(8,128)(2,1)S(1)} %broadcast_in_dim.3), dimensions={1} | concatenate | bytes 118784 | tf_op jit(solution)/shard_map/concatenate | solution.py:309
  1.6 3.0 %collective-permute-start = (bf16[8,3712]{1,0:T(8,128)(2,1)S(1)}, bf16[8,3712]{1,0:T(8,128)(2,1)S(1)}, u32[]{:S(2)}, u32[]{:S(2)}) collective-permute-start(bf16[8,3712]{1,0:T(8,128)(2,1)S(1)} %concatenate.25), channel_id=1, source_target_pairs={{0,4},{4,8},{8,12},{12,0},{1,5},{5,9},{9,13},{13,1},{2,6},{6,10},{... | collective-permute-start | bytes 178184 | tf_op jit(solution)/shard_map/ppermute | solution.py:27
  4.6 2.6 %collective-permute-start.1 = (bf16[8,3712]{1,0:T(8,128)(2,1)S(1)}, bf16[8,3712]{1,0:T(8,128)(2,1)S(1)}, u32[]{:S(2)}, u32[]{:S(2)}) collective-permute-start(bf16[8,3712]{1,0:T(8,128)(2,1)S(1)} %concatenate.25), channel_id=1, source_target_pairs={{0,8},{4,12},{8,0},{12,4},{1,9},{5,13},{9,1},{13,5},{2,10},{6,14},... | collective-permute-start | bytes 178184 | tf_op jit(solution)/shard_map/ppermute | solution.py:27
  7.2 1.3 %collective-permute-start.2 = (bf16[8,3712]{1,0:T(8,128)(2,1)S(1)}, bf16[8,3712]{1,0:T(8,128)(2,1)S(1)}, u32[]{:S(2)}, u32[]{:S(2)}) collective-permute-start(bf16[8,3712]{1,0:T(8,128)(2,1)S(1)} %concatenate.25), channel_id=1, source_target_pairs={{0,12},{4,0},{8,4},{12,8},{1,13},{5,1},{9,5},{13,9},{2,14},{6,2},{... | collective-permute-start | bytes 178184 | tf_op jit(solution)/shard_map/ppermute | solution.py:27
  8.6 0.5 collective-permute-done
  9.0 2.3 %collective-permute-done.1 = bf16[8,3712]{1,0:T(8,128)(2,1)S(1)} collective-permute-done((bf16[8,3712]{1,0:T(8,128)(2,1)S(1)}, bf16[8,3712]{1,0:T(8,128)(2,1)S(1)}, u32[]{:S(2)}, u32[]{:S(2)}) %collective-permute-start.1) | collective-permute-done | bytes 59424 | tf_op jit(solution)/shard_map/ppermute | solution.py:27
  11.4 0.4 collective-permute-done.2
  11.8 1.5 %collective-permute-start.4 = (bf16[32,1024]{1,0:T(8,128)(2,1)S(1)}, bf16[32,1024]{1,0:T(8,128)(2,1)S(1)}, u32[]{:S(2)}, u32[]{:S(2)}) collective-permute-start(bf16[32,1024]{1,0:T(8,128)(2,1)S(1)} %pad_maximum_fusion.2), channel_id=1, source_target_pairs={{0,2},{1,3},{2,0},{3,1},{4,6},{5,7},{6,4},{7,5},{8,10},{9,11},{10,... | collective-permute-start | bytes 196616 | tf_op jit(solution)/shard_map/ppermute | solution.py:32
  13.4 0.6 collective-permute-start.3
  14.0 2.3 %copy-done = bf16[896,2560]{1,0:T(8,128)(2,1)S(1)} copy-done((bf16[896,2560]{1,0:T(8,128)(2,1)S(1)}, bf16[896,2560]{1,0:T(8,128)(2,1)}, u32[]{:S(2)}) %copy-start) | copy-done | bytes 4587544
  16.3 0.5 load.2.up_ref
  16.8 0.1 collective-permute-done.4
  16.9 0.5 collective-permute-start.6
  17.4 0.7 collective-permute-done.5.refs_2_
  18.2 0.2 collective-permute-done.6.refs_3_
  18.3 0.3 copy-done.1
  18.6 1.8 %shared_in.1 = (bf16[2,32,2560]{2,1,0:T(8,128)(2,1)S(1)}, bf16[2,32,2560]{2,1,0:T(8,128)(2,1)S(1)}, bf16[2,32,2560]{2,1,0:T(8,128)(2,1)S(1)}, bf16[2,32,2560]{2,1,0:T(8,128)(2,1)S(1)}) custom-call(bf16[896,2560]{1,0:T(8,128)(2,1)S(1)} %copy-done.1, bf16[896,2560]{1,0:T(8,128)(2,1)S(1)} %load.2.up_ref, bf16[32,896]{1,0:T(8,128)(2,1)S(1)} %slice.74.refs_0_, ...), custom_call_target="tpu_custom_call" | custom-call | flops 1174405120 | bytes 1310720 | tf_op jit(solution)/shard_map/shared_in/pallas_call | solution.py:118
  20.5 0.2 collective-permute-start.7
  20.7 1.8 %collective-permute-start.10 = (bf16[2,32,2560]{2,1,0:T(8,128)(2,1)S(1)}, bf16[2,32,2560]{2,1,0:T(8,128)(2,1)S(1)}, u32[]{:S(2)}, u32[]{:S(2)}) collective-permute-start(bf16[2,32,2560]{2,1,0:T(8,128)(2,1)S(1)} %get-tuple-element.45), channel_id=1, source_target_pairs={{0,4},{4,8},{8,12},{12,0},{1,5},{5,9},{9,13},{13,1},{2,6},{6,10},{... | collective-permute-start | bytes 983048 | tf_op jit(solution)/shard_map/ppermute | solution.py:27
  22.5 2.1 %collective-permute-start.8 = (bf16[2,32,2560]{2,1,0:T(8,128)(2,1)S(1)}, bf16[2,32,2560]{2,1,0:T(8,128)(2,1)S(1)}, u32[]{:S(2)}, u32[]{:S(2)}) collective-permute-start(bf16[2,32,2560]{2,1,0:T(8,128)(2,1)S(1)} %get-tuple-element.43), channel_id=1, source_target_pairs={{0,12},{4,0},{8,4},{12,8},{1,13},{5,1},{9,5},{13,9},{2,14},{6,2},{... | collective-permute-start | bytes 983048 | tf_op jit(solution)/shard_map/ppermute | solution.py:27
  24.5 0.1 pad_maximum_fusion.x_ref
  24.6 27.3 %experts.1 = (f32[128,128]{1,0:T(8,128)S(1)}, f32[64,3584]{1,0:T(8,128)S(1)}, bf16[64,3584]{1,0:T(8,128)(2,1)S(1)}) custom-call(s32[1]{0:T(128)} %bitcast.first_ref, bf16[128,3712]{1,0:T(8,128)(2,1)S(1)} %pad_maximum_fusion.x_ref, f32[1,3584]{1,0:T(1,128)S(1)} %reshape.7.scale_ref, bf16[8,3584,512]{2,1,0:T(8,128)(2,1)} %gate_ref.3, ...), custom_call_target="tpu_custom_call" | custom-call | flops 11274289152 | bytes 88080384 | tf_op jit(solution)/shard_map/experts/pallas_call | solution.py:207
  51.9 1.4 %collective-permute-done.9 = bf16[2,32,2560]{2,1,0:T(8,128)(2,1)S(1)} collective-permute-done((bf16[2,32,2560]{2,1,0:T(8,128)(2,1)S(1)}, bf16[2,32,2560]{2,1,0:T(8,128)(2,1)S(1)}, u32[]{:S(2)}, u32[]{:S(2)}) %collective-permute-start.9) | collective-permute-done | bytes 327712 | tf_op jit(solution)/shard_map/ppermute | solution.py:27
  53.3 0.2 convert_add_fusion.1
  53.5 0.1 fusion.1.refs_0_
  53.6 0.3 collective-permute-start.11
  53.9 1.5 %collective-permute-start.12 = (bf16[32,2560]{1,0:T(8,128)(2,1)S(1)}, bf16[32,2560]{1,0:T(8,128)(2,1)S(1)}, u32[]{:S(2)}, u32[]{:S(2)}) collective-permute-start(bf16[32,2560]{1,0:T(8,128)(2,1)S(1)} %fusion.1.refs_0_), channel_id=1, source_target_pairs={{0,8},{4,12},{8,0},{12,4},{1,9},{5,13},{9,1},{13,5},{2,10},{6,14},... | collective-permute-start | bytes 491528 | tf_op jit(solution)/shard_map/ppermute | solution.py:27
  55.3 2.8 %collective-permute-start.13 = (bf16[32,2560]{1,0:T(8,128)(2,1)S(1)}, bf16[32,2560]{1,0:T(8,128)(2,1)S(1)}, u32[]{:S(2)}, u32[]{:S(2)}) collective-permute-start(bf16[32,2560]{1,0:T(8,128)(2,1)S(1)} %fusion.1.refs_0_), channel_id=1, source_target_pairs={{0,12},{4,0},{8,4},{12,8},{1,13},{5,1},{9,5},{13,9},{2,14},{6,2},{... | collective-permute-start | bytes 491528 | tf_op jit(solution)/shard_map/ppermute | solution.py:27
  58.2 0.1 fusion.5
  58.3 1.5 %collective-permute-start.15 = (bf16[32,1792]{1,0:T(8,128)(2,1)S(1)}, bf16[32,1792]{1,0:T(8,128)(2,1)S(1)}, u32[]{:S(2)}, u32[]{:S(2)}) collective-permute-start(bf16[32,1792]{1,0:T(8,128)(2,1)S(1)} %get-tuple-element.70), channel_id=1, source_target_pairs={{0,2},{1,3},{2,0},{3,1},{4,6},{5,7},{6,4},{7,5},{8,10},{9,11},{10,... | collective-permute-start | bytes 344072 | tf_op jit(solution)/shard_map/ppermute | solution.py:32
  59.8 0.6 collective-permute-start.16
  60.4 2.3 %copy-done.2 = bf16[2560,896]{1,0:T(8,128)(2,1)S(1)} copy-done((bf16[2560,896]{1,0:T(8,128)(2,1)S(1)}, bf16[2560,896]{1,0:T(8,128)(2,1)}, u32[]{:S(2)}) %copy-start.2) | copy-done | bytes 4587544
  62.7 0.5 load.3.down_ref
  63.2 5.7 %collective-permute-done.12.refs_2_ = bf16[32,2560]{1,0:T(8,128)(2,1)S(1)} collective-permute-done((bf16[32,2560]{1,0:T(8,128)(2,1)S(1)}, bf16[32,2560]{1,0:T(8,128)(2,1)S(1)}, u32[]{:S(2)}, u32[]{:S(2)}) %collective-permute-start.12) | collective-permute-done | bytes 163872 | tf_op jit(solution)/shard_map/ppermute | solution.py:27
  68.9 0.9 shared_out.1
  69.8 0.1 collective-permute-start.17
  69.9 1.6 %collective-permute-start.19 = (bf16[32,896]{1,0:T(8,128)(2,1)S(1)}, bf16[32,896]{1,0:T(8,128)(2,1)S(1)}, u32[]{:S(2)}, u32[]{:S(2)}) collective-permute-start(bf16[32,896]{1,0:T(8,128)(2,1)S(1)} %get-tuple-element.75), channel_id=1, source_target_pairs={{0,3},{1,2},{2,1},{3,0},{4,7},{5,6},{6,5},{7,4},{8,11},{9,10},{10,... | collective-permute-start | bytes 172040 | tf_op jit(solution)/shard_map/ppermute | solution.py:277
  71.5 0.6 collective-permute-start.18
  72.2 1.6 %collective-permute-done.19 = bf16[32,896]{1,0:T(8,128)(2,1)S(1)} collective-permute-done((bf16[32,896]{1,0:T(8,128)(2,1)S(1)}, bf16[32,896]{1,0:T(8,128)(2,1)S(1)}, u32[]{:S(2)}, u32[]{:S(2)}) %collective-permute-start.19) | collective-permute-done | bytes 57376 | tf_op jit(solution)/shard_map/ppermute | solution.py:277
  73.8 2.0 %collective-permute-done.18 = bf16[32,896]{1,0:T(8,128)(2,1)S(1)} collective-permute-done((bf16[32,896]{1,0:T(8,128)(2,1)S(1)}, bf16[32,896]{1,0:T(8,128)(2,1)S(1)}, u32[]{:S(2)}, u32[]{:S(2)}) %collective-permute-start.18) | collective-permute-done | bytes 57376 | tf_op jit(solution)/shard_map/ppermute | solution.py:32
  75.9 4.4 %collective-permute-start.20 = (bf16[8,3584]{1,0:T(8,128)(2,1)S(1)}, bf16[8,3584]{1,0:T(8,128)(2,1)S(1)}, u32[]{:S(2)}, u32[]{:S(2)}) collective-permute-start(bf16[8,3584]{1,0:T(8,128)(2,1)S(1)} %get-tuple-element.71), channel_id=1, source_target_pairs={{0,12},{4,0},{8,4},{12,8},{1,13},{5,1},{9,5},{13,9},{2,14},{6,2},{... | collective-permute-start | bytes 172040 | tf_op jit(solution)/shard_map/ppermute | solution.py:27
  80.3 0.5 collective-permute-start.21
  80.8 0.2 collective-permute-start.22
  80.9 1.2 %collective-permute-done.20 = bf16[8,3584]{1,0:T(8,128)(2,1)S(1)} collective-permute-done((bf16[8,3584]{1,0:T(8,128)(2,1)S(1)}, bf16[8,3584]{1,0:T(8,128)(2,1)S(1)}, u32[]{:S(2)}, u32[]{:S(2)}) %collective-permute-start.20) | collective-permute-done | bytes 57376 | tf_op jit(solution)/shard_map/ppermute | solution.py:27
  82.1 3.3 %collective-permute-done.21 = bf16[8,3584]{1,0:T(8,128)(2,1)S(1)} collective-permute-done((bf16[8,3584]{1,0:T(8,128)(2,1)S(1)}, bf16[8,3584]{1,0:T(8,128)(2,1)S(1)}, u32[]{:S(2)}, u32[]{:S(2)}) %collective-permute-start.21) | collective-permute-done | bytes 57376 | tf_op jit(solution)/shard_map/ppermute | solution.py:27
  85.4 1.4 %collective-permute-done.22 = bf16[8,3584]{1,0:T(8,128)(2,1)S(1)} collective-permute-done((bf16[8,3584]{1,0:T(8,128)(2,1)S(1)}, bf16[8,3584]{1,0:T(8,128)(2,1)S(1)}, u32[]{:S(2)}, u32[]{:S(2)}) %collective-permute-start.22) | collective-permute-done | bytes 57376 | tf_op jit(solution)/shard_map/ppermute | solution.py:27
  86.7 0.7 fusion.4
  (39 shorter events, 0.4 us)
Async XLA Ops:
  1.6 7.4 %collective-permute-start = (bf16[8,3712]{1,0:T(8,128)(2,1)S(1)}, bf16[8,3712]{1,0:T(8,128)(2,1)S(1)}, u32[]{:S(2)}, u32[]{:S(2)}) collective-permute-start(bf16[8,3712]{1,0:T(8,128)(2,1)S(1)} %concatenate.25), channel_id=1, source_target_pairs={{0,4},{4,8},{8,12},{12,0},{1,5},{5,9},{9,13},{13,1},{2,6},{6,10},{... | collective-permute-start | bytes 178184 | tf_op jit(solution)/shard_map/ppermute | solution.py:27
  4.6 6.7 %collective-permute-start.1 = (bf16[8,3712]{1,0:T(8,128)(2,1)S(1)}, bf16[8,3712]{1,0:T(8,128)(2,1)S(1)}, u32[]{:S(2)}, u32[]{:S(2)}) collective-permute-start(bf16[8,3712]{1,0:T(8,128)(2,1)S(1)} %concatenate.25), channel_id=1, source_target_pairs={{0,8},{4,12},{8,0},{12,4},{1,9},{5,13},{9,1},{13,5},{2,10},{6,14},... | collective-permute-start | bytes 178184 | tf_op jit(solution)/shard_map/ppermute | solution.py:27
  7.2 4.5 %collective-permute-start.2 = (bf16[8,3712]{1,0:T(8,128)(2,1)S(1)}, bf16[8,3712]{1,0:T(8,128)(2,1)S(1)}, u32[]{:S(2)}, u32[]{:S(2)}) collective-permute-start(bf16[8,3712]{1,0:T(8,128)(2,1)S(1)} %concatenate.25), channel_id=1, source_target_pairs={{0,12},{4,0},{8,4},{12,8},{1,13},{5,1},{9,5},{13,9},{2,14},{6,2},{... | collective-permute-start | bytes 178184 | tf_op jit(solution)/shard_map/ppermute | solution.py:27
  11.8 5.1 %collective-permute-start.4 = (bf16[32,1024]{1,0:T(8,128)(2,1)S(1)}, bf16[32,1024]{1,0:T(8,128)(2,1)S(1)}, u32[]{:S(2)}, u32[]{:S(2)}) collective-permute-start(bf16[32,1024]{1,0:T(8,128)(2,1)S(1)} %pad_maximum_fusion.2), channel_id=1, source_target_pairs={{0,2},{1,3},{2,0},{3,1},{4,6},{5,7},{6,4},{7,5},{8,10},{9,11},{10,... | collective-permute-start | bytes 196616 | tf_op jit(solution)/shard_map/ppermute | solution.py:32
  13.4 7.1 %collective-permute-start.3 = (bf16[32,3584]{1,0:T(8,128)(2,1)S(1)}, bf16[32,3584]{1,0:T(8,128)(2,1)S(1)}, u32[]{:S(2)}, u32[]{:S(2)}) collective-permute-start(bf16[32,3584]{1,0:T(8,128)(2,1)S(1)} %slice.92), channel_id=1, source_target_pairs={{0,2},{1,3},{2,0},{3,1},{4,6},{5,7},{6,4},{7,5},{8,10},{9,11},{10,... | collective-permute-start | bytes 688136 | tf_op jit(solution)/shard_map/ppermute | solution.py:32
  14.0 2.3 %copy-start = (bf16[896,2560]{1,0:T(8,128)(2,1)S(1)}, bf16[896,2560]{1,0:T(8,128)(2,1)}, u32[]{:S(2)}) copy-start(bf16[896,2560]{1,0:T(8,128)(2,1)} %refs_0_.1) | copy-start | bytes 13762564
  16.3 2.3 %copy-start.1 = (bf16[896,2560]{1,0:T(8,128)(2,1)S(1)}, bf16[896,2560]{1,0:T(8,128)(2,1)}, u32[]{:S(2)}) copy-start(bf16[896,2560]{1,0:T(8,128)(2,1)} %gate_ref.2) | copy-start | bytes 13762564
  16.9 1.2 %collective-permute-start.5 = (bf16[32,896]{1,0:T(8,128)(2,1)S(1)}, bf16[32,896]{1,0:T(8,128)(2,1)S(1)}, u32[]{:S(2)}, u32[]{:S(2)}) collective-permute-start(bf16[32,896]{1,0:T(8,128)(2,1)S(1)} %slice.74.refs_0_), channel_id=1, source_target_pairs={{0,1},{1,0},{2,3},{3,2},{4,5},{5,4},{6,7},{7,6},{8,9},{9,8},{10,11... | collective-permute-start | bytes 172040 | tf_op jit(solution)/shard_map/ppermute | solution.py:37
  16.9 1.4 %collective-permute-start.6 = (bf16[32,896]{1,0:T(8,128)(2,1)S(1)}, bf16[32,896]{1,0:T(8,128)(2,1)S(1)}, u32[]{:S(2)}, u32[]{:S(2)}) collective-permute-start(bf16[32,896]{1,0:T(8,128)(2,1)S(1)} %slice.75.refs_1_), channel_id=1, source_target_pairs={{0,1},{1,0},{2,3},{3,2},{4,5},{5,4},{6,7},{7,6},{8,9},{9,8},{10,11... | collective-permute-start | bytes 172040 | tf_op jit(solution)/shard_map/ppermute | solution.py:37
  17.4 3.2 %copy-start.3 = (f32[3584]{0:T(1024)S(1)}, f32[3584]{0:T(1024)}, u32[]{:S(2)}) copy-start(f32[3584]{0:T(1024)} %param.19) | copy-start | bytes 43012
  20.5 4.1 %collective-permute-start.7 = (bf16[64,3712]{1,0:T(8,128)(2,1)S(1)}, bf16[64,3712]{1,0:T(8,128)(2,1)S(1)}, u32[]{:S(2)}, u32[]{:S(2)}) collective-permute-start(bf16[64,3712]{1,0:T(8,128)(2,1)S(1)} %maximum_maximum_fusion), channel_id=1, source_target_pairs={{0,1},{1,0},{2,3},{3,2},{4,5},{5,4},{6,7},{7,6},{8,9},{9,8},{10,11... | collective-permute-start | bytes 1425416 | tf_op jit(solution)/shard_map/ppermute | solution.py:37
  20.7 31.2 %collective-permute-start.10 = (bf16[2,32,2560]{2,1,0:T(8,128)(2,1)S(1)}, bf16[2,32,2560]{2,1,0:T(8,128)(2,1)S(1)}, u32[]{:S(2)}, u32[]{:S(2)}) collective-permute-start(bf16[2,32,2560]{2,1,0:T(8,128)(2,1)S(1)} %get-tuple-element.45), channel_id=1, source_target_pairs={{0,4},{4,8},{8,12},{12,0},{1,5},{5,9},{9,13},{13,1},{2,6},{6,10},{... | collective-permute-start | bytes 983048 | tf_op jit(solution)/shard_map/ppermute | solution.py:27
  22.5 29.4 %collective-permute-start.8 = (bf16[2,32,2560]{2,1,0:T(8,128)(2,1)S(1)}, bf16[2,32,2560]{2,1,0:T(8,128)(2,1)S(1)}, u32[]{:S(2)}, u32[]{:S(2)}) collective-permute-start(bf16[2,32,2560]{2,1,0:T(8,128)(2,1)S(1)} %get-tuple-element.43), channel_id=1, source_target_pairs={{0,12},{4,0},{8,4},{12,8},{1,13},{5,1},{9,5},{13,9},{2,14},{6,2},{... | collective-permute-start | bytes 983048 | tf_op jit(solution)/shard_map/ppermute | solution.py:27
  24.5 28.8 %collective-permute-start.9 = (bf16[2,32,2560]{2,1,0:T(8,128)(2,1)S(1)}, bf16[2,32,2560]{2,1,0:T(8,128)(2,1)S(1)}, u32[]{:S(2)}, u32[]{:S(2)}) collective-permute-start(bf16[2,32,2560]{2,1,0:T(8,128)(2,1)S(1)} %get-tuple-element.44), channel_id=1, source_target_pairs={{0,8},{4,12},{8,0},{12,4},{1,9},{5,13},{9,1},{13,5},{2,10},{6,14},... | collective-permute-start | bytes 983048 | tf_op jit(solution)/shard_map/ppermute | solution.py:27
  53.3 4.9 %collective-permute-start.14 = (bf16[64,3584]{1,0:T(8,128)(2,1)S(1)}, bf16[64,3584]{1,0:T(8,128)(2,1)S(1)}, u32[]{:S(2)}, u32[]{:S(2)}) collective-permute-start(bf16[64,3584]{1,0:T(8,128)(2,1)S(1)} %get-tuple-element.60), channel_id=1, source_target_pairs={{0,1},{1,0},{2,3},{3,2},{4,5},{5,4},{6,7},{7,6},{8,9},{9,8},{10,11... | collective-permute-start | bytes 1376264 | tf_op jit(solution)/shard_map/ppermute | solution.py:37
  53.6 9.6 %collective-permute-start.11 = (bf16[32,2560]{1,0:T(8,128)(2,1)S(1)}, bf16[32,2560]{1,0:T(8,128)(2,1)S(1)}, u32[]{:S(2)}, u32[]{:S(2)}) collective-permute-start(bf16[32,2560]{1,0:T(8,128)(2,1)S(1)} %fusion.1.refs_0_), channel_id=1, source_target_pairs={{0,4},{4,8},{8,12},{12,0},{1,5},{5,9},{9,13},{13,1},{2,6},{6,10},{... | collective-permute-start | bytes 491528 | tf_op jit(solution)/shard_map/ppermute | solution.py:27
  53.9 15.0 %collective-permute-start.12 = (bf16[32,2560]{1,0:T(8,128)(2,1)S(1)}, bf16[32,2560]{1,0:T(8,128)(2,1)S(1)}, u32[]{:S(2)}, u32[]{:S(2)}) collective-permute-start(bf16[32,2560]{1,0:T(8,128)(2,1)S(1)} %fusion.1.refs_0_), channel_id=1, source_target_pairs={{0,8},{4,12},{8,0},{12,4},{1,9},{5,13},{9,1},{13,5},{2,10},{6,14},... | collective-permute-start | bytes 491528 | tf_op jit(solution)/shard_map/ppermute | solution.py:27
  55.3 13.5 %collective-permute-start.13 = (bf16[32,2560]{1,0:T(8,128)(2,1)S(1)}, bf16[32,2560]{1,0:T(8,128)(2,1)S(1)}, u32[]{:S(2)}, u32[]{:S(2)}) collective-permute-start(bf16[32,2560]{1,0:T(8,128)(2,1)S(1)} %fusion.1.refs_0_), channel_id=1, source_target_pairs={{0,12},{4,0},{8,4},{12,8},{1,13},{5,1},{9,5},{13,9},{2,14},{6,2},{... | collective-permute-start | bytes 491528 | tf_op jit(solution)/shard_map/ppermute | solution.py:27
  58.3 11.4 %collective-permute-start.15 = (bf16[32,1792]{1,0:T(8,128)(2,1)S(1)}, bf16[32,1792]{1,0:T(8,128)(2,1)S(1)}, u32[]{:S(2)}, u32[]{:S(2)}) collective-permute-start(bf16[32,1792]{1,0:T(8,128)(2,1)S(1)} %get-tuple-element.70), channel_id=1, source_target_pairs={{0,2},{1,3},{2,0},{3,1},{4,6},{5,7},{6,4},{7,5},{8,10},{9,11},{10,... | collective-permute-start | bytes 344072 | tf_op jit(solution)/shard_map/ppermute | solution.py:32
  59.8 9.9 %collective-permute-start.16 = (bf16[32,1792]{1,0:T(8,128)(2,1)S(1)}, bf16[32,1792]{1,0:T(8,128)(2,1)S(1)}, u32[]{:S(2)}, u32[]{:S(2)}) collective-permute-start(bf16[32,1792]{1,0:T(8,128)(2,1)S(1)} %get-tuple-element.69), channel_id=1, source_target_pairs={{0,2},{1,3},{2,0},{3,1},{4,6},{5,7},{6,4},{7,5},{8,10},{9,11},{10,... | collective-permute-start | bytes 344072 | tf_op jit(solution)/shard_map/ppermute | solution.py:32
  60.4 2.3 %copy-start.2 = (bf16[2560,896]{1,0:T(8,128)(2,1)S(1)}, bf16[2560,896]{1,0:T(8,128)(2,1)}, u32[]{:S(2)}) copy-start(bf16[2560,896]{1,0:T(8,128)(2,1)} %refs_0_.2) | copy-start | bytes 13762564
  69.8 2.3 %collective-permute-start.17 = (bf16[32,896]{1,0:T(8,128)(2,1)S(1)}, bf16[32,896]{1,0:T(8,128)(2,1)S(1)}, u32[]{:S(2)}, u32[]{:S(2)}) collective-permute-start(bf16[32,896]{1,0:T(8,128)(2,1)S(1)} %get-tuple-element.74), channel_id=1, source_target_pairs={{0,1},{1,0},{2,3},{3,2},{4,5},{5,4},{6,7},{7,6},{8,9},{9,8},{10,11... | collective-permute-start | bytes 172040 | tf_op jit(solution)/shard_map/ppermute | solution.py:277
  69.9 3.9 %collective-permute-start.19 = (bf16[32,896]{1,0:T(8,128)(2,1)S(1)}, bf16[32,896]{1,0:T(8,128)(2,1)S(1)}, u32[]{:S(2)}, u32[]{:S(2)}) collective-permute-start(bf16[32,896]{1,0:T(8,128)(2,1)S(1)} %get-tuple-element.75), channel_id=1, source_target_pairs={{0,3},{1,2},{2,1},{3,0},{4,7},{5,6},{6,5},{7,4},{8,11},{9,10},{10,... | collective-permute-start | bytes 172040 | tf_op jit(solution)/shard_map/ppermute | solution.py:277
  71.5 4.2 %collective-permute-start.18 = (bf16[32,896]{1,0:T(8,128)(2,1)S(1)}, bf16[32,896]{1,0:T(8,128)(2,1)S(1)}, u32[]{:S(2)}, u32[]{:S(2)}) collective-permute-start(bf16[32,896]{1,0:T(8,128)(2,1)S(1)} %slice.124), channel_id=1, source_target_pairs={{0,2},{1,3},{2,0},{3,1},{4,6},{5,7},{6,4},{7,5},{8,10},{9,11},{10,... | collective-permute-start | bytes 172040 | tf_op jit(solution)/shard_map/ppermute | solution.py:32
  75.9 6.2 %collective-permute-start.20 = (bf16[8,3584]{1,0:T(8,128)(2,1)S(1)}, bf16[8,3584]{1,0:T(8,128)(2,1)S(1)}, u32[]{:S(2)}, u32[]{:S(2)}) collective-permute-start(bf16[8,3584]{1,0:T(8,128)(2,1)S(1)} %get-tuple-element.71), channel_id=1, source_target_pairs={{0,12},{4,0},{8,4},{12,8},{1,13},{5,1},{9,5},{13,9},{2,14},{6,2},{... | collective-permute-start | bytes 172040 | tf_op jit(solution)/shard_map/ppermute | solution.py:27
  80.3 5.1 %collective-permute-start.21 = (bf16[8,3584]{1,0:T(8,128)(2,1)S(1)}, bf16[8,3584]{1,0:T(8,128)(2,1)S(1)}, u32[]{:S(2)}, u32[]{:S(2)}) collective-permute-start(bf16[8,3584]{1,0:T(8,128)(2,1)S(1)} %get-tuple-element.73), channel_id=1, source_target_pairs={{0,8},{4,12},{8,0},{12,4},{1,9},{5,13},{9,1},{13,5},{2,10},{6,14},... | collective-permute-start | bytes 172040 | tf_op jit(solution)/shard_map/ppermute | solution.py:27
  80.8 6.0 %collective-permute-start.22 = (bf16[8,3584]{1,0:T(8,128)(2,1)S(1)}, bf16[8,3584]{1,0:T(8,128)(2,1)S(1)}, u32[]{:S(2)}, u32[]{:S(2)}) collective-permute-start(bf16[8,3584]{1,0:T(8,128)(2,1)S(1)} %get-tuple-element.72), channel_id=1, source_target_pairs={{0,4},{4,8},{8,12},{12,0},{1,5},{5,9},{9,13},{13,1},{2,6},{6,10},{... | collective-permute-start | bytes 172040 | tf_op jit(solution)/shard_map/ppermute | solution.py:27
